TPU v7x, 32 devices: a whole 2x2x4 slice. The times are simulated.
32 devices in a mesh: ctx: 8 (over y, x, core), tp: 4 (over z).
Axes of the slice: x: 2, y: 2, z: 4, core: 2. Of those that a mesh axis runs over, the one named last changes fastest.
Arguments:
- hidden_in: bfloat16 [6144, 1024], P('ctx'), may hold values from -6 to 6
- doc_lengths: int32 [8], replicated, may hold values from 1 to 5760, as said below
- cotangent: bfloat16 [6144, 1024], P('ctx'), may hold values from -6 to 6
- attn_gain: float32 [2, 1024], replicated, may hold values from 0.5 to 1.5
- ffn_gain: float32 [2, 1024], replicated, may hold values from 0.5 to 1.5
- qk_gain: float32 [2, 2, 128], replicated, may hold values from 0.5 to 1.5
- w_query: bfloat16 [2, 1024, 2048], P(None, None, 'tp'), may hold values from -0.1875 to 0.1875
- key_weight: bfloat16 [2, 1024, 1024], P(None, None, 'tp'), may hold values from -0.1875 to 0.1875
- value_weight: bfloat16 [2, 1024, 1024], P(None, None, 'tp'), may hold values from -0.1875 to 0.1875
- w_out: bfloat16 [2, 2048, 1024], P(None, 'tp'), may hold values from -2 to 2
- w_gate: bfloat16 [2, 1024, 3072], P(None, None, 'tp'), may hold values from -0.1875 to 0.1875
- w_up: bfloat16 [2, 1024, 3072], P(None, None, 'tp'), may hold values from -0.1875 to 0.1875
- w_down: bfloat16 [2, 3072, 1024], P(None, 'tp'), may hold values from -0.109375 to 0.109375
Outputs:
- hidden_out: bfloat16 [6144, 1024], P('ctx')
- hidden_grad: float32 [6144, 1024], P('ctx')
- attn_gain_grad: float32 [2, 1024], P(None, 'ctx')
- ffn_gain_grad: float32 [2, 1024], P(None, 'ctx')
- qk_gain_grad: float32 [2, 2, 128], replicated
- query_grad: float32 [2, 1024, 2048], P(None, 'ctx', 'tp')
- key_grad: float32 [2, 1024, 1024], P(None, 'ctx', 'tp')
- value_grad: float32 [2, 1024, 1024], P(None, 'ctx', 'tp')
- out_grad: float32 [2, 2048, 1024], P(None, ('tp', 'ctx'))
- gate_grad: float32 [2, 1024, 3072], P(None, 'ctx', 'tp')
- up_grad: float32 [2, 1024, 3072], P(None, 'ctx', 'tp')
- down_grad: float32 [2, 3072, 1024], P(None, ('tp', 'ctx'))
Inputs may be any that keep to these rules, and one draw needn't show every extreme that they name: `doc_lengths`: lengths of 8 packed documents in order, summing to 6144; exactly one of them, at a place drawn from the seed, has 5760 tokens.
All inputs are finite; a program needn't handle non-finite values.
Results may differ from a plain program's by a relative error of at most 0.03.
Values may be sent and summed in bfloat16 or wider, within the bound.
A program may use at most 256 MiB of HBM per device.

v0:
```python
import jax
import jax.numpy as jnp
from jax import lax
from jax.sharding import PartitionSpec as P

HEAD_SIZE = 128
ATTENTION_WINDOW = 1024


EPS = 1e-06
THETA = 1000000.0


def passed_along(value, axis, steps):
    count = lax.axis_size(axis)
    leading, last = (max(0, -steps), min(count, count - steps))
    return lax.ppermute(value, axis, [(source, source + steps) for source in range(leading, last)])


def matrix_product(left, right):
    return jnp.dot(left, right, preferred_element_type=jnp.float32)


def times_transposed(left, right):
    return lax.dot_general(
        left, right, (((1,), (1,)), ((), ())), preferred_element_type=jnp.float32
    )


def transposed_times(left, right):
    return lax.dot_general(
        left, right, (((0,), (0,)), ((), ())), preferred_element_type=jnp.float32
    )


def doc_info(lengths, place):
    ends = jnp.cumsum(lengths)
    passed = ends[None, :] <= place[:, None]
    segment = jnp.sum(passed.astype(jnp.int32), axis=1)
    begin = jnp.sum(jnp.where(passed, lengths[None, :], 0), axis=1)
    return (segment, place - begin)


def rope_tables(positions):
    half = HEAD_SIZE // 2
    freq = THETA ** (-(jnp.arange(half, dtype=jnp.float32) * 2.0) / HEAD_SIZE)
    angle = positions.astype(jnp.float32)[:, None] * freq[None, :]
    return (jnp.cos(angle), jnp.sin(angle))


def rotate(value_rows, cosine, sine):
    half = value_rows.shape[-1] // 2
    first = value_rows[..., :half]
    second = value_rows[..., half:]
    cosine = cosine[:, None, :]
    sine = sine[:, None, :]
    return jnp.concatenate(
        [first * cosine - second * sine, second * cosine + first * sine], axis=-1
    )


def unrotate(grad, cosine, sine):
    half = grad.shape[-1] // 2
    first = grad[..., :half]
    second = grad[..., half:]
    cosine = cosine[:, None, :]
    sine = sine[:, None, :]
    return jnp.concatenate(
        [first * cosine + second * sine, second * cosine - first * sine], axis=-1
    )


def norm_rows(value_rows, gain):
    inverse = lax.rsqrt(jnp.mean(value_rows * value_rows, axis=-1, keepdims=True) + EPS)
    unit = value_rows * inverse
    return (unit * gain, unit, inverse)


def norm_back(grad, unit, inverse, gain):
    scaled = grad * gain
    inner = jnp.mean(scaled * unit, axis=-1, keepdims=True)
    width = grad.shape[-1]
    gain_grad = jnp.sum((grad * unit).reshape(-1, width), axis=0)
    return (inverse * (scaled - unit * inner), gain_grad)


def branch_total(left, right):
    return lax.psum(matrix_product(left, right).astype(jnp.bfloat16), "tp").astype(jnp.float32)


def input_total(pairs):
    total = None
    for left, right in pairs:
        piece = times_transposed(left, right)
        total = piece if total is None else total + piece
    return lax.psum(total.astype(jnp.bfloat16), "tp").astype(jnp.float32)


def make_tables(lengths, rows):
    start = lax.axis_index("ctx") * rows
    own_place = start + jnp.arange(rows, dtype=jnp.int32)
    key_place = start - ATTENTION_WINDOW + jnp.arange(ATTENTION_WINDOW + rows, dtype=jnp.int32)
    own_segment, own_position = doc_info(lengths, own_place)
    key_segment, unused = doc_info(lengths, jnp.maximum(key_place, 0))
    key_segment = jnp.where(key_place >= 0, key_segment, -1)
    cosine, sine = rope_tables(own_position)
    return {
        "cosine": cosine,
        "sine": sine,
        "own_segment": own_segment,
        "own_place": own_place,
        "key_segment": key_segment,
        "key_place": key_place,
    }


def block_scores(query_block, key_rows, query_segment, query_place, tables):
    scores = jnp.einsum(
        "qgrd,kgd->grqk", query_block, key_rows, preferred_element_type=jnp.float32
    ) * HEAD_SIZE ** (-0.5)
    gap = query_place[:, None] - tables["key_place"][None, :]
    visible = (
        (query_segment[:, None] == tables["key_segment"][None, :])
        & (gap >= 0)
        & (gap < ATTENTION_WINDOW)
    )
    return jnp.where(visible[None, None], scores, -1e30)


def block_split(rows):
    return (rows, rows // rows)


def attend_forward(grouped_heads, key_rows, value_rows, tables):
    rows, groups, repeat, width = grouped_heads.shape
    block, count = block_split(rows)

    def one_block(item):
        query_block, query_segment, query_place = item
        scores = block_scores(query_block, key_rows, query_segment, query_place, tables)
        top = jnp.max(scores, axis=-1, keepdims=True)
        weights = jnp.exp(scores - top)
        total = jnp.sum(weights, axis=-1, keepdims=True)
        probs = (weights / total).astype(jnp.bfloat16)
        mixed = jnp.einsum("grqk,kgd->qgrd", probs, value_rows, preferred_element_type=jnp.float32)
        return (mixed, (top + jnp.log(total))[..., 0])

    items = (
        grouped_heads.reshape(count, block, groups, repeat, width),
        tables["own_segment"].reshape(count, block),
        tables["own_place"].reshape(count, block),
    )
    mixed, log_total = lax.map(one_block, items)
    return (mixed.reshape(rows, groups * repeat * width), log_total)


def attend_backward(grouped_heads, key_rows, value_rows, log_total, grad_mixed, tables):
    rows, groups, repeat, width = grouped_heads.shape
    block, count = block_split(rows)
    scale = HEAD_SIZE ** (-0.5)

    def one_block(carry, item):
        query_block, grad_block, block_total, query_segment, query_place = item
        scores = block_scores(query_block, key_rows, query_segment, query_place, tables)
        probs = jnp.exp(scores - block_total[..., None])
        grad_probs = jnp.einsum(
            "qgrd,kgd->grqk", grad_block, value_rows, preferred_element_type=jnp.float32
        )
        inner = jnp.sum(probs * grad_probs, axis=-1, keepdims=True)
        grad_scores = (probs * (grad_probs - inner)).astype(jnp.bfloat16)
        grad_query = (
            jnp.einsum("grqk,kgd->qgrd", grad_scores, key_rows, preferred_element_type=jnp.float32)
            * scale
        )
        key_total = (
            carry[0]
            + jnp.einsum(
                "grqk,qgrd->kgd", grad_scores, query_block, preferred_element_type=jnp.float32
            )
            * scale
        )
        value_total = carry[1] + jnp.einsum(
            "grqk,qgrd->kgd",
            probs.astype(jnp.bfloat16),
            grad_block,
            preferred_element_type=jnp.float32,
        )
        return ((key_total, value_total), grad_query)

    start_carry = (jnp.zeros(key_rows.shape, jnp.float32), jnp.zeros(value_rows.shape, jnp.float32))
    items = (
        grouped_heads.reshape(count, block, groups, repeat, width),
        grad_mixed.reshape(count, block, groups, repeat, width),
        log_total,
        tables["own_segment"].reshape(count, block),
        tables["own_place"].reshape(count, block),
    )
    totals, grad_query = lax.scan(one_block, start_carry, items)
    return (totals[0], totals[1], grad_query.reshape(rows, groups * repeat, width))


def halo_plan(rows):
    reach = -(-ATTENTION_WINDOW // rows)
    return [(hop, min(rows, ATTENTION_WINDOW - (hop - 1) * rows)) for hop in range(reach, 0, -1)]


def layer_forward(stream, weights, tables):
    attn_gain, ffn_gain, qk_gain, w_query, key_weight, value_weight, w_out, w_gate, w_up, w_down = (
        weights
    )
    rows = tables["own_place"].shape[0]
    normed, unit_first, inverse_first = norm_rows(stream, attn_gain)
    first_input = normed.astype(jnp.bfloat16)
    query_proj = matrix_product(first_input, w_query).reshape(rows, -1, HEAD_SIZE)
    key_projected = matrix_product(first_input, key_weight).reshape(rows, -1, HEAD_SIZE)
    own_values = (
        matrix_product(first_input, value_weight).astype(jnp.bfloat16).reshape(rows, -1, HEAD_SIZE)
    )
    query_normed, query_unit, query_inverse = norm_rows(query_proj, qk_gain[0])
    key_normed, key_unit, key_inverse = norm_rows(key_projected, qk_gain[1])
    query_rows = rotate(query_normed, tables["cosine"], tables["sine"]).astype(jnp.bfloat16)
    own_keys = rotate(key_normed, tables["cosine"], tables["sine"]).astype(jnp.bfloat16)
    far_keys = []
    far_values = []
    for hop, need in halo_plan(rows):
        got_keys, got_values = passed_along(
            (own_keys[rows - need :], own_values[rows - need :]), "ctx", hop
        )
        far_keys.append(got_keys)
        far_values.append(got_values)
    key_rows = jnp.concatenate(far_keys + [own_keys], axis=0)
    value_rows = jnp.concatenate(far_values + [own_values], axis=0)
    groups = own_keys.shape[1]
    grouped_heads = query_rows.reshape(rows, groups, query_rows.shape[1] // groups, HEAD_SIZE)
    attended, log_total = attend_forward(grouped_heads, key_rows, value_rows, tables)
    attended_low = attended.astype(jnp.bfloat16)
    middle = stream + branch_total(attended_low, w_out)
    normed_second, unit_second, inverse_second = norm_rows(middle, ffn_gain)
    second_in = normed_second.astype(jnp.bfloat16)
    gate_act = matrix_product(second_in, w_gate)
    up_act = matrix_product(second_in, w_up)
    hidden = (gate_act * jax.nn.sigmoid(gate_act) * up_act).astype(jnp.bfloat16)
    result = middle + branch_total(hidden, w_down)
    return {
        "unit_first": unit_first,
        "inverse_first": inverse_first,
        "first_in": first_input,
        "query_unit": query_unit,
        "query_inverse": query_inverse,
        "key_unit": key_unit,
        "key_inverse": key_inverse,
        "grouped": grouped_heads,
        "keys": key_rows,
        "values": value_rows,
        "log_total": log_total,
        "attended": attended_low,
        "unit_second": unit_second,
        "inverse_second": inverse_second,
        "second_in": second_in,
        "gate_act": gate_act,
        "up_act": up_act,
        "hidden": hidden,
        "result": result,
    }


def layer_backward(saved, grad, weights, tables):
    attn_gain, ffn_gain, qk_gain, w_query, key_weight, value_weight, w_out, w_gate, w_up, w_down = (
        weights
    )
    rows = tables["own_place"].shape[0]
    grad_low = grad.astype(jnp.bfloat16)
    grad_hidden = times_transposed(grad_low, w_down)
    down_total = transposed_times(saved["hidden"], grad_low)
    gate_act = saved["gate_act"]
    sigma = jax.nn.sigmoid(gate_act)
    grad_gate = (grad_hidden * saved["up_act"] * (sigma * (1.0 + gate_act * (1.0 - sigma)))).astype(
        jnp.bfloat16
    )
    grad_up = (grad_hidden * gate_act * sigma).astype(jnp.bfloat16)
    gate_total = transposed_times(saved["second_in"], grad_gate)
    up_total = transposed_times(saved["second_in"], grad_up)
    grad_second = input_total([(grad_gate, w_gate), (grad_up, w_up)])
    branch_second, ffn_gain_total = norm_back(
        grad_second, saved["unit_second"], saved["inverse_second"], ffn_gain
    )
    grad_middle = grad + branch_second
    middle_low = grad_middle.astype(jnp.bfloat16)
    out_total = transposed_times(saved["attended"], middle_low)
    grouped_heads = saved["grouped"]
    grad_attended = (
        times_transposed(middle_low, w_out).astype(jnp.bfloat16).reshape(grouped_heads.shape)
    )
    key_grads, value_grads, grad_query = attend_backward(
        grouped_heads, saved["keys"], saved["values"], saved["log_total"], grad_attended, tables
    )
    own_key_grad = key_grads[ATTENTION_WINDOW:]
    own_value_grad = value_grads[ATTENTION_WINDOW:]
    offset = 0
    for hop, need in halo_plan(rows):
        back_keys, back_values = (
            passed_along(
                key_grads[offset : offset + need].astype(jnp.bfloat16), "ctx", -hop
            ).astype(jnp.float32),
            passed_along(
                value_grads[offset : offset + need].astype(jnp.bfloat16), "ctx", -hop
            ).astype(jnp.float32),
        )
        own_key_grad = own_key_grad.at[rows - need :].add(back_keys)
        own_value_grad = own_value_grad.at[rows - need :].add(back_values)
        offset = offset + need
    query_normed_grad = unrotate(grad_query, tables["cosine"], tables["sine"])
    query_proj_grad, query_gain_total = norm_back(
        query_normed_grad, saved["query_unit"], saved["query_inverse"], qk_gain[0]
    )
    key_normed_grad = unrotate(own_key_grad, tables["cosine"], tables["sine"])
    key_proj_grad, key_gain_total = norm_back(
        key_normed_grad, saved["key_unit"], saved["key_inverse"], qk_gain[1]
    )
    query_low = query_proj_grad.reshape(rows, -1).astype(jnp.bfloat16)
    key_low = key_proj_grad.reshape(rows, -1).astype(jnp.bfloat16)
    value_low = own_value_grad.reshape(rows, -1).astype(jnp.bfloat16)
    first_input = saved["first_in"]
    query_total = transposed_times(first_input, query_low)
    key_total = transposed_times(first_input, key_low)
    value_total = transposed_times(first_input, value_low)
    grad_first = input_total(
        [(query_low, w_query), (key_low, key_weight), (value_low, value_weight)]
    )
    branch_first, attn_gain_total = norm_back(
        grad_first, saved["unit_first"], saved["inverse_first"], attn_gain
    )
    grads = (
        attn_gain_total,
        ffn_gain_total,
        jnp.stack([query_gain_total, key_gain_total]),
        query_total,
        key_total,
        value_total,
        out_total,
        gate_total,
        up_total,
        down_total,
    )
    return (grad_middle + branch_first, grads)


def body(
    hidden_in,
    doc_lengths,
    cotangent,
    attn_gain,
    ffn_gain,
    qk_gain,
    w_query,
    key_weight,
    value_weight,
    w_out,
    w_gate,
    w_up,
    w_down,
):
    rows = hidden_in.shape[0]
    tables = make_tables(doc_lengths, rows)
    layers = w_query.shape[0]

    def pick(layer_index):
        return (
            attn_gain[layer_index],
            ffn_gain[layer_index],
            qk_gain[layer_index],
            w_query[layer_index],
            key_weight[layer_index],
            value_weight[layer_index],
            w_out[layer_index],
            w_gate[layer_index],
            w_up[layer_index],
            w_down[layer_index],
        )

    stream = hidden_in.astype(jnp.float32)
    grad = cotangent.astype(jnp.float32)
    kept = []
    for layer_index in range(layers):
        saved = layer_forward(stream, pick(layer_index), tables)
        kept.append(saved)
        stream = saved["result"]
    done = [None] * layers
    gain_parts = [None] * layers
    for layer_index in range(layers - 1, -1, -1):
        grad, grads = layer_backward(kept[layer_index], grad, pick(layer_index), tables)
        gain_parts[layer_index] = grads[2]
        wide = grads[:2] + grads[3:]
        done[layer_index] = wide
    stacked = [jnp.stack([part[position] for part in done]) for position in range(9)]
    totals = list(
        (
            lax.psum_scatter(
                stacked[0].astype(jnp.bfloat16), "ctx", scatter_dimension=1, tiled=True
            ).astype(jnp.float32),
            lax.psum_scatter(
                stacked[1].astype(jnp.bfloat16), "ctx", scatter_dimension=1, tiled=True
            ).astype(jnp.float32),
            lax.psum_scatter(
                stacked[2].astype(jnp.bfloat16), "ctx", scatter_dimension=1, tiled=True
            ).astype(jnp.float32),
            lax.psum_scatter(
                stacked[3].astype(jnp.bfloat16), "ctx", scatter_dimension=1, tiled=True
            ).astype(jnp.float32),
            lax.psum_scatter(
                stacked[4].astype(jnp.bfloat16), "ctx", scatter_dimension=1, tiled=True
            ).astype(jnp.float32),
            lax.psum_scatter(
                stacked[5].astype(jnp.bfloat16), "ctx", scatter_dimension=1, tiled=True
            ).astype(jnp.float32),
            lax.psum_scatter(
                stacked[6].astype(jnp.bfloat16), "ctx", scatter_dimension=1, tiled=True
            ).astype(jnp.float32),
            lax.psum_scatter(
                stacked[7].astype(jnp.bfloat16), "ctx", scatter_dimension=1, tiled=True
            ).astype(jnp.float32),
            lax.psum_scatter(
                stacked[8].astype(jnp.bfloat16), "ctx", scatter_dimension=1, tiled=True
            ).astype(jnp.float32),
        )
    )
    qk_total = lax.psum(jnp.stack(gain_parts), ("ctx", "tp"))
    hidden_out = stream.astype(jnp.bfloat16)
    return (
        hidden_out,
        grad,
        totals[0],
        totals[1],
        qk_total,
        totals[2],
        totals[3],
        totals[4],
        totals[5],
        totals[6],
        totals[7],
        totals[8],
    )


def solution(mesh):
    placed = (
        P("ctx", None),
        P(),
        P("ctx", None),
        P(),
        P(),
        P(),
        P(None, None, "tp"),
        P(None, None, "tp"),
        P(None, None, "tp"),
        P(None, "tp", None),
        P(None, None, "tp"),
        P(None, None, "tp"),
        P(None, "tp", None),
    )
    return jax.shard_map(
        body,
        mesh=mesh,
        in_specs=placed,
        out_specs=(
            P("ctx", None),
            P("ctx", None),
            P(None, "ctx"),
            P(None, "ctx"),
            P(),
            P(None, "ctx", "tp"),
            P(None, "ctx", "tp"),
            P(None, "ctx", "tp"),
            P(None, ("tp", "ctx"), None),
            P(None, "ctx", "tp"),
            P(None, "ctx", "tp"),
            P(None, ("tp", "ctx"), None),
        ),
        check_vma=False,
    )
```

profile of v0, /device:TPU:0, one launch (start us, length us, event | category | flops | bytes accessed | tf_op | source)
XLA Modules:
  0.0 1244.3 jit_solution(14803500007163848702)
XLA Ops:
  13.4 5.6 collective-permute-start.2
  23.8 3.3 collective-permute-start.1
  28.6 2.8 collective-permute-start
  33.9 3.5 multiply_reduce_fusion.8
  37.6 3.0 fusion.19
  44.8 7.3 fusion.179
  52.0 3.1 fusion.6
  55.2 4.2 copy-done
  59.4 6.1 fusion.95
  65.5 3.6 convolution_convert_fusion.1
  69.5 68.3 %all-reduce.9.cloned.1.call-done = bf16[768,1024]{1,0:T(8,128)(2,1)} async-done(((bf16[768,1024]{1,0:T(8,128)(2,1)}), bf16[768,1024]{1,0:T(8,128)(2,1)}) %all-reduce.9.cloned.1.call-update) | async-done | bytes 1572880 | tf_op jit(solution)/shard_map/psum | solution.py:88
  144.3 2.9 multiply_convert_fusion.8
  148.3 2.5 convolution_convert_fusion.9
  154.4 64.8 %all-reduce.11.cloned.1.call-done = bf16[768,1024]{1,0:T(8,128)(2,1)} async-done(((bf16[768,1024]{1,0:T(8,128)(2,1)}), bf16[768,1024]{1,0:T(8,128)(2,1)}) %all-reduce.11.cloned.1.call-update) | async-done | bytes 1572880 | tf_op jit(solution)/shard_map/psum | solution.py:88
  219.2 2.7 multiply_reduce_fusion.1
  227.8 3.4 collective-permute-start.6
  237.9 4.1 collective-permute-start.5
  242.1 3.1 collective-permute-start.4
  245.8 6.8 fusion.180
  252.7 3.1 fusion.7
  255.8 4.2 copy-done.1
  260.0 5.4 fusion.94
  265.4 3.8 convolution_convert_fusion
  269.4 66.3 %all-reduce.13.cloned.1.call-done = bf16[768,1024]{1,0:T(8,128)(2,1)} async-done(((bf16[768,1024]{1,0:T(8,128)(2,1)}), bf16[768,1024]{1,0:T(8,128)(2,1)}) %all-reduce.13.cloned.1.call-update) | async-done | bytes 1572880 | tf_op jit(solution)/shard_map/psum | solution.py:88
  335.7 2.8 multiply_reduce_fusion
  338.9 2.7 copy-done.133
  346.4 3.6 multiply_convert_fusion.5
  351.5 2.6 add_convert_fusion.3
  354.9 67.5 %all-reduce.15.cloned.1.call-done = bf16[768,1024]{1,0:T(8,128)(2,1)} async-done(((bf16[768,1024]{1,0:T(8,128)(2,1)}), bf16[768,1024]{1,0:T(8,128)(2,1)}) %all-reduce.15.cloned.1.call-update) | async-done | bytes 1572880 | tf_op jit(solution)/shard_map/psum | solution.py:96
  422.4 3.1 fusion.42
  428.9 12.6 %fusion.182 = (bf16[1792,2,128]{0,2,1:T(8,128)(2,1)S(1)}, f32[1792,2,128]{0,2,1:T(8,128)}) fusion(bf16[768,2,2,128]{0,3,2,1:T(8,128)(2,1)S(1)} %bitcast.338, f32[2,2,768,1792]{2,3,1,0:T(8,128)} %copy-done.1, f32[2,2,768]{2,1,0:T(2,128)S(1)} %log_add_fusion.1), kind=kOutput, calls=%fused_computation.349 | convolution fusion | flops 1420754944 | bytes 25571328 | tf_op jit(solution)/shard_map/while/body/eval_jaxpr/grqk,qgrd->kgd/dot_general | solution.py:182
  442.9 14.2 %fusion.3 = (f32[2,2,768]{2,1,0:T(2,128)S(1)}, f32[2,1792,768,2]{2,1,3,0:T(8,128)}) fusion(f32[2,2,768,1792]{2,3,1,0:T(8,128)} %copy-done.1, f32[2,2,768]{2,1,0:T(2,128)S(1)} %log_add_fusion.1, bf16[768,2,2,128]{0,3,2,1:T(8,128)(2,1)S(1)} %bitcast.339, bf16[768,2,128]{0,2,1:T(8,128)(2,1)} %bitcast.31, bf16[768,2,128]{0,2,1:T(8,128)(2,1)} %collective-permute-done.5, ...), kind=kOutput, calls=%fused_computation.7 | convolution fusion | flops 1428550656 | bytes 45768704 | tf_op jit(solution)/shard_map/while/body/eval_jaxpr/qgrd,kgd->grqk/dot_general | solution.py:166
  457.1 15.1 %fusion.5 = bf16[2,2,768,1792]{2,3,1,0:T(8,128)(2,1)S(1)} fusion(f32[2,1792,768,2]{2,1,3,0:T(8,128)} %get-tuple-element.352, f32[2,2,768,1792]{2,3,1,0:T(8,128)} %copy-done.1, f32[2,2,768]{2,1,0:T(2,128)S(1)} %get-tuple-element.351, f32[2,2,768]{2,1,0:T(2,128)S(1)} %log_add_fusion.1), kind=kLoop, calls=%fused_computation.9 | loop fusion | flops 22020096 | bytes 55074816 | tf_op jit(solution)/shard_map/while/body/eval_jaxpr/convert_element_type | solution.py:170
  472.3 4.0 fusion.181
  481.6 2.7 convolution_multiply_fusion.1
  496.7 72.2 %all-reduce.17.cloned.1.call-done = bf16[768,1024]{1,0:T(8,128)(2,1)} async-done(((bf16[768,1024]{1,0:T(8,128)(2,1)}), bf16[768,1024]{1,0:T(8,128)(2,1)}) %all-reduce.17.cloned.1.call-update) | async-done | bytes 1572880 | tf_op jit(solution)/shard_map/psum | solution.py:96
  568.9 3.1 fusion.43
  581.3 2.6 add_convert_fusion.1
  584.7 3.0 fusion.115
  587.7 3.1 fusion.113
  590.8 61.4 %all-reduce.19.cloned.1.call-done = bf16[768,1024]{1,0:T(8,128)(2,1)} async-done(((bf16[768,1024]{1,0:T(8,128)(2,1)}), bf16[768,1024]{1,0:T(8,128)(2,1)}) %all-reduce.19.cloned.1.call-update) | async-done | bytes 1572880 | tf_op jit(solution)/shard_map/psum | solution.py:96
  652.3 2.8 fusion.44
  658.5 12.4 fusion.184
  673.1 13.8 %fusion = (f32[2,2,768]{2,1,0:T(2,128)S(1)}, f32[2,1792,768,2]{2,1,3,0:T(8,128)}) fusion(f32[2,2,768,1792]{2,3,1,0:T(8,128)} %copy-done, f32[2,2,768]{2,1,0:T(2,128)S(1)} %log_add_fusion, bf16[768,2,2,128]{0,3,2,1:T(8,128)(2,1)S(1)} %bitcast.337, bf16[768,2,128]{0,2,1:T(8,128)(2,1)} %bitcast.3, bf16[768,2,128]{0,2,1:T(8,128)(2,1)} %collective-permute-done.1, ...), kind=kOutput, calls=%fused_computation.2 | convolution fusion | flops 1428550656 | bytes 45768704 | tf_op jit(solution)/shard_map/while/body/eval_jaxpr/qgrd,kgd->grqk/dot_general | solution.py:166
  686.9 15.1 %fusion.2 = bf16[2,2,768,1792]{2,3,1,0:T(8,128)(2,1)S(1)} fusion(f32[2,1792,768,2]{2,1,3,0:T(8,128)} %get-tuple-element.358, f32[2,2,768,1792]{2,3,1,0:T(8,128)} %copy-done, f32[2,2,768]{2,1,0:T(2,128)S(1)} %get-tuple-element.357, f32[2,2,768]{2,1,0:T(2,128)S(1)} %log_add_fusion), kind=kLoop, calls=%fused_computation.4 | loop fusion | flops 22020096 | bytes 55074816 | tf_op jit(solution)/shard_map/while/body/eval_jaxpr/convert_element_type | solution.py:170
  702.0 5.3 fusion.183
  718.9 6.3 collective-permute-done.12
  735.6 2.8 fusion.93
  742.3 3.3 fusion.91
  749.1 3.3 fusion.89
  755.9 3.3 fusion.111
  765.3 6.2 convolution_multiply_fusion
  778.1 4.1 convolution_convert_fusion.8
  788.8 39.1 %psum.71 = f32[2,2,128]{2,1,0:T(2,128)} all-reduce(f32[2,2,128]{2,1,0:T(2,128)S(1)} %pad_maximum_fusion.21), channel_id=1, replica_groups=mesh['ctx'=8,'tp'=4] {'ctx','tp'}, use_global_device_ids=true, to_apply=%region_44.45 | all-reduce | flops 512 | bytes 4096 | tf_op jit(solution)/shard_map/psum | solution.py:427
  829.6 6.7 reduce-scatter.16.cloned.1.call-done
  837.9 48.3 %reduce-scatter.26.cloned.1.call-done = bf16[2,96,1024]{2,1,0:T(8,128)(2,1)} async-done(((bf16[2,768,1024]{2,1,0:T(8,128)(2,1)}), bf16[2,96,1024]{2,1,0:T(8,128)(2,1)}) %reduce-scatter.26.cloned.1.call-update) | async-done | bytes 393232 | tf_op jit(solution)/shard_map/reduce_scatter | solution.py:422
  888.1 47.7 %reduce-scatter.24.cloned.1.call-done = bf16[2,128,768]{2,1,0:T(8,128)(2,1)} async-done(((bf16[2,1024,768]{2,1,0:T(8,128)(2,1)}), bf16[2,128,768]{2,1,0:T(8,128)(2,1)}) %reduce-scatter.24.cloned.1.call-update) | async-done | bytes 393232 | tf_op jit(solution)/shard_map/reduce_scatter | solution.py:419
  937.7 48.5 %reduce-scatter.22.cloned.1.call-done = bf16[2,128,768]{2,1,0:T(8,128)(2,1)} async-done(((bf16[2,1024,768]{2,1,0:T(8,128)(2,1)}), bf16[2,128,768]{2,1,0:T(8,128)(2,1)}) %reduce-scatter.22.cloned.1.call-update) | async-done | bytes 393232 | tf_op jit(solution)/shard_map/reduce_scatter | solution.py:416
  988.1 42.6 %reduce-scatter.20.cloned.1.call-done = bf16[2,64,1024]{2,1,0:T(8,128)(2,1)} async-done(((bf16[2,512,1024]{2,1,0:T(8,128)(2,1)}), bf16[2,64,1024]{2,1,0:T(8,128)(2,1)}) %reduce-scatter.20.cloned.1.call-update) | async-done | bytes 262160 | tf_op jit(solution)/shard_map/reduce_scatter | solution.py:413
  1032.5 43.0 %reduce-scatter.14.cloned.1.call-done = bf16[2,128,512]{2,1,0:T(8,128)(2,1)} async-done(((bf16[2,1024,512]{2,1,0:T(8,128)(2,1)}), bf16[2,128,512]{2,1,0:T(8,128)(2,1)}) %reduce-scatter.14.cloned.1.call-update) | async-done | bytes 262160 | tf_op jit(solution)/shard_map/reduce_scatter | solution.py:404
  1077.3 122.5 %all-reduce.21.cloned.1.call-done = (bf16[768,1024]{1,0:T(8,128)(2,1)}, bf16[768,1024]{1,0:T(8,128)(2,1)}) async-done(((bf16[768,1024]{1,0:T(8,128)(2,1)}, bf16[768,1024]{1,0:T(8,128)(2,1)}), (bf16[768,1024]{1,0:T(8,128)(2,1)}, bf16[768,1024]{1,0:T(8,128)(2,1)})) %all-reduce.21.cloned.1.call-update) | async-done | bytes 3145744 | tf_op jit(solution)/shard_map/psum | solution.py:88
  1199.8 2.7 fusion.47
  1203.4 4.6 fusion.32
  1209.8 26.4 %reduce-scatter.28.cloned.1.call-done = bf16[128,2]{1,0:T(8,128)(2,1)} async-done(((bf16[1024,2]{1,0:T(8,128)(2,1)}), bf16[128,2]{1,0:T(8,128)(2,1)}) %reduce-scatter.28.cloned.1.call-update) | async-done | bytes 528
  (513 shorter events, 156.7 us)
Async XLA Ops:
  7.2 130.6 %all-reduce.9.cloned.1.call-start = ((), (), s32[]{:S(2)}) async-start(), calls=%async_computation.9 | async-start | bytes 3145728 | tf_op jit(solution)/shard_map/psum | solution.py:88
  8.1 25.9 %copy-start.110 = (f32[1,1024]{1,0:T(1,128)}, f32[1,1024]{1,0:T(1,128)S(1)}, u32[]{:S(2)}) copy-start(f32[1,1024]{1,0:T(1,128)S(1)} %get-tuple-element.330) | copy-start | bytes 12292
  8.1 213.8 %copy-start.98 = (f32[1,1024]{1,0:T(1,128)}, f32[1,1024]{1,0:T(1,128)S(1)}, u32[]{:S(2)}) copy-start(f32[1,1024]{1,0:T(1,128)S(1)} %get-tuple-element.329) | copy-start | bytes 12292
  10.0 23.9 %copy-start.108 = (f32[768]{0:T(1024)}, f32[768]{0:T(1024)S(1)}, u32[]{:S(2)}) copy-start(f32[768]{0:T(1024)S(1)} %add_rsqrt_fusion.7) | copy-start | bytes 9220
  12.0 28.6 %copy-start.120 = (f32[128]{0:T(128)}, f32[128]{0:T(128)S(1)}, u32[]{:S(2)}) copy-start(f32[128]{0:T(128)S(1)} %get-tuple-element.334) | copy-start | bytes 1540
  12.0 212.2 %copy-start.117 = (f32[128]{0:T(128)}, f32[128]{0:T(128)S(1)}, u32[]{:S(2)}) copy-start(f32[128]{0:T(128)S(1)} %get-tuple-element.336) | copy-start | bytes 1540
  12.0 222.3 %copy-start.122 = (f32[128]{0:T(128)}, f32[128]{0:T(128)S(1)}, u32[]{:S(2)}) copy-start(f32[128]{0:T(128)S(1)} %get-tuple-element.333) | copy-start | bytes 1540
  13.4 10.4 copy-start.48
  13.4 10.4 copy-start.50
  13.4 31.4 %collective-permute-start.2 = (bf16[256,2,128]{0,2,1:T(8,128)(2,1)S(1)}, bf16[256,2,128]{0,2,1:T(8,128)(2,1)}, u32[]{:S(2)}, u32[]{:S(2)}) collective-permute-start(bf16[256,2,128]{0,2,1:T(8,128)(2,1)S(1)} %fusion.157), channel_id=1, source_target_pairs={{0,8},{4,12},{8,16},{12,20},{16,24},{20,28},{1,9},{5,13},{9,17},{1... | collective-permute-start | bytes 393224 | tf_op jit(solution)/shard_map/ppermute | solution.py:17
  19.8 11.7 copy-start.21
  19.8 24.9 %collective-permute-start.3 = (bf16[768,2,128]{0,2,1:T(8,128)(2,1)}, bf16[768,2,128]{0,2,1:T(8,128)(2,1)}, u32[]{:S(2)}, u32[]{:S(2)}) collective-permute-start(bf16[768,2,128]{0,2,1:T(8,128)(2,1)} %pad_maximum_fusion.13), channel_id=1, source_target_pairs={{0,4},{4,8},{8,12},{12,16},{16,20},{20,24},{24,28},{1,5},{5,9},{9,... | collective-permute-start | bytes 1179656 | tf_op jit(solution)/shard_map/ppermute | solution.py:17
  23.8 31.4 %collective-permute-start.1 = (bf16[768,2,128]{0,2,1:T(8,128)(2,1)}, bf16[768,2,128]{0,2,1:T(8,128)(2,1)}, u32[]{:S(2)}, u32[]{:S(2)}) collective-permute-start(bf16[768,2,128]{0,2,1:T(8,128)(2,1)} %bitcast.3), channel_id=1, source_target_pairs={{0,4},{4,8},{8,12},{12,16},{16,20},{20,24},{24,28},{1,5},{5,9},{9,... | collective-permute-start | bytes 1179656 | tf_op jit(solution)/shard_map/ppermute | solution.py:17
  28.6 26.5 %collective-permute-start = (bf16[256,2,128]{0,2,1:T(8,128)(2,1)}, bf16[256,2,128]{0,2,1:T(8,128)(2,1)S(1)}, u32[]{:S(2)}, u32[]{:S(2)}) collective-permute-start(bf16[256,2,128]{0,2,1:T(8,128)(2,1)} %bitcast.2), channel_id=1, source_target_pairs={{0,8},{4,12},{8,16},{12,20},{16,24},{20,28},{1,9},{5,13},{9,17},{1... | collective-permute-start | bytes 393224 | tf_op jit(solution)/shard_map/ppermute | solution.py:17
  55.1 10.4 copy-start.104
  55.1 10.4 copy-start.84
  69.2 150.0 %all-reduce.11.cloned.1.call-start = ((), (), s32[]{:S(2)}) async-start(), calls=%async_computation.10 | async-start | bytes 3145728 | tf_op jit(solution)/shard_map/psum | solution.py:88
  69.5 71.1 %copy-start.100 = (f32[1,1024]{1,0:T(1,128)}, f32[1,1024]{1,0:T(1,128)S(1)}, u32[]{:S(2)}) copy-start(f32[1,1024]{1,0:T(1,128)S(1)} %get-tuple-element.328) | copy-start | bytes 12292
  69.5 269.1 %copy-start.92 = (f32[1,1024]{1,0:T(1,128)}, f32[1,1024]{1,0:T(1,128)S(1)}, u32[]{:S(2)}) copy-start(f32[1,1024]{1,0:T(1,128)S(1)} %get-tuple-element.327) | copy-start | bytes 12292
  150.9 184.8 %all-reduce.13.cloned.1.call-start = ((), (), s32[]{:S(2)}) async-start(), calls=%async_computation.11 | async-start | bytes 3145728 | tf_op jit(solution)/shard_map/psum | solution.py:88
  223.5 9.7 copy-start.64
  227.8 17.4 %collective-permute-start.6 = (bf16[256,2,128]{0,2,1:T(8,128)(2,1)S(1)}, bf16[256,2,128]{0,2,1:T(8,128)(2,1)S(1)}, u32[]{:S(2)}, u32[]{:S(2)}) collective-permute-start(bf16[256,2,128]{0,2,1:T(8,128)(2,1)S(1)} %fusion.156), channel_id=1, source_target_pairs={{0,8},{4,12},{8,16},{12,20},{16,24},{20,28},{1,9},{5,13},{9,17},{1... | collective-permute-start | bytes 393224 | tf_op jit(solution)/shard_map/ppermute | solution.py:17
  231.2 14.6 %collective-permute-start.7 = (bf16[768,2,128]{0,2,1:T(8,128)(2,1)S(1)}, bf16[768,2,128]{0,2,1:T(8,128)(2,1)}, u32[]{:S(2)}, u32[]{:S(2)}) collective-permute-start(bf16[768,2,128]{0,2,1:T(8,128)(2,1)S(1)} %pad_maximum_fusion.14), channel_id=1, source_target_pairs={{0,4},{4,8},{8,12},{12,16},{16,20},{20,24},{24,28},{1,5},{5,9},{9,... | collective-permute-start | bytes 1179656 | tf_op jit(solution)/shard_map/ppermute | solution.py:17
  235.8 16.8 %copy-start.43 = (bf16[768,2,2,64]{3,0,2,1:T(8,128)(2,1)}, bf16[768,2,2,64]{3,0,2,1:T(8,128)(2,1)S(1)}, u32[]{:S(2)}) copy-start(bf16[768,2,2,64]{3,0,2,1:T(8,128)(2,1)S(1)} %copy.81) | copy-start | bytes 1179652
  236.2 16.4 %copy-start.45 = (bf16[768,2,2,64]{3,0,2,1:T(8,128)(2,1)}, bf16[768,2,2,64]{3,0,2,1:T(8,128)(2,1)S(1)}, u32[]{:S(2)}) copy-start(bf16[768,2,2,64]{3,0,2,1:T(8,128)(2,1)S(1)} %copy.82) | copy-start | bytes 1179652
  237.9 17.8 %collective-permute-start.5 = (bf16[768,2,128]{0,2,1:T(8,128)(2,1)}, bf16[768,2,128]{0,2,1:T(8,128)(2,1)}, u32[]{:S(2)}, u32[]{:S(2)}) collective-permute-start(bf16[768,2,128]{0,2,1:T(8,128)(2,1)} %bitcast.31), channel_id=1, source_target_pairs={{0,4},{4,8},{8,12},{12,16},{16,20},{20,24},{24,28},{1,5},{5,9},{9,... | collective-permute-start | bytes 1179656 | tf_op jit(solution)/shard_map/ppermute | solution.py:17
  242.1 13.7 %collective-permute-start.4 = (bf16[256,2,128]{0,2,1:T(8,128)(2,1)}, bf16[256,2,128]{0,2,1:T(8,128)(2,1)S(1)}, u32[]{:S(2)}, u32[]{:S(2)}) collective-permute-start(bf16[256,2,128]{0,2,1:T(8,128)(2,1)} %bitcast.30), channel_id=1, source_target_pairs={{0,8},{4,12},{8,16},{12,20},{16,24},{20,28},{1,9},{5,13},{9,17},{1... | collective-permute-start | bytes 393224 | tf_op jit(solution)/shard_map/ppermute | solution.py:17
  269.2 153.2 %all-reduce.15.cloned.1.call-start = ((), (), s32[]{:S(2)}) async-start(), calls=%async_computation.12 | async-start | bytes 3145728 | tf_op jit(solution)/shard_map/psum | solution.py:96
  338.5 87.0 %copy-start.4 = (f32[768,1024]{1,0:T(8,128)}, f32[768,1024]{1,0:T(8,128)S(1)}, u32[]{:S(2)}) copy-start(f32[768,1024]{1,0:T(8,128)S(1)} %get-tuple-element.299) | copy-start | bytes 9437188
  354.1 214.8 %all-reduce.17.cloned.1.call-start = ((), (), s32[]{:S(2)}) async-start(), calls=%async_computation.13 | async-start | bytes 3145728 | tf_op jit(solution)/shard_map/psum | solution.py:96
  428.9 14.0 %copy-start.87 = (bf16[256,2,128]{0,2,1:T(8,128)(2,1)S(1)}, bf16[256,2,128]{0,2,1:T(8,128)(2,1)}, u32[]{:S(2)}) copy-start(bf16[256,2,128]{0,2,1:T(8,128)(2,1)} %copy-done.86) | copy-start | bytes 393220
  457.1 15.2 %copy-start.44 = (bf16[768,2,2,64]{3,0,2,1:T(8,128)(2,1)S(1)}, bf16[768,2,2,64]{3,0,2,1:T(8,128)(2,1)}, u32[]{:S(2)}) copy-start(bf16[768,2,2,64]{3,0,2,1:T(8,128)(2,1)} %copy-done.43) | copy-start | bytes 1179652
  457.1 15.2 %copy-start.46 = (bf16[768,2,2,64]{3,0,2,1:T(8,128)(2,1)S(1)}, bf16[768,2,2,64]{3,0,2,1:T(8,128)(2,1)}, u32[]{:S(2)}) copy-start(bf16[768,2,2,64]{3,0,2,1:T(8,128)(2,1)} %copy-done.45) | copy-start | bytes 1179652
  476.4 13.8 %collective-permute-start.10 = (bf16[256,2,128]{0,2,1:T(8,128)(2,1)}, bf16[256,2,128]{0,2,1:T(8,128)(2,1)S(1)}, u32[]{:S(2)}, u32[]{:S(2)}) collective-permute-start(bf16[256,2,128]{0,2,1:T(8,128)(2,1)} %slice.470), channel_id=1, source_target_pairs={{8,0},{12,4},{16,8},{20,12},{24,16},{28,20},{9,1},{13,5},{17,9},{2... | collective-permute-start | bytes 393224 | tf_op jit(solution)/shard_map/ppermute | solution.py:17
  477.7 16.1 %collective-permute-start.11 = (bf16[768,2,128]{0,2,1:T(8,128)(2,1)}, bf16[768,2,128]{0,2,1:T(8,128)(2,1)S(1)}, u32[]{:S(2)}, u32[]{:S(2)}) collective-permute-start(bf16[768,2,128]{0,2,1:T(8,128)(2,1)} %slice.471), channel_id=1, source_target_pairs={{4,0},{8,4},{12,8},{16,12},{20,16},{24,20},{28,24},{5,1},{9,5},{13... | collective-permute-start | bytes 1179656 | tf_op jit(solution)/shard_map/ppermute | solution.py:17
  479.0 12.0 collective-permute-start.8
  480.3 10.8 collective-permute-start.9
  494.6 74.3 %copy-start.7 = (f32[768,1024]{1,0:T(8,128)S(1)}, f32[768,1024]{1,0:T(8,128)}, u32[]{:S(2)}) copy-start(f32[768,1024]{1,0:T(8,128)} %copy-done.6) | copy-start | bytes 9437188
  494.6 74.3 %copy-start.97 = (f32[768]{0:T(1024)S(1)}, f32[768]{0:T(1024)}, u32[]{:S(2)}) copy-start(f32[768]{0:T(1024)} %copy-done.96) | copy-start | bytes 9220
  494.6 74.3 %copy-start.99 = (f32[1,1024]{1,0:T(1,128)S(1)}, f32[1,1024]{1,0:T(1,128)}, u32[]{:S(2)}) copy-start(f32[1,1024]{1,0:T(1,128)} %copy-done.98) | copy-start | bytes 12292
  496.5 155.8 %all-reduce.19.cloned.1.call-start = ((), (), s32[]{:S(2)}) async-start(), calls=%async_computation.14 | async-start | bytes 3145728 | tf_op jit(solution)/shard_map/psum | solution.py:96
  584.0 203.4 %reduce-scatter.30.cloned.1.call-start = ((), (), s32[]{:S(2)}) async-start(), calls=%async_computation.23 | async-start | bytes 294912
  584.7 67.6 %copy-start.3 = (bf16[768,1024]{1,0:T(8,128)(2,1)S(1)}, bf16[768,1024]{1,0:T(8,128)(2,1)}, u32[]{:S(2)}) copy-start(bf16[768,1024]{1,0:T(8,128)(2,1)} %param.37) | copy-start | bytes 4718596
  584.7 67.6 %copy-start.10 = (bf16[768,1024]{1,0:T(8,128)(2,1)S(1)}, bf16[768,1024]{1,0:T(8,128)(2,1)}, u32[]{:S(2)}) copy-start(bf16[768,1024]{1,0:T(8,128)(2,1)} %all-reduce.9.cloned.1.call-done) | copy-start | bytes 4718596
  584.7 67.6 %copy-start.95 = (f32[768]{0:T(1024)S(1)}, f32[768]{0:T(1024)}, u32[]{:S(2)}) copy-start(f32[768]{0:T(1024)} %copy-done.94) | copy-start | bytes 9220
  658.5 14.6 %copy-start.85 = (bf16[256,2,128]{0,2,1:T(8,128)(2,1)S(1)}, bf16[256,2,128]{0,2,1:T(8,128)(2,1)}, u32[]{:S(2)}) copy-start(bf16[256,2,128]{0,2,1:T(8,128)(2,1)} %copy-done.84) | copy-start | bytes 393220
  670.8 16.0 %copy-start.47 = (bf16[1792,2,128]{0,2,1:T(8,128)(2,1)}, bf16[1792,2,128]{0,2,1:T(8,128)(2,1)S(1)}, u32[]{:S(2)}) copy-start(bf16[1792,2,128]{0,2,1:T(8,128)(2,1)S(1)} %get-tuple-element.361) | copy-start | bytes 2752516
  671.6 46.3 %collective-permute-start.14 = (bf16[256,2,128]{0,2,1:T(8,128)(2,1)}, bf16[256,2,128]{0,2,1:T(8,128)(2,1)}, u32[]{:S(2)}, u32[]{:S(2)}) collective-permute-start(bf16[256,2,128]{0,2,1:T(8,128)(2,1)} %slice.482), channel_id=1, source_target_pairs={{8,0},{12,4},{16,8},{20,12},{24,16},{28,20},{9,1},{13,5},{17,9},{2... | collective-permute-start | bytes 393224 | tf_op jit(solution)/shard_map/ppermute | solution.py:17
  686.8 15.2 %copy-start.41 = (bf16[768,2,2,64]{3,0,2,1:T(8,128)(2,1)S(1)}, bf16[768,2,2,64]{3,0,2,1:T(8,128)(2,1)}, u32[]{:S(2)}) copy-start(bf16[768,2,2,64]{3,0,2,1:T(8,128)(2,1)} %copy.75) | copy-start | bytes 1179652
  686.8 15.2 %copy-start.42 = (bf16[768,2,2,64]{3,0,2,1:T(8,128)(2,1)S(1)}, bf16[768,2,2,64]{3,0,2,1:T(8,128)(2,1)}, u32[]{:S(2)}) copy-start(bf16[768,2,2,64]{3,0,2,1:T(8,128)(2,1)} %copy.76) | copy-start | bytes 1179652
  711.7 14.4 %collective-permute-start.15 = (bf16[768,2,128]{0,2,1:T(8,128)(2,1)}, bf16[768,2,128]{0,2,1:T(8,128)(2,1)}, u32[]{:S(2)}, u32[]{:S(2)}) collective-permute-start(bf16[768,2,128]{0,2,1:T(8,128)(2,1)} %slice.483), channel_id=1, source_target_pairs={{4,0},{8,4},{12,8},{16,12},{20,16},{24,20},{28,24},{5,1},{9,5},{13... | collective-permute-start | bytes 1179656 | tf_op jit(solution)/shard_map/ppermute | solution.py:17
  714.2 13.8 %copy-start.109 = (f32[768]{0:T(1024)S(1)}, f32[768]{0:T(1024)}, u32[]{:S(2)}) copy-start(f32[768]{0:T(1024)} %copy-done.108) | copy-start | bytes 9220
  714.2 13.8 %copy-start.111 = (f32[1,1024]{1,0:T(1,128)S(1)}, f32[1,1024]{1,0:T(1,128)}, u32[]{:S(2)}) copy-start(f32[1,1024]{1,0:T(1,128)} %copy-done.110) | copy-start | bytes 12292
  714.2 10.9 collective-permute-start.12
  715.5 14.5 %collective-permute-start.13 = (bf16[768,2,128]{0,2,1:T(8,128)(2,1)}, bf16[768,2,128]{0,2,1:T(8,128)(2,1)}, u32[]{:S(2)}, u32[]{:S(2)}) collective-permute-start(bf16[768,2,128]{0,2,1:T(8,128)(2,1)} %slice.477), channel_id=1, source_target_pairs={{4,0},{8,4},{12,8},{16,12},{20,16},{24,20},{28,24},{5,1},{9,5},{13... | collective-permute-start | bytes 1179656 | tf_op jit(solution)/shard_map/ppermute | solution.py:17
  717.8 110.2 %reduce-scatter.18.cloned.1.call-start = ((), (), s32[]{:S(2)}) async-start(), calls=%async_computation.17 | async-start | bytes 1179648 | tf_op jit(solution)/shard_map/reduce_scatter | solution.py:410
  730.0 106.3 %reduce-scatter.16.cloned.1.call-start = ((), (), s32[]{:S(2)}) async-start(), calls=%async_computation.16 | async-start | bytes 1179648 | tf_op jit(solution)/shard_map/reduce_scatter | solution.py:407
  734.9 151.2 %reduce-scatter.26.cloned.1.call-start = ((), (), s32[]{:S(2)}) async-start(), calls=%async_computation.21 | async-start | bytes 3538944 | tf_op jit(solution)/shard_map/reduce_scatter | solution.py:422
  741.8 193.9 %reduce-scatter.24.cloned.1.call-start = ((), (), s32[]{:S(2)}) async-start(), calls=%async_computation.20 | async-start | bytes 3538944 | tf_op jit(solution)/shard_map/reduce_scatter | solution.py:419
  749.0 237.2 %reduce-scatter.22.cloned.1.call-start = ((), (), s32[]{:S(2)}) async-start(), calls=%async_computation.19 | async-start | bytes 3538944 | tf_op jit(solution)/shard_map/reduce_scatter | solution.py:416
  755.8 274.9 %reduce-scatter.20.cloned.1.call-start = ((), (), s32[]{:S(2)}) async-start(), calls=%async_computation.18 | async-start | bytes 2359296 | tf_op jit(solution)/shard_map/reduce_scatter | solution.py:413
  761.7 313.8 %reduce-scatter.14.cloned.1.call-start = ((), (), s32[]{:S(2)}) async-start(), calls=%async_computation.15 | async-start | bytes 2359296 | tf_op jit(solution)/shard_map/reduce_scatter | solution.py:404
  776.8 423.0 %all-reduce.21.cloned.1.call-start = ((), (), s32[]{:S(2)}) async-start(), calls=%async_computation.24 | async-start | bytes 6291456 | tf_op jit(solution)/shard_map/psum | solution.py:88
  786.7 449.5 %reduce-scatter.28.cloned.1.call-start = ((), (), s32[]{:S(2)}) async-start(), calls=%async_computation.22 | async-start | bytes 294912
  (121 other events, 346.1 us)
Sparse Core Ops, SparseCore 0:
  69.3 68.4 all-reduce.8
  151.0 68.1 all-reduce.10
  269.3 66.3 all-reduce.12
  354.2 68.1 all-reduce.14
  496.6 72.2 all-reduce.16
  584.1 68.1 all-reduce.18
  717.9 38.6 reduce-scatter.29
  760.1 36.1 reduce-scatter.17
  799.8 36.3 reduce-scatter.15
  839.8 46.2 reduce-scatter.25
  889.5 46.1 reduce-scatter.23
  939.9 46.2 reduce-scatter.21
  989.5 41.2 reduce-scatter.19
  1034.2 41.2 reduce-scatter.13
  1078.3 121.4 all-reduce.20
  1203.5 32.5 reduce-scatter.27
where the time goes:
time: 1250 us; the launch traced here: 1240 us
  waiting for transfers between devices  794 us (64%)
  matrix products  179 us (14%)
  other arithmetic  111 us (9%)
  local copies, waits for them, and re-layouts  66.3 us (5%)
  starting transfers between devices  39.2 us (3%)
  blocking collectives  39.1 us (3%)
  between operations  16.4 us (1%)
    psum x4, waiting for transfers between devices, branch_total(): lax.psum(matrix_product(left, right).astype(jnp.bfloat16), 'tp')  322 us
    psum x3, waiting for transfers between devices, input_total(): return lax.psum(total.astype(jnp.bfloat16), 'tp').astype(jnp.float32)  201 us
    reduce_scatter x1, waiting for transfers between devices, body(): lax.psum_scatter(stacked[6].astype(jnp.bfloat16), 'ctx', scatter_dimensio...  48.5 us
    reduce_scatter x1, waiting for transfers between devices, body(): lax.psum_scatter(stacked[8].astype(jnp.bfloat16), 'ctx', scatter_dimensio...  48.3 us
    reduce_scatter x1, waiting for transfers between devices, body(): lax.psum_scatter(stacked[7].astype(jnp.bfloat16), 'ctx', scatter_dimensio...  47.7 us
    unnamed x310, local copies, waits for them, and re-layouts  43.7 us
    reduce_scatter x1, waiting for transfers between devices, body(): lax.psum_scatter(stacked[2].astype(jnp.bfloat16), 'ctx', scatter_dimensio...  43 us
    reduce_scatter x1, waiting for transfers between devices, body(): lax.psum_scatter(stacked[5].astype(jnp.bfloat16), 'ctx', scatter_dimensio...  42.6 us
  transfers between devices with their start and end apart: 32, of which 16 were waited for; matrix products, arithmetic and copies ran while one was open for 14% of the time, Pallas kernels for 0%

commit v1 on v0

v1 whole, which is shorter than its diff:
```python
import types

import jax
import jax.numpy as jnp
from jax import lax
from jax.experimental import pallas as pl
from jax.experimental.pallas import tpu as pltpu
from jax.sharding import PartitionSpec as P

HEAD_SIZE = 128
ATTENTION_WINDOW = 1024
EPS = 1e-06
THETA = 1000000.0

UNIT = 64
WIDE = 128
KEY_BLOCK = 384
HOP = 2
CTX = "ctx"
TP = "tp"
MESH = pl.DeviceIdType.MESH
F32 = jnp.float32
BF16 = jnp.bfloat16
SCALE = HEAD_SIZE ** (-0.5)
EXP2_SCALE = SCALE * 1.4426950408889634
ANY = pl.ANY
VMEM = pltpu.VMEM
DMA = pltpu.SemaphoreType.DMA


def dot_nn(left, right):
    return jnp.dot(left, right, preferred_element_type=F32)


def dot_nt(left, right):
    return lax.dot_general(left, right, (((1,), (1,)), ((), ())), preferred_element_type=F32)


def dot_tn(left, right):
    return lax.dot_general(left, right, (((0,), (0,)), ((), ())), preferred_element_type=F32)


def rms_inverse(value_rows):
    return lax.rsqrt(jnp.mean(value_rows * value_rows, axis=-1, keepdims=True) + EPS)


def rotate(value_rows, cosine, sine):
    return value_rows * cosine + pltpu.roll(value_rows, HEAD_SIZE // 2, 1) * sine


def unrotate(grad, cosine, sine):
    return grad * cosine + pltpu.roll(grad * sine, HEAD_SIZE // 2, 1)


def norm_back(grad, unit, inverse, gain):
    scaled = grad * gain
    inner = jnp.mean(scaled * unit, axis=-1, keepdims=True)
    return inverse * (scaled - unit * inner)


def column_sum(value_rows):
    return jnp.sum(value_rows, axis=0, keepdims=True)


def make_tables(lengths, rows):
    start = lax.axis_index(CTX) * rows
    spot = start + jnp.arange(rows, dtype=jnp.int32)
    passed = jnp.cumsum(lengths)[None, :] <= spot[:, None]
    begin = jnp.sum(jnp.where(passed, lengths[None, :], 0), axis=1)
    half = HEAD_SIZE // 2
    freq = THETA ** (-(jnp.arange(half, dtype=F32) * 2.0) / HEAD_SIZE)
    angle = (spot - begin).astype(F32)[:, None] * freq[None, :]
    cosine, sine = jnp.cos(angle), jnp.sin(angle)
    lowest = jnp.maximum(begin, spot - (ATTENTION_WINDOW - 1)) - (start - ATTENTION_WINDOW)
    return types.SimpleNamespace(
        cosine=jnp.concatenate([cosine, cosine], axis=1),
        sine=jnp.concatenate([-sine, sine], axis=1),
        lowest=lowest[:, None],
    )


def halo_plan(rows):
    reach = -(-ATTENTION_WINDOW // rows)
    plan = []
    for hop in range(1, reach + 1):
        need = min(rows, ATTENTION_WINDOW - (hop - 1) * rows)
        plan.append((hop, need, ATTENTION_WINDOW - (hop - 1) * rows - need))
    return plan


def unit_rows(u):
    return pl.ds(pl.multiple_of(u * UNIT, UNIT), UNIT)


def wide_rows(w):
    return pl.ds(pl.multiple_of(w * WIDE, WIDE), WIDE)


def subs(w):
    return [w * (WIDE // UNIT) + i for i in range(WIDE // UNIT)]


def shaped(*shape, kind=BF16):
    return jax.ShapeDtypeStruct(shape, kind)


def listed(value):
    return list(value) if isinstance(value, list) else [value]


def run_kernel(body, ins, outs, scratch, collective_id):
    groups = [ins, outs, scratch]
    flat = [[x for value in group.values() for x in listed(value)] for group in groups]

    def named(values, chosen):
        values = list(values)
        found = {}
        for group in chosen:
            for name, value in group.items():
                if isinstance(value, list):
                    found[name] = [values.pop(0) for unused in value]
                else:
                    found[name] = values.pop(0)
        return types.SimpleNamespace(**found)

    results = pl.pallas_call(
        lambda *refs: body(named(refs, groups)),
        out_shape=[shape for shape, unused in flat[1]],
        in_specs=[pl.BlockSpec(memory_space=space) for unused, space in flat[0]],
        out_specs=[pl.BlockSpec(memory_space=space) for unused, space in flat[1]],
        scratch_shapes=flat[2],
        compiler_params=pltpu.CompilerParams(
            collective_id=collective_id, has_side_effects=True, vmem_limit_bytes=62 * 2**20
        ),
    )(*[array for array, unused in flat[0]])
    return named(results, [outs])


def place():
    return lax.axis_index(CTX), lax.axis_index(TP)


def remote(source, target, send, receive, device):
    return pltpu.make_async_remote_copy(
        src_ref=source,
        dst_ref=target,
        send_sem=send,
        recv_sem=receive,
        device_id=device,
        device_id_type=MESH,
    )


def greet(partners):
    barrier = pltpu.get_barrier_semaphore()
    total = 0
    for exists, device in partners:
        total = total + jnp.where(exists, 1, 0)

        @pl.when(exists)
        def _():
            pl.semaphore_signal(barrier, inc=1, device_id=device, device_id_type=MESH)

    pl.semaphore_wait(barrier, total)


def line_partners():
    c, t = place()
    outer = (t == 0) | (t == 3)
    return [
        (outer, (c, jnp.where(t == 0, 1, 2))),
        (jnp.logical_not(outer), (c, jnp.where(t == 1, 0, 3))),
        (jnp.logical_not(outer), (c, jnp.clip(3 - t, 1, 2))),
    ]


def halo_partners(rows, count):
    c, t = place()
    partners = []
    for hop, unused, unused_too in halo_plan(rows):
        partners.append((c + hop < count, (jnp.minimum(c + hop, count - 1), t)))
        partners.append((c >= hop, (jnp.maximum(c - hop, 0), t)))
    return partners


class LineSum:
    def __init__(self, refs):
        self.part, self.total, self.inner, self.sems = refs
        self.c, self.t = place()
        self.outer = (self.t == 0) | (self.t == 3)
        self.is_inner = jnp.logical_not(self.outer)

    def copy(self, source, target, u, send, receive, to):
        return remote(
            source.at[u],
            target.at[u],
            self.sems.at[send, u],
            self.sems.at[receive, u],
            (self.c, to),
        )

    def inwards(self, u):
        return self.copy(self.part, self.total, u, 0, 1, jnp.where(self.t < 2, 1, 2))

    def across(self, u):
        return self.copy(self.part, self.inner, u, 0, 2, jnp.clip(3 - self.t, 1, 2))

    def outwards(self, u):
        return self.copy(self.total, self.total, u, 3, 4, jnp.where(self.t < 2, 0, 3))

    def push(self, w, value):
        for i, u in enumerate(subs(w)):
            self.part[u] = value[i * UNIT : (i + 1) * UNIT].astype(BF16)

        @pl.when(self.outer)
        def _():
            for u in subs(w):
                self.inwards(u).start()

    def meet(self, u):
        @pl.when(self.is_inner)
        def _():
            self.inwards(u).wait_recv()
            self.part[u] = (self.part[u].astype(F32) + self.total[u].astype(F32)).astype(BF16)
            self.across(u).start()

    def spread(self, u):
        @pl.when(self.is_inner)
        def _():
            self.across(u).wait_recv()
            self.total[u] = (self.part[u].astype(F32) + self.inner[u].astype(F32)).astype(BF16)
            self.outwards(u).start()

    def take(self, u):
        @pl.when(self.outer)
        def _():
            self.outwards(u).wait_recv()

        return self.total[u].astype(F32)

    def take_wide(self, w):
        return jnp.concatenate([self.take(u) for u in subs(w)], axis=0)

    def finish(self, u):
        @pl.when(self.outer)
        def _():
            self.inwards(u).wait_send()

        @pl.when(self.is_inner)
        def _():
            self.across(u).wait_send()
            self.outwards(u).wait_send()

    def stages(self, begin, hop=HOP):
        return [(begin + 2 * hop, self.spread, 1), (begin + hop, self.meet, 1)]


def line_scratch(units, width):
    block = VMEM((units, UNIT, width), BF16)
    return [block, block, block, DMA((5, units))]


def pipeline(units, stages, tasks=()):
    steps = units + max(delay + 1 - taken for delay, unused, taken in stages)

    def step(s, carry):
        for delay, function, taken in stages:
            ready = (s >= delay) & (s < units + delay)
            if taken > 1:
                ready = ready & ((s - delay) % taken == 0)

            @pl.when(ready)
            def _():
                function((s - delay) // taken if taken > 1 else s - delay)

        for at, task in tasks:
            if at < steps:

                @pl.when(s == at)
                def _():
                    task()

        return carry

    lax.fori_loop(0, steps, step, 0)
    for at, task in tasks:
        if at >= steps:
            task()


def each_of(number, function):
    def step(u, carry):
        function(u)
        return carry

    lax.fori_loop(0, number, step, 0)


class Loads:
    def __init__(self, sems):
        self.sems, self.number = sems, 0

    def __call__(self, source, target):
        copy = pltpu.make_async_copy(source, target, self.sems.at[self.number])
        copy.start()
        self.number += 1
        return copy


def wait_all(*copies):
    for copy in copies:
        copy.wait()


class Stores:
    def __init__(self, sems):
        self.sems, self.copies = sems, []

    def __call__(self, source, target):
        index = len(self.copies)

        def copy(u):
            rows = unit_rows(u)
            return pltpu.make_async_copy(source.at[rows], target.at[rows], self.sems.at[index, u])

        self.copies.append(copy)
        return copy

    def finish(self, u):
        for copy in self.copies:
            copy(u).wait()


def send_out(units, *copies):
    for u in units:
        for copy in copies:
            copy(u).start()


class Halo:
    def __init__(self, keys, sems, rows, count):
        self.keys, self.sems, self.rows, self.count = keys, sems, rows, count
        self.plan = halo_plan(rows)
        self.c, self.t = place()

    def copy(self, index, u, hop, need, offset):
        target = pl.multiple_of(offset + u * UNIT - (self.rows - need), UNIT)
        return remote(
            self.keys.at[pl.ds(pl.multiple_of(ATTENTION_WINDOW + u * UNIT, UNIT), UNIT)],
            self.keys.at[pl.ds(target, UNIT)],
            self.sems.at[2 * index, u],
            self.sems.at[2 * index + 1, u],
            (jnp.minimum(self.c + hop, self.count - 1), self.t),
        )

    def each(self, u, function, receives):
        for index, (hop, need, offset) in enumerate(self.plan):
            exists = self.c >= hop if receives else self.c + hop < self.count

            @pl.when(exists & (u >= (self.rows - need) // UNIT))
            def _():
                function(self.copy(index, u, hop, need, offset))

    def blank(self):
        width = self.keys.shape[1]
        for hop, need, offset in self.plan:

            @pl.when(self.c < hop)
            def _():
                self.keys[offset : offset + need] = jnp.zeros((need, width), BF16)

    def send(self, u):
        self.each(u, lambda copy: copy.start(), False)

    def finish(self, u):
        self.each(u, lambda copy: copy.wait_recv(), True)
        self.each(u, lambda copy: copy.wait_send(), False)


def project(n, first, number, stream, layer):
    rows = pl.ds(pl.multiple_of(first, number), number)
    own = pl.ds(pl.multiple_of(ATTENTION_WINDOW + first, number), number)
    normed = (stream * rms_inverse(stream) * n.attn_gain[layer : layer + 1]).astype(BF16)
    n.a1_v[rows] = normed
    key = dot_nn(normed, n.wk_v[...])
    query = dot_nn(normed, n.wq_v[...])
    n.qraw_v[rows] = query
    n.kraw_v[rows] = key
    cosine, sine = n.cosine[rows], n.sine[rows]
    for raw, out, out_rows, which in ((key, n.kv_v, own, 1), (query, n.q_v, rows, 0)):
        gain = n.qk_gain[layer, which : which + 1]
        for head in range(raw.shape[1] // HEAD_SIZE):
            cols = slice(head * HEAD_SIZE, (head + 1) * HEAD_SIZE)
            part = raw[:, cols]
            part = part * rms_inverse(part) * gain
            out[out_rows, cols] = rotate(part, cosine, sine).astype(BF16)
    n.kv_v[own, key.shape[1] :] = dot_nn(normed, n.wv_v[...]).astype(BF16)


def project_shapes(s):
    return dict(
        a1=((s.rows, s.model), BF16),
        qraw=((s.rows, s.queries), F32),
        kraw=((s.rows, s.keys), F32),
        q=((s.rows, s.queries), BF16),
        kv=((ATTENTION_WINDOW + s.rows, 2 * s.keys), BF16),
    )


def outputs(shapes):
    return {x: (shaped(*shape, kind=kind), ANY) for x, (shape, kind) in shapes.items()}


def buffers(shapes):
    return {x + "_v": VMEM(shape, kind) for x, (shape, kind) in shapes.items()}


def project_ins(w, tables):
    return dict(
        attn_gain=(w.attn_gain, VMEM),
        qk_gain=(w.qk_gain, VMEM),
        cosine=(tables.cosine, VMEM),
        sine=(tables.sine, VMEM),
        wq=(w.w_query, ANY),
        wk=(w.key_weight, ANY),
        wv=(w.value_weight, ANY),
    )


def project_scratch(s):
    return buffers(project_shapes(s)) | dict(
        wq_v=VMEM((s.model, s.queries), BF16),
        wk_v=VMEM((s.model, s.keys), BF16),
        wv_v=VMEM((s.model, s.keys), BF16),
        halo_sems=DMA((2 * len(halo_plan(s.rows)), s.units)),
    )


def first_projection(stream, w, tables, s):
    def body(n):
        loads = Loads(n.load_sems)
        weights = (
            loads(n.wk.at[0], n.wk_v),
            loads(n.wv.at[0], n.wv_v),
            loads(n.wq.at[0], n.wq_v),
        )
        stores = Stores(n.store_sems)
        made = (
            stores(n.a1_v, n.a1),
            stores(n.qraw_v, n.qraw),
            stores(n.kraw_v, n.kraw),
            stores(n.q_v, n.q),
        )
        halo = Halo(n.kv_v, n.halo_sems, s.rows, s.count)
        greet(halo_partners(s.rows, s.count))
        halo.blank()
        wait_all(*weights)

        def each(i):
            project(n, i * WIDE, WIDE, n.x[wide_rows(i)].astype(F32), 0)
            for u in subs(i):
                halo.send(u)
            send_out(subs(i), *made)

        each_of(s.rows // WIDE, each)
        each_of(s.units, halo.finish)
        keys = loads(n.kv_v, n.kv)
        each_of(s.units, stores.finish)
        keys.wait()

    return run_kernel(
        body,
        dict(x=(stream, VMEM)) | project_ins(w, tables),
        outputs(project_shapes(s)),
        project_scratch(s) | dict(load_sems=DMA((4,)), store_sems=DMA((4, s.units))),
        1,
    )


def key_block(i, block):
    return pl.ds(pl.multiple_of(i * WIDE + block * KEY_BLOCK, HEAD_SIZE), KEY_BLOCK)


def visible(i, lowest, block, repeat):
    shape = (WIDE, KEY_BLOCK)
    col = block * KEY_BLOCK + lax.broadcasted_iota(jnp.int32, shape, 1)
    seen = col >= lowest - i * WIDE
    if (block + 1) * KEY_BLOCK > ATTENTION_WINDOW:
        row = ATTENTION_WINDOW + lax.broadcasted_iota(jnp.int32, shape, 0)
        seen = seen & (col <= row)
    keep = jnp.where(seen, 1.0, 0.0)
    return jnp.concatenate([keep] * repeat, axis=0)


def key_blocks():
    return (ATTENTION_WINDOW + WIDE) // KEY_BLOCK


def stacked(value, group, repeat):
    first = group * repeat
    return jnp.concatenate(
        [value[:, (first + r) * HEAD_SIZE : (first + r + 1) * HEAD_SIZE] for r in range(repeat)],
        axis=0,
    )


def head_cols(index):
    return slice(index * HEAD_SIZE, (index + 1) * HEAD_SIZE)


def attend(n, i, s):
    rows = wide_rows(i)
    lowest = n.lowest[rows]
    lane = lax.broadcasted_iota(jnp.int32, (WIDE, HEAD_SIZE), 1)
    query_rows = n.qin_v[rows]
    queries = [stacked(query_rows, g, s.repeat) for g in range(s.groups)]
    mixed = [jnp.zeros((s.repeat * WIDE, HEAD_SIZE), F32) for unused in queries]
    total = [jnp.zeros((s.repeat * WIDE, 1), F32) for unused in queries]
    for block in range(key_blocks()):
        keys = key_block(i, block)
        keep = visible(i, lowest, block, s.repeat)
        for g in range(s.groups):
            scores = dot_nt(queries[g], n.kvin_v[keys, head_cols(g)])
            weights = jnp.exp2(scores * EXP2_SCALE) * keep
            total[g] = total[g] + jnp.sum(weights, axis=-1, keepdims=True)
            values = n.kvin_v[keys, head_cols(s.groups + g)]
            mixed[g] = mixed[g] + dot_nn(weights.astype(BF16), values)
    inverses = jnp.zeros((WIDE, HEAD_SIZE), F32)
    for g in range(s.groups):
        inverse = 1.0 / total[g]
        result = (mixed[g] * inverse).astype(BF16)
        for r in range(s.repeat):
            head = g * s.repeat + r
            part = slice(r * WIDE, (r + 1) * WIDE)
            n.o_v[rows, head_cols(head)] = result[part]
            inverses = jnp.where(lane == head, inverse[part], inverses)
    n.inv_v[rows] = inverses


def attend_back(n, i, grad_out, keys_ref, query_ref, s):
    rows = wide_rows(i)
    lowest = n.lowest[rows]
    query_rows, mixed_rows, inverses = query_ref[rows], n.o_v[rows], n.inv_v[rows]
    queries, grads, inners, scales, found = [], [], [], [], []
    for g in range(s.groups):
        queries.append(stacked(query_rows, g, s.repeat))
        grads.append(stacked(grad_out, g, s.repeat))
        mixed = stacked(mixed_rows, g, s.repeat)
        inners.append(
            jnp.sum(grads[g].astype(F32) * mixed.astype(F32), axis=-1, keepdims=True)
        )
        heads = [g * s.repeat + r for r in range(s.repeat)]
        scales.append(jnp.concatenate([inverses[:, h : h + 1] for h in heads], axis=0))
        found.append(jnp.zeros((s.repeat * WIDE, HEAD_SIZE), F32))
    for block in range(key_blocks()):
        keys = key_block(i, block)
        keep = visible(i, lowest, block, s.repeat)
        for g in range(s.groups):
            key_rows = keys_ref[keys, head_cols(g)]
            scores = dot_nt(queries[g], key_rows)
            probs = jnp.exp2(scores * EXP2_SCALE) * (keep * scales[g])
            grad_probs = dot_nt(grads[g], keys_ref[keys, head_cols(s.groups + g)])
            grad_scores = (probs * (grad_probs - inners[g])).astype(BF16)
            found[g] = found[g] + dot_nn(grad_scores, key_rows)
            n.dkv_v[keys, head_cols(g)] += dot_tn(grad_scores, queries[g])
            n.dkv_v[keys, head_cols(s.groups + g)] += dot_tn(probs.astype(BF16), grads[g])
    return [
        found[g][r * WIDE : (r + 1) * WIDE] for g in range(s.groups) for r in range(s.repeat)
    ]


def head_back(n, rows, grad, raw, which, layer):
    gain = n.qk_gain[layer, which : which + 1]
    turned = unrotate(grad, n.cosine[rows], n.sine[rows])
    inverse = rms_inverse(raw)
    unit = raw * inverse
    n.qk_sum[which : which + 1] += column_sum(turned * unit)
    return norm_back(turned, unit, inverse, gain).astype(BF16)


class Returns:
    def __init__(self, n, s):
        self.grads, self.low, self.back, self.sems = n.dkv_v, n.low_v, n.back_v, n.return_sems
        self.s, self.plan = s, halo_plan(s.rows)
        self.c, self.t = place()
        self.blocks = []
        for index, (hop, need, offset) in enumerate(self.plan):
            for b in range(need // WIDE):
                self.blocks.append((index, hop, offset + b * WIDE, b * WIDE))
        self.blocks.sort(key=lambda item: item[2])

    def copy(self, number):
        index, hop, source, target = self.blocks[number]
        return remote(
            self.low.at[pl.ds(source, WIDE)],
            self.back[index].at[pl.ds(target, WIDE)],
            self.sems.at[0, number],
            self.sems.at[1, number],
            (jnp.maximum(self.c - hop, 0), self.t),
        )

    def blank(self):
        for index, (hop, need, unused) in enumerate(self.plan):

            @pl.when(self.c + hop >= self.s.count)
            def _():
                self.back[index][...] = jnp.zeros((need, self.low.shape[1]), BF16)

    def send(self, number):
        rows = pl.ds(self.blocks[number][2], WIDE)

        @pl.when(self.c >= self.blocks[number][1])
        def _():
            self.low[rows] = self.grads[rows].astype(BF16)
            self.copy(number).start()

    def send_complete(self, i):
        for number, block in enumerate(self.blocks):
            if block[2] // WIDE < self.s.rows // WIDE - 1:

                @pl.when(i == block[2] // WIDE)
                def _():
                    self.send(number)

    def send_rest(self):
        for number, block in enumerate(self.blocks):
            if block[2] // WIDE >= self.s.rows // WIDE - 1:
                self.send(number)

    def receive(self):
        for number, block in enumerate(self.blocks):

            @pl.when(self.c + block[1] < self.s.count)
            def _():
                self.copy(number).wait_recv()

    def finish(self):
        for number, block in enumerate(self.blocks):

            @pl.when(self.c >= block[1])
            def _():
                self.copy(number).wait_send()


def attention_back_scratch(s):
    plan = halo_plan(s.rows)
    return dict(
        dkv_v=VMEM((ATTENTION_WINDOW + s.rows, 2 * s.keys), F32),
        low_v=VMEM((ATTENTION_WINDOW, 2 * s.keys), BF16),
        back_v=[VMEM((need, 2 * s.keys), BF16) for unused, need, unused_too in plan],
        total_v=VMEM((WIDE, 2 * s.keys), F32),
        return_sems=DMA((2, ATTENTION_WINDOW // WIDE)),
    )


def attention_back_shapes(s):
    return dict(
        dyb=((s.rows, s.model), BF16),
        dgate=((s.rows, s.hidden), BF16),
        dup=((s.rows, s.hidden), BF16),
        dhb=((s.rows, s.model), BF16),
        dq=((s.rows, s.queries), BF16),
        dk=((s.rows, s.keys), BF16),
        dv=((s.rows, s.keys), BF16),
    )


def attention_back_outs(s):
    return outputs(attention_back_shapes(s)) | dict(
        dres=(shaped(s.rows, s.model, kind=F32), ANY),
        ffn_sum=(shaped(1, s.model, kind=F32), VMEM),
        qk_sum=(shaped(2, HEAD_SIZE, kind=F32), VMEM),
    )


def back_start(n, returns):
    returns.blank()
    n.dkv_v[...] = jnp.zeros_like(n.dkv_v)
    n.ffn_sum[...] = jnp.zeros_like(n.ffn_sum)
    n.qk_sum[...] = jnp.zeros_like(n.qk_sum)


def feed_back(n, i, gate, up, lower, made):
    here = wide_rows(i)
    low = n.g_v[here].astype(BF16)
    n.dyb_v[here] = low
    grad_hidden = dot_nt(low, n.wd_v[...])
    sigma = jax.nn.sigmoid(gate)
    dgate = (grad_hidden * up * (sigma * (1.0 + gate * (1.0 - sigma)))).astype(BF16)
    dup = (grad_hidden * gate * sigma).astype(BF16)
    n.dgate_v[here] = dgate
    n.dup_v[here] = dup
    lower.push(i, dot_nt(dgate, n.wg_v[...]) + dot_nt(dup, n.wu_v[...]))
    send_out(subs(i), *made)


def attention_back(n, i, middle, keys_ref, query_ref, layer, lower, returns, made, s):
    here = wide_rows(i)
    grad_in = lower.take_wide(i)
    inverse = rms_inverse(middle)
    unit = middle * inverse
    n.ffn_sum[...] += column_sum(grad_in * unit)
    total = n.g_v[here] + norm_back(grad_in, unit, inverse, n.ffn_gain[layer : layer + 1])
    n.g_v[here] = total
    low = total.astype(BF16)
    n.dhb_v[here] = low
    grad_out = dot_nt(low, n.wo_v[...]).astype(BF16)
    pieces = attend_back(n, i, grad_out, keys_ref, query_ref, s)
    returns.send_complete(i)
    for head, piece in enumerate(pieces):
        n.dq_v[here, head_cols(head)] = head_back(
            n, here, piece * SCALE, n.qraw_v[here, head_cols(head)], 0, layer
        )
    send_out(subs(i), *made)


def keys_back(n, layer, returns, made, s):
    def each(i):
        here = wide_rows(i)
        own = pl.ds(pl.multiple_of(ATTENTION_WINDOW + i * WIDE, WIDE), WIDE)
        n.total_v[...] = n.dkv_v[own]
        for index, (hop, need, unused) in enumerate(returns.plan):
            skipped = s.rows - need

            @pl.when(i >= skipped // WIDE)
            def _():
                part = pl.ds(pl.multiple_of(i * WIDE - skipped, WIDE), WIDE)
                n.total_v[...] += n.back_v[index][part].astype(F32)

        for g in range(s.groups):
            n.dk_v[here, head_cols(g)] = head_back(
                n, here, n.total_v[:, head_cols(g)] * SCALE, n.kraw_v[here, head_cols(g)], 1, layer
            )
        n.dv_v[here] = n.total_v[:, s.keys :].astype(BF16)
        send_out(subs(i), *made)

    each_of(s.rows // WIDE, each)


def feed(n, i, middle, layer):
    here = wide_rows(i)
    normed = (middle * rms_inverse(middle) * n.ffn_gain[layer : layer + 1]).astype(BF16)
    n.a2_v[here] = normed
    gate = dot_nn(normed, n.wg_v[...])
    up = dot_nn(normed, n.wu_v[...])
    inside = (gate * jax.nn.sigmoid(gate) * up).astype(BF16)
    n.hidden_v[here] = inside
    return gate, up, dot_nn(inside, n.wd_v[...])


def layer_ins(stream, saved, w, tables):
    return dict(
        x=(stream, ANY),
        qin=(saved.q, ANY),
        kvin=(saved.kv, ANY),
        ffn_gain=(w.ffn_gain, VMEM),
        lowest=(tables.lowest, VMEM),
        wo=(w.w_out, ANY),
        wg=(w.w_gate, ANY),
        wu=(w.w_up, ANY),
        wd=(w.w_down, ANY),
    )


def weight_scratch(s):
    return dict(
        wo_v=VMEM((s.queries, s.model), BF16),
        wg_v=VMEM((s.model, s.hidden), BF16),
        wu_v=VMEM((s.model, s.hidden), BF16),
        wd_v=VMEM((s.hidden, s.model), BF16),
    )


def layer_scratch(stream, s):
    return weight_scratch(s) | dict(
        x_v=VMEM((s.rows, s.model), stream.dtype),
        qin_v=VMEM((s.rows, s.queries), BF16),
        kvin_v=VMEM((ATTENTION_WINDOW + s.rows, 2 * s.keys), BF16),
        load_sems=DMA((16,)),
        store_sems=DMA((16, s.units)),
        first=line_scratch(s.units, s.model),
        second=line_scratch(s.units, s.model),
    )


def layer_loads(n, loads, layer):
    early = (
        loads(n.qin, n.qin_v),
        loads(n.kvin, n.kvin_v),
        loads(n.wo.at[layer], n.wo_v),
    )
    late = (
        loads(n.x, n.x_v),
        loads(n.wg.at[layer], n.wg_v),
        loads(n.wu.at[layer], n.wu_v),
        loads(n.wd.at[layer], n.wd_v),
    )
    return early, late


def kept_shapes(s):
    return dict(
        o=((s.rows, s.queries), BF16),
        a2=((s.rows, s.model), BF16),
        hidden=((s.rows, s.hidden), BF16),
    )


def forward_shapes(s):
    return kept_shapes(s) | dict(
        inv=((s.rows, HEAD_SIZE), F32),
        h=((s.rows, s.model), F32),
        gate=((s.rows, s.hidden), BF16),
        up=((s.rows, s.hidden), BF16),
        y=((s.rows, s.model), F32),
    )


def forward_layer(layer, stream, saved, w, tables, s):
    def body(n):
        loads = Loads(n.load_sems)
        early, late = layer_loads(n, loads, layer)
        above = (
            loads(n.wq.at[layer + 1], n.wq_v),
            loads(n.wk.at[layer + 1], n.wk_v),
            loads(n.wv.at[layer + 1], n.wv_v),
        )
        stores = Stores(n.store_sems)
        mixed = (stores(n.o_v, n.o), stores(n.inv_v, n.inv))
        fed = (
            stores(n.h_v, n.h),
            stores(n.a2_v, n.a2),
            stores(n.hidden_v, n.hidden),
            stores(n.gate_v, n.gate),
            stores(n.up_v, n.up),
        )
        closed = (
            stores(n.y_v, n.y),
            stores(n.a1_v, n.a1),
            stores(n.qraw_v, n.qraw),
            stores(n.kraw_v, n.kraw),
            stores(n.q_v, n.q),
        )
        first, second = LineSum(n.first), LineSum(n.second)
        halo = Halo(n.kv_v, n.halo_sems, s.rows, s.count)
        greet(line_partners() + halo_partners(s.rows, s.count))
        halo.blank()
        wait_all(*early)

        def mix(i):
            attend(n, i, s)
            first.push(i, dot_nn(n.o_v[wide_rows(i)], n.wo_v[...]))
            send_out(subs(i), *mixed)

        def feed_wide(i):
            pl.when(i == 0)(lambda: wait_all(*late))
            here = wide_rows(i)
            middle = n.x_v[here].astype(F32) + first.take_wide(i)
            n.h_v[here] = middle
            gate, up, part = feed(n, i, middle, layer)
            second.push(i, part)
            n.gate_v[here] = gate.astype(BF16)
            n.up_v[here] = up.astype(BF16)
            send_out(subs(i), *fed)

        def close(u):
            pl.when(u == 0)(lambda: wait_all(*above))
            here = unit_rows(u)
            result = n.h_v[here] + second.take(u)
            n.y_v[here] = result
            project(n, u * UNIT, UNIT, result, layer + 1)
            halo.send(u)
            send_out([u], *closed)

        at = 3 * HOP + 1
        pipeline(
            s.units,
            second.stages(at)
            + first.stages(0)
            + [(at + 3 * HOP, close, 1), (at, feed_wide, WIDE // UNIT), (0, mix, WIDE // UNIT)],
        )
        each_of(s.units, halo.finish)
        keys = loads(n.kv_v, n.kv)

        def finish(u):
            first.finish(u)
            second.finish(u)
            stores.finish(u)

        each_of(s.units, finish)
        keys.wait()

    return run_kernel(
        body,
        layer_ins(stream, saved, w, tables) | project_ins(w, tables),
        outputs(forward_shapes(s)) | outputs(project_shapes(s)),
        layer_scratch(stream, s) | buffers(forward_shapes(s)) | project_scratch(s),
        2 + layer,
    )


def turn_layer(layer, stream, saved, cotangent, w, tables, s):
    def body(n):
        loads = Loads(n.load_sems)
        early, late = layer_loads(n, loads, layer)
        late = late + (loads(n.grad, n.grad_v),)
        raws = (loads(n.qraw, n.qraw_v), loads(n.kraw, n.kraw_v))
        stores = Stores(n.store_sems)
        mixed = (stores(n.o_v, n.o),)
        fed = (stores(n.a2_v, n.a2), stores(n.hidden_v, n.hidden))
        fed_back = (stores(n.dyb_v, n.dyb), stores(n.dgate_v, n.dgate), stores(n.dup_v, n.dup))
        closed = (stores(n.y_v, n.y),)
        turned = (stores(n.g_v, n.dres), stores(n.dhb_v, n.dhb), stores(n.dq_v, n.dq))
        keyed = (stores(n.dk_v, n.dk), stores(n.dv_v, n.dv))
        first, second, lower = LineSum(n.first), LineSum(n.second), LineSum(n.lower)
        returns = Returns(n, s)
        greet(line_partners() + halo_partners(s.rows, s.count))
        back_start(n, returns)
        wait_all(*early)

        def mix(i):
            attend(n, i, s)
            first.push(i, dot_nn(n.o_v[wide_rows(i)], n.wo_v[...]))
            send_out(subs(i), *mixed)

        def feed_both(i):
            pl.when(i == 0)(lambda: wait_all(*late))
            here = wide_rows(i)
            middle = n.x_v[here] + first.take_wide(i)
            n.x_v[here] = middle
            n.g_v[here] = n.grad_v[here].astype(F32)
            gate, up, part = feed(n, i, middle, layer)
            feed_back(n, i, gate, up, lower, fed_back)
            second.push(i, part)
            send_out(subs(i), *fed)

        def close(u):
            here = unit_rows(u)
            n.y_v[here] = (n.x_v[here] + second.take(u)).astype(BF16)
            send_out([u], *closed)

        def attention(i):
            pl.when(i == 0)(lambda: wait_all(*raws))
            middle = n.x_v[wide_rows(i)]
            attention_back(
                n, i, middle, n.kvin_v, n.qin_v, layer, lower, returns, turned, s
            )

        at = 3 * HOP + 1
        pipeline(
            s.units,
            lower.stages(at)
            + second.stages(at, HOP + 1)
            + first.stages(0)
            + [
                (at + 3 * HOP + 3, close, 1),
                (at + 3 * HOP + 1, attention, WIDE // UNIT),
                (at, feed_both, WIDE // UNIT),
                (0, mix, WIDE // UNIT),
            ],
        )
        returns.send_rest()
        returns.receive()
        keys_back(n, layer, returns, keyed, s)
        returns.finish()

        def finish(u):
            first.finish(u)
            second.finish(u)
            lower.finish(u)
            stores.finish(u)

        each_of(s.units, finish)

    shapes = kept_shapes(s) | dict(y=((s.rows, s.model), BF16))
    return run_kernel(
        body,
        layer_ins(stream, saved, w, tables)
        | dict(
            grad=(cotangent, ANY),
            qraw=(saved.qraw, ANY),
            kraw=(saved.kraw, ANY),
            qk_gain=(w.qk_gain, VMEM),
            cosine=(tables.cosine, VMEM),
            sine=(tables.sine, VMEM),
        ),
        outputs(shapes) | attention_back_outs(s),
        layer_scratch(stream, s)
        | buffers(shapes)
        | buffers(attention_back_shapes(s))
        | attention_back_scratch(s)
        | dict(
            inv_v=VMEM((s.rows, HEAD_SIZE), F32),
            grad_v=VMEM((s.rows, s.model), BF16),
            g_v=VMEM((s.rows, s.model), F32),
            qraw_v=VMEM((s.rows, s.queries), F32),
            kraw_v=VMEM((s.rows, s.keys), F32),
            lower=line_scratch(s.units, s.model),
        ),
        2 + layer,
    )


def halving_partners(count):
    c, t = place()
    return [(c >= 0, (c ^ (1 << b), t)) for b in range(count.bit_length() - 1)]


class Scatter:
    def __init__(self, n, s, sizes, factors=None):
        self.n, self.s, self.sizes, self.factors = n, s, sizes, factors
        self.bits = s.count.bit_length() - 1
        self.c, self.t = place()
        self.loads = []

    def bit(self, b):
        return (self.c >> b) & 1

    def order(self, index):
        rest = list(range(1, self.bits))
        return [0] + (rest if index % 2 == 0 else rest[::-1])

    def spot(self, picks):
        low = 0 if self.factors else 1
        return tuple(picks.get(b, slice(None)) for b in range(self.bits - 1, low - 1, -1))

    def own(self, index):
        return (self.n.whole_v if self.factors else self.n.own)[index]

    def copy(self, index, step):
        order = self.order(index)
        picks = {b: self.bit(b) for b in order[:step]}
        picks[order[step]] = 1 - self.bit(order[step])
        if step == 0 and not self.factors:
            source = self.n.whole[index].at[
                (slice(None),) * (self.bits - 1) + (1 - self.bit(0),)
            ]
        else:
            source = self.own(index).at[self.spot(picks)]
        sems = self.n.scatter_sems
        return remote(
            source,
            self.n.got[index * self.bits + step],
            sems.at[0, index, step],
            sems.at[1, index, step],
            (self.c ^ (1 << order[step]), self.t),
        )

    def load(self, index):
        return pltpu.make_async_copy(
            self.n.whole[index].at[(slice(None),) * (self.bits - 1) + (self.bit(0),)],
            self.n.own[index],
            self.n.scatter_load_sems.at[index],
        )

    def start(self, index):
        if self.factors:
            left, right, needed = self.factors[index]
            wait_all(*needed)
            line = self.sizes[index][0]
            half = self.s.count // 2
            for part in range(2):
                product = dot_tn(left[:, part * half * line : (part + 1) * half * line], right[...])
                for k in range(half):
                    block = part * half + k
                    at = tuple((block >> b) & 1 for b in range(self.bits - 1, -1, -1))
                    self.own(index)[at + (slice(0, line),)] = product[
                        k * line : (k + 1) * line
                    ].astype(BF16)
        else:
            self.load(index).start()
        self.copy(index, 0).start()

    def add(self, index, step):
        order = self.order(index)
        if step == 0 and not self.factors:
            self.load(index).wait()
        self.copy(index, step).wait_recv()
        free = [b for b in range(self.bits - 1, 0, -1) if b not in order[: step + 1]]
        own, got = self.own(index), self.n.got[index * self.bits + step]
        line = self.sizes[index][0]

        def one(k, carry):
            picks = {b: (k >> (len(free) - 1 - i)) & 1 for i, b in enumerate(free)}
            here = self.spot({b: self.bit(b) for b in order[: step + 1]} | picks)
            total = own[here].astype(F32) + got[tuple(picks[b] for b in free)].astype(F32)
            if step == self.bits - 1:
                self.n.sums_v[index][...] = total[:line]
            else:
                own[here] = total.astype(BF16)
            return carry

        if free:
            lax.fori_loop(0, 1 << len(free), one, 0)
        else:
            one(0, 0)
        if step < self.bits - 1:
            self.copy(index, step + 1).start()
        else:
            self.store(index).start()

    def store(self, index):
        target = self.n.sums[index].at[0] if self.factors else self.n.sums[index]
        return pltpu.make_async_copy(
            self.n.sums_v[index], target, self.n.scatter_store_sems.at[index]
        )

    def tasks(self, every, bases):
        found = []
        for index in range(len(self.sizes)):
            found.append((bases[0] + index * every, lambda index=index: self.start(index)))
            for step in range(self.bits):
                at = bases[min(step + 1, len(bases) - 1)] + index * every
                at += 100 * max(0, step + 2 - len(bases))
                found.append((at, lambda index=index, step=step: self.add(index, step)))
        found.sort(key=lambda item: item[0])
        return found

    def finish(self):
        for index in range(len(self.sizes)):
            self.store(index).wait()
            for step in range(self.bits):
                self.copy(index, step).wait_send()


def scatter_scratch(s, sizes, computed):
    bits = s.count.bit_length() - 1
    tails = [(line + -line % 16, width) for line, width in sizes]
    found = dict(
        sums_v=[VMEM(size, F32) for size in sizes],
        got=[
            VMEM((2,) * (bits - 1 - step) + tail, BF16) for tail in tails for step in range(bits)
        ],
        scatter_sems=DMA((2, len(sizes), bits)),
        scatter_load_sems=DMA((len(sizes),)),
        scatter_store_sems=DMA((len(sizes),)),
    )
    if computed:
        return found | dict(whole_v=[VMEM((2,) * bits + tail, BF16) for tail in tails])
    return found | dict(own=[VMEM((2,) * (bits - 1) + tail, BF16) for tail in tails])


def block_view(array, s):
    bits = s.count.bit_length() - 1
    line = array.shape[0] // s.count
    view = array.reshape((2,) * bits + (line, array.shape[1]))
    if line % 16:
        view = jnp.pad(view, [(0, 0)] * bits + [(0, -line % 16), (0, 0)])
    return view


def factor_pairs(k):
    return [
        (k.a2, k.dup),
        (k.a2, k.dgate),
        (k.a1, k.dq),
        (k.hidden, k.dyb),
        (k.o, k.dhb),
        (k.a1, k.dk),
        (k.a1, k.dv),
    ]


def grad_sizes(s):
    return [
        (s.model // s.count, s.hidden),
        (s.model // s.count, s.hidden),
        (s.model // s.count, s.queries),
        (s.hidden // s.count, s.model),
        (s.queries // s.count, s.model),
        (s.model // s.count, s.keys),
        (s.model // s.count, s.keys),
    ]


def head_ins(k, w):
    return dict(
        hq=(k.dq, ANY),
        hk=(k.dk, ANY),
        hv=(k.dv, ANY),
        wq=(w.w_query, ANY),
        wk=(w.key_weight, ANY),
        wv=(w.value_weight, ANY),
        x=(k.x, ANY),
        attn_gain=(w.attn_gain, VMEM),
        grad=(k.dres, ANY),
    )


def head_scratch(k, s):
    return dict(
        hq_v=VMEM((s.rows, s.queries), BF16),
        hk_v=VMEM((s.rows, s.keys), BF16),
        hv_v=VMEM((s.rows, s.keys), BF16),
        wq_v=VMEM((s.model, s.queries), BF16),
        wk_v=VMEM((s.model, s.keys), BF16),
        wv_v=VMEM((s.model, s.keys), BF16),
        x_v=VMEM((s.rows, s.model), k.x.dtype),
        g_v=VMEM((s.rows, s.model), F32),
        upper=line_scratch(s.units, s.model),
        load_sems=DMA((32,)),
        store_sems=DMA((10, s.units)),
    )


def head_loads(n, loads, layer):
    early = (
        loads(n.hq, n.hq_v),
        loads(n.wq.at[layer], n.wq_v),
        loads(n.hk, n.hk_v),
        loads(n.wk.at[layer], n.wk_v),
        loads(n.hv, n.hv_v),
        loads(n.wv.at[layer], n.wv_v),
    )
    return early, (loads(n.x, n.x_v), loads(n.grad, n.g_v))


def head_inputs(n, i, upper):
    here = wide_rows(i)
    upper.push(
        i,
        dot_nt(n.hq_v[here], n.wq_v[...])
        + dot_nt(n.hk_v[here], n.wk_v[...])
        + dot_nt(n.hv_v[here], n.wv_v[...]),
    )


def head_norm(n, here, grad_in, layer):
    stream = n.x_v[here].astype(F32)
    inverse = rms_inverse(stream)
    unit = stream * inverse
    n.attn_sum[...] += column_sum(grad_in * unit)
    n.g_v[here] += norm_back(grad_in, unit, inverse, n.attn_gain[layer : layer + 1])


def backward_layer(layer, kept, w, tables, s):
    above, here_kept = kept[layer + 1], kept[layer]
    sizes = grad_sizes(s)

    def body(n):
        loads = Loads(n.load_sems)
        early, middle_loads = head_loads(n, loads, layer + 1)
        scatter = Scatter(n, s, sizes)
        feeds = (
            loads(n.wd.at[layer], n.wd_v),
            loads(n.gate, n.gate_v),
            loads(n.up, n.up_v),
            loads(n.wg.at[layer], n.wg_v),
            loads(n.wu.at[layer], n.wu_v),
        )
        lates = (
            loads(n.wo.at[layer], n.wo_v),
            loads(n.q, n.q_v),
            loads(n.kv, n.kv_v),
            loads(n.o, n.o_v),
            loads(n.inv, n.inv_v),
            loads(n.qraw, n.qraw_v),
            loads(n.kraw, n.kraw_v),
        )
        stores = Stores(n.store_sems)
        fed_back = (stores(n.dyb_v, n.dyb), stores(n.dgate_v, n.dgate), stores(n.dup_v, n.dup))
        turned = (stores(n.g_v, n.dres), stores(n.dhb_v, n.dhb), stores(n.dq_v, n.dq))
        keyed = (stores(n.dk_v, n.dk), stores(n.dv_v, n.dv))
        upper, lower = LineSum(n.upper), LineSum(n.lower)
        returns = Returns(n, s)
        greet(line_partners() + halo_partners(s.rows, s.count) + halving_partners(s.count))
        n.attn_sum[...] = jnp.zeros_like(n.attn_sum)
        back_start(n, returns)
        wait_all(*early)

        def middle_copy(i):
            rows = wide_rows(i)
            return pltpu.make_async_copy(n.h.at[rows], n.x_v.at[rows], n.middle_sems.at[i])

        def inputs(i):
            head_inputs(n, i, upper)

        def pass_norm(i):
            pl.when(i == 0)(lambda: wait_all(*middle_loads, *feeds))
            here = wide_rows(i)
            head_norm(n, here, upper.take_wide(i), layer + 1)
            middle_copy(i).start()
            gate, up = n.gate_v[here].astype(F32), n.up_v[here].astype(F32)
            feed_back(n, i, gate, up, lower, fed_back)

        def attention(i):
            pl.when(i == 0)(lambda: wait_all(*lates))
            middle_copy(i).wait()
            attention_back(
                n, i, n.x_v[wide_rows(i)], n.kv_v, n.q_v, layer, lower, returns, turned, s
            )

        at = 3 * HOP + 1
        pipeline(
            s.units,
            lower.stages(at)
            + upper.stages(0)
            + [
                (at + 3 * HOP + 1, attention, WIDE // UNIT),
                (at, pass_norm, WIDE // UNIT),
                (0, inputs, WIDE // UNIT),
            ],
            scatter.tasks(1, SCATTER_MIDDLE),
        )
        returns.send_rest()
        returns.receive()
        keys_back(n, layer, returns, keyed, s)
        returns.finish()
        scatter.finish()

        def finish(u):
            upper.finish(u)
            lower.finish(u)
            stores.finish(u)

        each_of(s.units, finish)

    whole = [
        block_view(dot_tn(left, right).astype(BF16), s) for left, right in factor_pairs(above)
    ]
    held = dict(
        gate=here_kept.gate,
        up=here_kept.up,
        q=here_kept.q,
        kv=here_kept.kv,
        o=here_kept.o,
        inv=here_kept.inv,
        qraw=here_kept.qraw,
        kraw=here_kept.kraw,
    )
    return run_kernel(
        body,
        head_ins(above, w)
        | {x: (array, ANY) for x, array in held.items()}
        | dict(
            h=(here_kept.h, ANY),
            wd=(w.w_down, ANY),
            wg=(w.w_gate, ANY),
            wu=(w.w_up, ANY),
            wo=(w.w_out, ANY),
            ffn_gain=(w.ffn_gain, VMEM),
            qk_gain=(w.qk_gain, VMEM),
            cosine=(tables.cosine, VMEM),
            sine=(tables.sine, VMEM),
            lowest=(tables.lowest, VMEM),
            whole=[(array, ANY) for array in whole],
        ),
        attention_back_outs(s)
        | dict(
            attn_sum=(shaped(1, s.model, kind=F32), VMEM),
            sums=[(shaped(*size, kind=F32), ANY) for size in sizes],
        ),
        head_scratch(above, s)
        | weight_scratch(s)
        | {x + "_v": VMEM(array.shape, array.dtype) for x, array in held.items()}
        | buffers(attention_back_shapes(s))
        | attention_back_scratch(s)
        | scatter_scratch(s, sizes, False)
        | dict(
            lower=line_scratch(s.units, s.model),
            middle_sems=DMA((s.rows // WIDE,)),
        ),
        20 + layer,
    )


def backward_end(kept, w, s):
    bottom = kept[0]
    sizes = grad_sizes(s)
    layers = len(kept)
    width = s.model // s.count
    bits = s.count.bit_length() - 1
    tp_bits = s.line.bit_length() - 1
    rounds = [(1 << b, 0) for b in range(bits)] + [(0, 1 << b) for b in range(tp_bits)]

    def body(n):
        c, t = place()
        loads = Loads(n.load_sems)
        early, lates = head_loads(n, loads, 0)
        a2, dup, dgate = loads(n.a2, n.a2_v), loads(n.dup, n.dup_v), loads(n.dgate, n.dgate_v)
        a1, hidden, dyb = loads(n.a1, n.a1_v), loads(n.hidden, n.hidden_v), loads(n.dyb, n.dyb_v)
        o, dhb = loads(n.o, n.o_v), loads(n.dhb, n.dhb_v)
        factors = [
            (n.a2_v, n.dup_v, (a2, dup)),
            (n.a2_v, n.dgate_v, (dgate,)),
            (n.a1_v, n.hq_v, (a1,)),
            (n.hidden_v, n.dyb_v, (hidden, dyb)),
            (n.o_v, n.dhb_v, (o, dhb)),
            (n.a1_v, n.hk_v, ()),
            (n.a1_v, n.hv_v, ()),
        ]
        scatter = Scatter(n, s, sizes, factors)
        stores = Stores(n.store_sems)
        out = stores(n.g_v, n.dres)
        upper = LineSum(n.upper)
        others = [(c >= 0, ((c + k) % s.count, t)) for k in range(1, s.count)]
        lines = [(c >= 0, (c, t ^ (1 << b))) for b in range(tp_bits)]
        greet(line_partners() + halving_partners(s.count) + others + lines)
        n.attn_sum[...] = jnp.zeros_like(n.attn_sum)
        n.acc[...] = jnp.zeros_like(n.acc)
        n.gains[...] = jnp.zeros_like(n.gains)
        for layer in range(layers):
            n.acc[0, 2 * layer : 2 * layer + 2] = n.qk_in[layer][...]
        wait_all(*early)
        above = [
            loads(n.done[(layer - 1) * len(sizes) + index], n.sums[index].at[layer])
            for layer in range(1, layers)
            for index in range(len(sizes))
        ]

        def head_copy(k):
            return remote(
                n.acc.at[k],
                n.other.at[k],
                n.small_sems.at[0, k],
                n.small_sems.at[1, k],
                (c ^ rounds[k][0], t ^ rounds[k][1]),
            )

        def head_step(k):
            if k > 0:
                head_copy(k - 1).wait_recv()
                n.acc[k] = n.acc[k - 1] + n.other[k - 1]
            if k < len(rounds):
                head_copy(k).start()

        def pass_norm(u):
            pl.when(u == 0)(lambda: wait_all(*lates))
            head_norm(n, unit_rows(u), upper.take(u), 0)
            send_out([u], out)

        tasks = scatter.tasks(1, SCATTER_END)
        tasks += [(2 * k + 1, lambda k=k: head_step(k)) for k in range(len(rounds) + 1)]
        tasks.sort(key=lambda item: item[0])
        pipeline(
            s.units,
            upper.stages(0)
            + [
                (3 * HOP, pass_norm, 1),
                (0, lambda i: head_inputs(n, i, upper), WIDE // UNIT),
            ],
            tasks,
        )
        gains = [n.attn_sum] + n.attn_in + n.ffn_in
        for d in range(s.count):
            for row, gain in enumerate(gains):
                n.gains[d, row : row + 1] = gain[:, d * width : (d + 1) * width]

        def gain_copy(k):
            to = (c + k) % s.count
            return remote(
                n.gains.at[to],
                n.gains_got.at[k],
                n.gain_sems.at[0, k],
                n.gain_sems.at[1, k],
                (to, t),
            )

        for k in range(1, s.count):
            gain_copy(k).start()
        for layer in range(layers):
            n.qk_total[layer] = n.acc[len(rounds), 2 * layer : 2 * layer + 2]
        total = n.gains[c]
        for k in range(1, s.count):
            gain_copy(k).wait_recv()
            total = total + n.gains_got[k]
        n.attn_total[...] = total[:layers]
        n.ffn_total[...] = total[layers : 2 * layers]
        for k in range(1, s.count):
            gain_copy(k).wait_send()
        for k in range(len(rounds)):
            head_copy(k).wait_send()
        scatter.finish()
        wait_all(*above)

        def finish(u):
            upper.finish(u)
            stores.finish(u)

        each_of(s.units, finish)

    held = dict(
        a1=bottom.a1,
        a2=bottom.a2,
        o=bottom.o,
        hidden=bottom.hidden,
        dyb=bottom.dyb,
        dgate=bottom.dgate,
        dup=bottom.dup,
        dhb=bottom.dhb,
    )
    small = (len(rounds) + 1, 2 * layers + -2 * layers % 8, HEAD_SIZE)
    slabs = (s.count, 2 * layers + -2 * layers % 8, width)
    return run_kernel(
        body,
        head_ins(bottom, w)
        | {x: (array, ANY) for x, array in held.items()}
        | dict(
            qk_in=[(k.qk_sum, VMEM) for k in kept],
            attn_in=[(k.attn_sum, VMEM) for k in kept[1:]],
            ffn_in=[(k.ffn_sum, VMEM) for k in kept],
            done=[(array, ANY) for k in kept[1:] for array in k.sums],
        ),
        dict(
            dres=(shaped(s.rows, s.model, kind=F32), ANY),
            attn_total=(shaped(layers, width, kind=F32), VMEM),
            ffn_total=(shaped(layers, width, kind=F32), VMEM),
            qk_total=(shaped(layers, 2, HEAD_SIZE, kind=F32), VMEM),
            sums=[(shaped(layers, *size, kind=F32), ANY) for size in sizes],
        ),
        head_scratch(bottom, s)
        | {x + "_v": VMEM(array.shape, array.dtype) for x, array in held.items()}
        | scatter_scratch(s, sizes, True)
        | dict(
            attn_sum=VMEM((1, s.model), F32),
            acc=VMEM(small, F32),
            other=VMEM(small, F32),
            gains=VMEM(slabs, F32),
            gains_got=VMEM(slabs, F32),
            small_sems=DMA((2, len(rounds))),
            gain_sems=DMA((2, s.count)),
        ),
        19,
    )


SCATTER_MIDDLE = (0, 3, 9, 16)
SCATTER_END = (0, 2, 7, 11)


def body(hidden_in, doc_lengths, cotangent, attn_gain, ffn_gain, qk_gain, w_query, *others):
    key_weight, value_weight, w_out, w_gate, w_up, w_down = others
    w = types.SimpleNamespace(
        attn_gain=attn_gain,
        ffn_gain=ffn_gain,
        qk_gain=qk_gain,
        w_query=w_query,
        key_weight=key_weight,
        value_weight=value_weight,
        w_out=w_out,
        w_gate=w_gate,
        w_up=w_up,
        w_down=w_down,
    )
    rows, model = hidden_in.shape
    layers, unused, queries = w_query.shape
    keys = key_weight.shape[2]
    s = types.SimpleNamespace(
        rows=rows,
        model=model,
        queries=queries,
        keys=keys,
        hidden=w_gate.shape[2],
        units=rows // UNIT,
        groups=keys // HEAD_SIZE,
        repeat=queries // keys,
        count=lax.axis_size(CTX),
        line=lax.axis_size(TP),
    )
    tables = make_tables(doc_lengths, rows)

    kept = []
    stream = hidden_in
    saved = first_projection(stream, w, tables, s)
    for layer in range(layers):
        if layer < layers - 1:
            result = forward_layer(layer, stream, saved, w, tables, s)
        else:
            result = turn_layer(layer, stream, saved, cotangent, w, tables, s)
        own = dict(a1=saved.a1, qraw=saved.qraw, kraw=saved.kraw, q=saved.q, kv=saved.kv)
        kept.append(types.SimpleNamespace(**(vars(result) | own | dict(x=stream))))
        stream = result.y
        saved = result

    for layer in range(layers - 2, -1, -1):
        result = backward_layer(layer, kept, w, tables, s)
        kept[layer + 1].attn_sum = result.attn_sum
        kept[layer + 1].sums = result.sums
        vars(kept[layer]).update(
            dyb=result.dyb,
            dgate=result.dgate,
            dup=result.dup,
            dhb=result.dhb,
            dq=result.dq,
            dk=result.dk,
            dv=result.dv,
            dres=result.dres,
            ffn_sum=result.ffn_sum,
            qk_sum=result.qk_sum,
        )
    end = backward_end(kept, w, s)
    up, gate, query, down, out, key, value = end.sums
    return (
        stream,
        end.dres,
        end.attn_total,
        end.ffn_total,
        end.qk_total,
        query,
        key,
        value,
        out,
        gate,
        up,
        down,
    )


def solution(mesh):
    by_rows = P(CTX, None)
    by_columns = P(None, None, TP)
    by_hidden = P(None, TP, None)
    grad_columns = P(None, CTX, TP)
    grad_rows = P(None, (TP, CTX), None)
    return jax.shard_map(
        body,
        mesh=mesh,
        in_specs=(by_rows, P(), by_rows, P(), P(), P())
        + (by_columns,) * 3
        + (by_hidden,)
        + (by_columns,) * 2
        + (by_hidden,),
        out_specs=(by_rows, by_rows, P(None, CTX), P(None, CTX), P())
        + (grad_columns,) * 3
        + (grad_rows,)
        + (grad_columns,) * 2
        + (grad_rows,),
        check_vma=False,
    )
```

time: 1250 us -> 483 us (0.39)
  waiting for transfers between devices: 794 us -> 0 us
  Pallas kernels: 0 us -> 444 us
  matrix products: 179 us -> 15.7 us
  other arithmetic: 111 us -> 5.11 us
  local copies, waits for them, and re-layouts: 66.3 us -> 11.5 us
  starting transfers between devices: 39.2 us -> 0 us
  blocking collectives: 39.1 us -> 0 us
  between operations: 16.4 us -> 1.06 us
    psum x7 -> x0, waiting for transfers between devices: 523 us -> none  [the longest x4 322 us: branch_total(): lax.psum(matrix_product(left, right).astype(jnp.bfloat16), 'tp')]
    pallas_call x0 -> x5, Pallas kernels: none -> 444 us  [run_kernel(): pl.pallas_call(lambda *refs: body(named(refs, groups)), out_shape=[shape...]
    reduce_scatter x7 -> x0, waiting for transfers between devices: 237 us -> none  [the longest x1 48.5 us: body(): lax.psum_scatter(stacked[6].astype(jnp.bfloat16), 'ctx', scatter_dimensio...]
    dot_general x54 -> x7, matrix products: 179 us -> 15.7 us  [dot_tn(): lax.dot_general(left, right, (((0,), (0,)), ((), ())), preferred_element_...]
    convert_element_type x22 -> x1, other arithmetic: 49.4 us -> 0.01 us  [make_tables(): angle = (spot - begin).astype(F32)[:, None] * freq[None, :]]
    psum x1 -> x0, blocking collectives: 39.1 us -> none  [body(): qk_total = lax.psum(jnp.stack(gain_parts), ('ctx', 'tp'))]
    ppermute x16 -> x0, starting transfers between devices: 37.3 us -> none  [passed_along(): lax.ppermute(value, axis, [(source, source + steps) for source in range(l...]
    unnamed x310 -> x56, local copies, waits for them, and re-layouts: 43.7 us -> 11.5 us
  transfers between devices with their start and end apart: 32 -> 0, of which waited for: 16 -> 0; matrix products, arithmetic and copies ran while one was open for 14% -> 0% of each run, Pallas kernels for 0% -> 0%
where the time goes in v1:
time: 483 us; the launch traced here: 477 us
  Pallas kernels  444 us (92%)
  matrix products  15.7 us (3%)
  local copies, waits for them, and re-layouts  11.5 us (2%)
  other arithmetic  5.11 us (1%)
    pallas_call x5, Pallas kernels, run_kernel(): pl.pallas_call(lambda *refs: body(named(refs, groups)), out_shape=[shape...  444 us
    dot_general x7, matrix products, dot_tn(): lax.dot_general(left, right, (((0,), (0,)), ((), ())), preferred_element_...  15.7 us
    unnamed x56, local copies, waits for them, and re-layouts  11.5 us

profile of v1, /device:TPU:0, one launch (start us, length us, event | category | flops | bytes accessed | tf_op | source)
XLA Modules:
  0.0 477.0 jit_solution(12943080298976945114)
XLA Ops:
  0.6 0.8 reduce-window.8
  1.5 0.7 select_reduce_fusion
  2.3 0.9 fusion.refs_4_.refs_26_
  3.2 1.4 fusion.1
  4.6 1.2 pad_maximum_fusion
  5.8 17.5 %shard_map.220 = (bf16[768,1024]{1,0:T(8,128)(2,1)}, f32[768,512]{1,0:T(8,128)}, f32[768,256]{1,0:T(8,128)}, bf16[768,512]{1,0:T(8,128)(2,1)}, bf16[1792,512]{1,0:T(8,128)(2,1)}) custom-call(bf16[768,1024]{1,0:T(8,128)(2,1)} %refs_6_.7, f32[2,1024]{1,0:T(2,128)} %refs_7_.9, f32[2,2,128]{2,1,0:T(2,128)} %refs_23_.1, ...), custom_call_target="tpu_custom_call" | custom-call | tf_op jit(solution)/shard_map/pallas_call | solution.py:126
  23.2 101.9 %shard_map.221 = (bf16[768,512]{1,0:T(8,128)(2,1)}, bf16[768,1024]{1,0:T(8,128)(2,1)}, bf16[768,768]{1,0:T(8,128)(2,1)}, f32[768,128]{1,0:T(8,128)}, f32[768,102...) custom-call(bf16[768,1024]{1,0:T(8,128)(2,1)} %refs_6_.7, ...), custom_call_target="tpu_custom_call" | custom-call | tf_op jit(solution)/shard_map/pallas_call | solution.py:126
  125.1 0.0 copy-start.14
  125.1 142.9 %shard_map.222 = (bf16[768,512]{1,0:T(8,128)(2,1)}, bf16[768,1024]{1,0:T(8,128)(2,1)}, bf16[768,768]{1,0:T(8,128)(2,1)}, bf16[768,1024]{1,0:T(8,128)(2,1)}, bf16...) custom-call(f32[768,1024]{1,0:T(8,128)} %get-tuple-element.75.refs_0, ...), custom_call_target="tpu_custom_call" | custom-call | tf_op jit(solution)/shard_map/pallas_call | solution.py:126
  268.0 0.0 copy-done.14
  268.0 0.0 copy-start.8
  268.0 2.5 convolution_convert_fusion.6
  270.5 0.0 copy-done.8
  270.5 0.0 copy-start.5
  270.5 1.4 convolution_convert_fusion.5
  271.9 0.0 copy-done.5
  271.9 0.0 copy-start.17
  271.9 0.0 copy-start.21
  271.9 2.0 convolution_convert_fusion.4
  273.9 0.0 copy-done.17
  273.9 0.0 copy-done.21
  273.9 0.0 copy-start.16
  273.9 0.0 copy-start.20
  274.0 2.0 convolution_convert_fusion.3
  275.9 0.0 copy-done.16
  275.9 0.0 copy-done.20
  275.9 0.0 copy-start.19
  275.9 2.6 convolution_convert_fusion.2
  278.5 0.0 copy-done.19
  278.5 0.0 copy-start.15
  278.5 0.0 copy-start.18
  278.5 2.6 convolution_convert_fusion.1
  281.1 0.0 copy-done.15
  281.1 0.0 copy-done.18
  281.1 2.7 convolution_convert_fusion
  283.8 109.3 %shard_map.223 = (bf16[768,1024]{1,0:T(8,128)(2,1)}, bf16[768,768]{1,0:T(8,128)(2,1)}, bf16[768,768]{1,0:T(8,128)(2,1)}, bf16[768,1024]{1,0:T(8,128)(2,1)}, bf16...) custom-call(bf16[768,512]{1,0:T(8,128)(2,1)} %get-tuple-element.81.r, ...), custom_call_target="tpu_custom_call" | custom-call | tf_op jit(solution)/shard_map/pallas_call | solution.py:126
  393.1 0.0 copy-start.1
  393.1 72.1 %shard_map.224 = (f32[768,1024]{1,0:T(8,128)}, f32[2,128]{1,0:T(2,128)}, f32[2,128]{1,0:T(2,128)}, f32[2,2,128]{2,1,0:T(2,128)}, f32[2,128,768]{2,1,0:T(8,128)},...) custom-call(bf16[768,512]{1,0:T(8,128)(2,1)} %get-tuple-element.100., ...), custom_call_target="tpu_custom_call" | custom-call | tf_op jit(solution)/shard_map/pallas_call | solution.py:126
  465.2 0.0 copy-done.1
  465.2 0.0 copy-start
  465.2 1.1 copy.42
  466.4 1.3 copy-done
  467.7 0.0 copy-start.10
  467.7 1.7 copy.43
  469.4 0.0 copy-done.13
  469.4 0.6 copy.44
  469.9 0.0 copy-done.12
  469.9 0.6 copy.45
  470.5 0.0 copy-done.11
  470.5 0.6 copy.46
  471.1 0.0 copy-done.7
  471.1 0.8 copy.47
  471.9 0.0 copy-done.10
  471.9 0.7 copy.48
  472.6 0.0 copy-done.9
  472.6 0.7 copy.49
  473.3 0.0 copy-done.6
  473.3 0.8 copy.50
  474.1 0.0 copy-done.4
  474.1 0.9 copy.51
  475.0 0.0 copy-done.3
  475.0 0.9 copy.52
  475.9 0.0 copy-done.2
  475.9 0.9 copy.53
  (12 shorter events, 0.0 us)
Async XLA Ops:
  125.1 142.9 %copy-start.14 = (bf16[768,1024]{1,0:T(8,128)(2,1)S(1)}, bf16[768,1024]{1,0:T(8,128)(2,1)}, u32[]{:S(2)}) copy-start(bf16[768,1024]{1,0:T(8,128)(2,1)} %get-tuple-element.95) | copy-start | bytes 4718596
  268.0 2.5 copy-start.8
  270.5 1.4 copy-start.5
  271.9 2.0 copy-start.17
  271.9 2.0 copy-start.21
  273.9 2.0 copy-start.16
  273.9 2.0 copy-start.20
  275.9 2.6 copy-start.19
  278.5 2.6 copy-start.15
  278.5 2.6 copy-start.18
  393.1 72.1 %copy-start.1 = (bf16[768,1024]{1,0:T(8,128)(2,1)S(1)}, bf16[768,1024]{1,0:T(8,128)(2,1)}, u32[]{:S(2)}) copy-start(bf16[768,1024]{1,0:T(8,128)(2,1)} %get-tuple-element.151) | copy-start | bytes 4718596
  465.2 2.5 copy-start
  467.7 1.7 copy-start.13
  467.7 2.3 copy-start.12
  467.7 2.8 copy-start.11
  467.7 3.4 copy-start.7
  467.7 4.2 copy-start.10
  469.4 3.2 copy-start.9
  469.4 3.9 copy-start.6
  471.1 3.0 copy-start.4
  472.6 2.4 copy-start.3
  474.1 1.8 copy-start.2

commit v2 on v1

--- a/solution.py
+++ b/solution.py
@@ -16,6 +16,7 @@
 WIDE = 128
 KEY_BLOCK = 384
 HOP = 2
+ARRIVED = 3 * HOP + WIDE // UNIT - 1
 CTX = "ctx"
 TP = "tp"
 MESH = pl.DeviceIdType.MESH
@@ -65,16 +66,18 @@
 def make_tables(lengths, rows):
     start = lax.axis_index(CTX) * rows
     spot = start + jnp.arange(rows, dtype=jnp.int32)
-    passed = jnp.cumsum(lengths)[None, :] <= spot[:, None]
+    order = jnp.arange(lengths.shape[0])
+    ends = jnp.sum(jnp.where(order[None, :] <= order[:, None], lengths[None, :], 0), axis=1)
+    passed = ends[None, :] <= spot[:, None]
     begin = jnp.sum(jnp.where(passed, lengths[None, :], 0), axis=1)
+    lane = jnp.arange(HEAD_SIZE)
     half = HEAD_SIZE // 2
-    freq = THETA ** (-(jnp.arange(half, dtype=F32) * 2.0) / HEAD_SIZE)
+    freq = THETA ** (-((lane % half).astype(F32) * 2.0) / HEAD_SIZE)
     angle = (spot - begin).astype(F32)[:, None] * freq[None, :]
-    cosine, sine = jnp.cos(angle), jnp.sin(angle)
     lowest = jnp.maximum(begin, spot - (ATTENTION_WINDOW - 1)) - (start - ATTENTION_WINDOW)
     return types.SimpleNamespace(
-        cosine=jnp.concatenate([cosine, cosine], axis=1),
-        sine=jnp.concatenate([-sine, sine], axis=1),
+        cosine=jnp.cos(angle),
+        sine=jnp.sin(angle) * jnp.where(lane < half, -1.0, 1.0)[None, :],
         lowest=lowest[:, None],
     )
 
@@ -130,7 +133,9 @@
         out_specs=[pl.BlockSpec(memory_space=space) for unused, space in flat[1]],
         scratch_shapes=flat[2],
         compiler_params=pltpu.CompilerParams(
-            collective_id=collective_id, has_side_effects=True, vmem_limit_bytes=62 * 2**20
+            collective_id=collective_id,
+            has_side_effects=collective_id is not None,
+            vmem_limit_bytes=62 * 2**20,
         ),
     )(*[array for array, unused in flat[0]])
     return named(results, [outs])
@@ -208,14 +213,19 @@
     def outwards(self, u):
         return self.copy(self.total, self.total, u, 3, 4, jnp.where(self.t < 2, 0, 3))
 
-    def push(self, w, value):
+    def hold(self, w, value):
         for i, u in enumerate(subs(w)):
             self.part[u] = value[i * UNIT : (i + 1) * UNIT].astype(BF16)
 
+    def send(self, u):
         @pl.when(self.outer)
         def _():
-            for u in subs(w):
-                self.inwards(u).start()
+            self.inwards(u).start()
+
+    def push(self, w, value):
+        self.hold(w, value)
+        for u in subs(w):
+            self.send(u)
 
     def meet(self, u):
         @pl.when(self.is_inner)
@@ -377,24 +387,31 @@
         self.each(u, lambda copy: copy.wait_send(), False)
 
 
-def project(n, first, number, stream, layer):
+def project_heads(n, raw, out, out_rows, rows, which, layer):
+    cosine, sine = n.cosine[rows], n.sine[rows]
+    gain = n.qk_gain[layer, which : which + 1]
+    for head in range(raw.shape[1] // HEAD_SIZE):
+        part = raw[:, head_cols(head)]
+        part = part * rms_inverse(part) * gain
+        out[out_rows, head_cols(head)] = rotate(part, cosine, sine).astype(BF16)
+
+
+def project_keys(n, first, number, stream, layer):
     rows = pl.ds(pl.multiple_of(first, number), number)
     own = pl.ds(pl.multiple_of(ATTENTION_WINDOW + first, number), number)
     normed = (stream * rms_inverse(stream) * n.attn_gain[layer : layer + 1]).astype(BF16)
     n.a1_v[rows] = normed
     key = dot_nn(normed, n.wk_v[...])
-    query = dot_nn(normed, n.wq_v[...])
+    n.kraw_v[rows] = key
+    n.kv_v[own, key.shape[1] :] = dot_nn(normed, n.wv_v[...]).astype(BF16)
+    project_heads(n, key, n.kv_v, own, rows, 1, layer)
+
+
+def project_queries(n, first, number, layer):
+    rows = pl.ds(pl.multiple_of(first, number), number)
+    query = dot_nn(n.a1_v[rows], n.wq_v[...])
     n.qraw_v[rows] = query
-    n.kraw_v[rows] = key
-    cosine, sine = n.cosine[rows], n.sine[rows]
-    for raw, out, out_rows, which in ((key, n.kv_v, own, 1), (query, n.q_v, rows, 0)):
-        gain = n.qk_gain[layer, which : which + 1]
-        for head in range(raw.shape[1] // HEAD_SIZE):
-            cols = slice(head * HEAD_SIZE, (head + 1) * HEAD_SIZE)
-            part = raw[:, cols]
-            part = part * rms_inverse(part) * gain
-            out[out_rows, cols] = rotate(part, cosine, sine).astype(BF16)
-    n.kv_v[own, key.shape[1] :] = dot_nn(normed, n.wv_v[...]).astype(BF16)
+    project_heads(n, query, n.q_v, rows, rows, 0, layer)
 
 
 def project_shapes(s):
@@ -456,13 +473,17 @@
         halo.blank()
         wait_all(*weights)
 
-        def each(i):
-            project(n, i * WIDE, WIDE, n.x[wide_rows(i)].astype(F32), 0)
+        def each_keys(i):
+            project_keys(n, i * WIDE, WIDE, n.x[wide_rows(i)].astype(F32), 0)
             for u in subs(i):
                 halo.send(u)
+
+        def each_queries(i):
+            project_queries(n, i * WIDE, WIDE, 0)
             send_out(subs(i), *made)
 
-        each_of(s.rows // WIDE, each)
+        each_of(s.rows // WIDE, each_keys)
+        each_of(s.rows // WIDE, each_queries)
         each_of(s.units, halo.finish)
         keys = loads(n.kv_v, n.kv)
         each_of(s.units, stores.finish)
@@ -665,8 +686,8 @@
     )
 
 
-def attention_back_outs(s):
-    return outputs(attention_back_shapes(s)) | dict(
+def attention_back_sums(s):
+    return dict(
         dres=(shaped(s.rows, s.model, kind=F32), ANY),
         ffn_sum=(shaped(1, s.model, kind=F32), VMEM),
         qk_sum=(shaped(2, HEAD_SIZE, kind=F32), VMEM),
@@ -868,11 +889,12 @@
             here = unit_rows(u)
             result = n.h_v[here] + second.take(u)
             n.y_v[here] = result
-            project(n, u * UNIT, UNIT, result, layer + 1)
+            project_keys(n, u * UNIT, UNIT, result, layer + 1)
             halo.send(u)
+            project_queries(n, u * UNIT, UNIT, layer + 1)
             send_out([u], *closed)
 
-        at = 3 * HOP + 1
+        at = ARRIVED
         pipeline(
             s.units,
             second.stages(at)
@@ -905,12 +927,10 @@
         early, late = layer_loads(n, loads, layer)
         late = late + (loads(n.grad, n.grad_v),)
         raws = (loads(n.qraw, n.qraw_v), loads(n.kraw, n.kraw_v))
+        a1 = loads(n.a1, n.a1_v)
         stores = Stores(n.store_sems)
-        mixed = (stores(n.o_v, n.o),)
-        fed = (stores(n.a2_v, n.a2), stores(n.hidden_v, n.hidden))
-        fed_back = (stores(n.dyb_v, n.dyb), stores(n.dgate_v, n.dgate), stores(n.dup_v, n.dup))
         closed = (stores(n.y_v, n.y),)
-        turned = (stores(n.g_v, n.dres), stores(n.dhb_v, n.dhb), stores(n.dq_v, n.dq))
+        turned = (stores(n.g_v, n.dres), stores(n.dq_v, n.dq))
         keyed = (stores(n.dk_v, n.dk), stores(n.dv_v, n.dv))
         first, second, lower = LineSum(n.first), LineSum(n.second), LineSum(n.lower)
         returns = Returns(n, s)
@@ -921,7 +941,6 @@
         def mix(i):
             attend(n, i, s)
             first.push(i, dot_nn(n.o_v[wide_rows(i)], n.wo_v[...]))
-            send_out(subs(i), *mixed)
 
         def feed_both(i):
             pl.when(i == 0)(lambda: wait_all(*late))
@@ -930,9 +949,8 @@
             n.x_v[here] = middle
             n.g_v[here] = n.grad_v[here].astype(F32)
             gate, up, part = feed(n, i, middle, layer)
-            feed_back(n, i, gate, up, lower, fed_back)
-            second.push(i, part)
-            send_out(subs(i), *fed)
+            feed_back(n, i, gate, up, lower, ())
+            second.hold(i, part)
 
         def close(u):
             here = unit_rows(u)
@@ -946,23 +964,51 @@
                 n, i, middle, n.kvin_v, n.qin_v, layer, lower, returns, turned, s
             )
 
-        at = 3 * HOP + 1
+        at = ARRIVED
+        def gradient(index):
+            left, right = factors[index]
+            block_products(n.grads_v[index], left, right, sizes[index][0], s)
+            gradient_store(index).start()
+
+        def gradient_store(index):
+            return pltpu.make_async_copy(n.grads_v[index], n.grads[index], n.grad_sems.at[index])
+
+        def end_keys():
+            returns.receive()
+            keys_back(n, layer, returns, keyed, s)
+            a1.wait()
+
+        factors = [
+            (n.a2_v, n.dup_v),
+            (n.a2_v, n.dgate_v),
+            (n.a1_v, n.dq_v),
+            (n.hidden_v, n.dyb_v),
+            (n.o_v, n.dhb_v),
+            (n.a1_v, n.dk_v),
+            (n.a1_v, n.dv_v),
+        ]
+        after = at + ARRIVED + s.units
+        tasks = [(after, returns.send_rest), (after + 4, end_keys)]
+        for index, step in enumerate((1, 2, 5, 3, 4, 6, 6)):
+            tasks.append((after + step, lambda index=index: gradient(index)))
+        tasks.sort(key=lambda item: item[0])
         pipeline(
             s.units,
             lower.stages(at)
-            + second.stages(at, HOP + 1)
+            + second.stages(OUTPUT_AT, HOP + 1)
             + first.stages(0)
             + [
-                (at + 3 * HOP + 3, close, 1),
-                (at + 3 * HOP + 1, attention, WIDE // UNIT),
+                (OUTPUT_AT, second.send, 1),
+                (OUTPUT_AT + 3 * HOP + 3, close, 1),
+                (at + ARRIVED, attention, WIDE // UNIT),
                 (at, feed_both, WIDE // UNIT),
                 (0, mix, WIDE // UNIT),
             ],
-        )
-        returns.send_rest()
-        returns.receive()
-        keys_back(n, layer, returns, keyed, s)
+            tasks,
+        )
         returns.finish()
+        for index in range(len(sizes)):
+            gradient_store(index).wait()
 
         def finish(u):
             first.finish(u)
@@ -972,24 +1018,36 @@
 
         each_of(s.units, finish)
 
-    shapes = kept_shapes(s) | dict(y=((s.rows, s.model), BF16))
+    sizes = grad_sizes(s)
+    backs = attention_back_shapes(s)
+    blocks = block_shapes(s, sizes)
     return run_kernel(
         body,
         layer_ins(stream, saved, w, tables)
         | dict(
             grad=(cotangent, ANY),
+            a1=(saved.a1, ANY),
             qraw=(saved.qraw, ANY),
             kraw=(saved.kraw, ANY),
             qk_gain=(w.qk_gain, VMEM),
             cosine=(tables.cosine, VMEM),
             sine=(tables.sine, VMEM),
         ),
-        outputs(shapes) | attention_back_outs(s),
+        outputs({x: backs[x] for x in dict(dq=0, dk=0, dv=0)})
+        | attention_back_sums(s)
+        | dict(
+            y=(shaped(s.rows, s.model), ANY),
+            grads=[(shaped(*block), ANY) for block in blocks],
+        ),
         layer_scratch(stream, s)
-        | buffers(shapes)
-        | buffers(attention_back_shapes(s))
+        | buffers(kept_shapes(s))
+        | buffers(backs)
         | attention_back_scratch(s)
         | dict(
+            y_v=VMEM((s.rows, s.model), BF16),
+            a1_v=VMEM((s.rows, s.model), BF16),
+            grads_v=[VMEM(block, BF16) for block in blocks],
+            grad_sems=DMA((len(sizes),)),
             inv_v=VMEM((s.rows, HEAD_SIZE), F32),
             grad_v=VMEM((s.rows, s.model), BF16),
             g_v=VMEM((s.rows, s.model), F32),
@@ -1006,12 +1064,28 @@
     return [(c >= 0, (c ^ (1 << b), t)) for b in range(count.bit_length() - 1)]
 
 
+def block_products(target, left, right, line, s):
+    bits = s.count.bit_length() - 1
+    half = s.count // 2
+    for part in range(2):
+        product = dot_tn(left[:, part * half * line : (part + 1) * half * line], right[...])
+        for k in range(half):
+            block = part * half + k
+            at = tuple((block >> b) & 1 for b in range(bits - 1, -1, -1))
+            target[at + (slice(0, line),)] = product[k * line : (k + 1) * line].astype(BF16)
+
+
+def block_shapes(s, sizes):
+    bits = s.count.bit_length() - 1
+    return [(2,) * bits + (line + -line % 16, width) for line, width in sizes]
+
+
 class Scatter:
     def __init__(self, n, s, sizes, factors=None):
         self.n, self.s, self.sizes, self.factors = n, s, sizes, factors
         self.bits = s.count.bit_length() - 1
         self.c, self.t = place()
-        self.loads = []
+        self.beside = []
 
     def bit(self, b):
         return (self.c >> b) & 1
@@ -1057,16 +1131,7 @@
         if self.factors:
             left, right, needed = self.factors[index]
             wait_all(*needed)
-            line = self.sizes[index][0]
-            half = self.s.count // 2
-            for part in range(2):
-                product = dot_tn(left[:, part * half * line : (part + 1) * half * line], right[...])
-                for k in range(half):
-                    block = part * half + k
-                    at = tuple((block >> b) & 1 for b in range(self.bits - 1, -1, -1))
-                    self.own(index)[at + (slice(0, line),)] = product[
-                        k * line : (k + 1) * line
-                    ].astype(BF16)
+            block_products(self.own(index), left, right, self.sizes[index][0], self.s)
         else:
             self.load(index).start()
         self.copy(index, 0).start()
@@ -1085,7 +1150,7 @@
             here = self.spot({b: self.bit(b) for b in order[: step + 1]} | picks)
             total = own[here].astype(F32) + got[tuple(picks[b] for b in free)].astype(F32)
             if step == self.bits - 1:
-                self.n.sums_v[index][...] = total[:line]
+                self.sum_of(index)[...] = total[:line]
             else:
                 own[here] = total.astype(BF16)
             return carry
@@ -1097,20 +1162,24 @@
         if step < self.bits - 1:
             self.copy(index, step + 1).start()
         else:
+            for other in self.beside:
+                other[index].wait()
             self.store(index).start()
 
+    def sum_of(self, index):
+        return self.n.sums_v[index].at[0] if self.factors else self.n.sums_v[index]
+
     def store(self, index):
-        target = self.n.sums[index].at[0] if self.factors else self.n.sums[index]
         return pltpu.make_async_copy(
-            self.n.sums_v[index], target, self.n.scatter_store_sems.at[index]
+            self.n.sums_v[index], self.n.sums[index], self.n.scatter_store_sems.at[index]
         )
 
     def tasks(self, every, bases):
         found = []
         for index in range(len(self.sizes)):
-            found.append((bases[0] + index * every, lambda index=index: self.start(index)))
+            found.append(((bases[0] + index) * every, lambda index=index: self.start(index)))
             for step in range(self.bits):
-                at = bases[min(step + 1, len(bases) - 1)] + index * every
+                at = (bases[min(step + 1, len(bases) - 1)] + index) * every
                 at += 100 * max(0, step + 2 - len(bases))
                 found.append((at, lambda index=index, step=step: self.add(index, step)))
         found.sort(key=lambda item: item[0])
@@ -1123,11 +1192,11 @@
                 self.copy(index, step).wait_send()
 
 
-def scatter_scratch(s, sizes, computed):
+def scatter_scratch(s, sizes, computed, layers):
     bits = s.count.bit_length() - 1
     tails = [(line + -line % 16, width) for line, width in sizes]
     found = dict(
-        sums_v=[VMEM(size, F32) for size in sizes],
+        sums_v=[VMEM(((layers,) if computed else ()) + size, F32) for size in sizes],
         got=[
             VMEM((2,) * (bits - 1 - step) + tail, BF16) for tail in tails for step in range(bits)
         ],
@@ -1290,17 +1359,17 @@
                 n, i, n.x_v[wide_rows(i)], n.kv_v, n.q_v, layer, lower, returns, turned, s
             )
 
-        at = 3 * HOP + 1
+        at = ARRIVED
         pipeline(
             s.units,
             lower.stages(at)
             + upper.stages(0)
             + [
-                (at + 3 * HOP + 1, attention, WIDE // UNIT),
+                (at + ARRIVED, attention, WIDE // UNIT),
                 (at, pass_norm, WIDE // UNIT),
                 (0, inputs, WIDE // UNIT),
             ],
-            scatter.tasks(1, SCATTER_MIDDLE),
+            scatter.tasks(64 // UNIT, SCATTER_MIDDLE),
         )
         returns.send_rest()
         returns.receive()
@@ -1315,7 +1384,7 @@
 
         each_of(s.units, finish)
 
-    whole = [
+    whole = above.grads or [
         block_view(dot_tn(left, right).astype(BF16), s) for left, right in factor_pairs(above)
     ]
     held = dict(
@@ -1345,7 +1414,8 @@
             lowest=(tables.lowest, VMEM),
             whole=[(array, ANY) for array in whole],
         ),
-        attention_back_outs(s)
+        outputs(attention_back_shapes(s))
+        | attention_back_sums(s)
         | dict(
             attn_sum=(shaped(1, s.model, kind=F32), VMEM),
             sums=[(shaped(*size, kind=F32), ANY) for size in sizes],
@@ -1355,7 +1425,7 @@
         | {x + "_v": VMEM(array.shape, array.dtype) for x, array in held.items()}
         | buffers(attention_back_shapes(s))
         | attention_back_scratch(s)
-        | scatter_scratch(s, sizes, False)
+        | scatter_scratch(s, sizes, False, 1)
         | dict(
             lower=line_scratch(s.units, s.model),
             middle_sems=DMA((s.rows // WIDE,)),
@@ -1402,10 +1472,12 @@
         for layer in range(layers):
             n.acc[0, 2 * layer : 2 * layer + 2] = n.qk_in[layer][...]
         wait_all(*early)
-        above = [
-            loads(n.done[(layer - 1) * len(sizes) + index], n.sums[index].at[layer])
+        scatter.beside = [
+            [
+                loads(n.done[(layer - 1) * len(sizes) + index], n.sums_v[index].at[layer])
+                for index in range(len(sizes))
+            ]
             for layer in range(1, layers)
-            for index in range(len(sizes))
         ]
 
         def head_copy(k):
@@ -1429,7 +1501,7 @@
             head_norm(n, unit_rows(u), upper.take(u), 0)
             send_out([u], out)
 
-        tasks = scatter.tasks(1, SCATTER_END)
+        tasks = scatter.tasks(64 // UNIT, SCATTER_END)
         tasks += [(2 * k + 1, lambda k=k: head_step(k)) for k in range(len(rounds) + 1)]
         tasks.sort(key=lambda item: item[0])
         pipeline(
@@ -1471,7 +1543,6 @@
         for k in range(len(rounds)):
             head_copy(k).wait_send()
         scatter.finish()
-        wait_all(*above)
 
         def finish(u):
             upper.finish(u)
@@ -1510,7 +1581,7 @@
         ),
         head_scratch(bottom, s)
         | {x + "_v": VMEM(array.shape, array.dtype) for x, array in held.items()}
-        | scatter_scratch(s, sizes, True)
+        | scatter_scratch(s, sizes, True, layers)
         | dict(
             attn_sum=VMEM((1, s.model), F32),
             acc=VMEM(small, F32),
@@ -1522,6 +1593,36 @@
         ),
         19,
     )
+
+
+OUTPUT_AT = 12
+def deliver(arrays):
+    def body(n):
+        copies = []
+        for index, (source, target, held) in enumerate(zip(n.given, n.result, n.held)):
+            copies.append(
+                (
+                    pltpu.make_async_copy(source, held, n.sems.at[0, index]),
+                    pltpu.make_async_copy(held, target, n.sems.at[1, index]),
+                )
+            )
+            copies[-1][0].start()
+        for fetch, put in copies:
+            fetch.wait()
+            put.start()
+        for fetch, put in copies:
+            put.wait()
+
+    return run_kernel(
+        body,
+        dict(given=[(array, ANY) for array in arrays]),
+        dict(result=[(shaped(*array.shape, kind=array.dtype), ANY) for array in arrays]),
+        dict(
+            held=[VMEM(array.shape, array.dtype) for array in arrays],
+            sems=DMA((2, len(arrays))),
+        ),
+        None,
+    ).result
 
 
 SCATTER_MIDDLE = (0, 3, 9, 16)
@@ -1568,7 +1669,7 @@
         else:
             result = turn_layer(layer, stream, saved, cotangent, w, tables, s)
         own = dict(a1=saved.a1, qraw=saved.qraw, kraw=saved.kraw, q=saved.q, kv=saved.kv)
-        kept.append(types.SimpleNamespace(**(vars(result) | own | dict(x=stream))))
+        kept.append(types.SimpleNamespace(**(dict(grads=None) | vars(result) | own | dict(x=stream))))
         stream = result.y
         saved = result
 
@@ -1589,13 +1690,14 @@
             qk_sum=result.qk_sum,
         )
     end = backward_end(kept, w, s)
-    up, gate, query, down, out, key, value = end.sums
+    small = [end.attn_total, end.ffn_total, end.qk_total]
+    stream, grad, *gains, up, gate, query, down, out, key, value = deliver(
+        [stream, end.dres] + small + end.sums
+    )
     return (
         stream,
-        end.dres,
-        end.attn_total,
-        end.ffn_total,
-        end.qk_total,
+        grad,
+        *gains,
         query,
         key,
         value,

time: 483 us -> 445 us (0.921)
  matrix products: 15.7 us -> 0 us
  local copies, waits for them, and re-layouts: 11.5 us -> 0 us
  Pallas kernels: 444 us -> 433 us
    dot_general x7 -> x0, matrix products: 15.7 us -> none  [dot_tn(): lax.dot_general(left, right, (((0,), (0,)), ((), ())), preferred_element_...]
    unnamed x56 -> x0, local copies, waits for them, and re-layouts: 11.5 us -> none
    pallas_call x5 -> x6, Pallas kernels: 444 us -> 433 us  [run_kernel(): pl.pallas_call(lambda *refs: body(named(refs, groups)), out_shape=[shape...]
where the time goes in v2:
time: 445 us; the launch traced here: 439 us
  Pallas kernels  433 us (97%)
  other arithmetic  4.94 us (1%)
    pallas_call x6, Pallas kernels, run_kernel(): pl.pallas_call(lambda *refs: body(named(refs, groups)), out_shape=[shape...  433 us

profile of v2, /device:TPU:0, one launch (start us, length us, event | category | flops | bytes accessed | tf_op | source)
XLA Modules:
  0.0 439.4 jit_solution(6587918978939214484)
XLA Ops:
  0.6 0.8 select_reduce_fusion.1
  1.4 0.7 select_reduce_fusion
  2.2 0.9 fusion.1.refs_4_.refs_26_
  3.1 2.5 fusion
  5.6 16.5 %shard_map.220 = (bf16[768,1024]{1,0:T(8,128)(2,1)}, f32[768,512]{1,0:T(8,128)}, f32[768,256]{1,0:T(8,128)}, bf16[768,512]{1,0:T(8,128)(2,1)}, bf16[1792,512]{1,0:T(8,128)(2,1)}) custom-call(bf16[768,1024]{1,0:T(8,128)(2,1)} %refs_6_.7, f32[2,1024]{1,0:T(2,128)} %refs_7_.9, f32[2,2,128]{2,1,0:T(2,128)} %refs_23_.1, ...), custom_call_target="tpu_custom_call" | custom-call | tf_op jit(solution)/shard_map/pallas_call | solution.py:129
  22.1 102.3 %shard_map.221 = (bf16[768,512]{1,0:T(8,128)(2,1)}, bf16[768,1024]{1,0:T(8,128)(2,1)}, bf16[768,768]{1,0:T(8,128)(2,1)}, f32[768,128]{1,0:T(8,128)}, f32[768,102...) custom-call(bf16[768,1024]{1,0:T(8,128)(2,1)} %refs_6_.7, ...), custom_call_target="tpu_custom_call" | custom-call | tf_op jit(solution)/shard_map/pallas_call | solution.py:129
  124.4 136.8 %shard_map.222 = (bf16[768,512]{1,0:T(8,128)(2,1)}, bf16[768,256]{1,0:T(8,128)(2,1)}, bf16[768,256]{1,0:T(8,128)(2,1)}, f32[768,1024]{1,0:T(8,128)}, f32[1,1024]...) custom-call(f32[768,1024]{1,0:T(8,128)} %get-tuple-element.87.refs_0, ...), custom_call_target="tpu_custom_call" | custom-call | tf_op jit(solution)/shard_map/pallas_call | solution.py:129
  261.2 101.4 %shard_map.223 = (bf16[768,1024]{1,0:T(8,128)(2,1)}, bf16[768,768]{1,0:T(8,128)(2,1)}, bf16[768,768]{1,0:T(8,128)(2,1)}, bf16[768,1024]{1,0:T(8,128)(2,1)}, bf16...) custom-call(bf16[768,512]{1,0:T(8,128)(2,1)} %get-tuple-element.94.r, ...), custom_call_target="tpu_custom_call" | custom-call | tf_op jit(solution)/shard_map/pallas_call | solution.py:129
  362.6 69.6 %shard_map.224 = (f32[768,1024]{1,0:T(8,128)}, f32[2,128]{1,0:T(2,128)}, f32[2,128]{1,0:T(2,128)}, f32[2,2,128]{2,1,0:T(2,128)}, f32[2,128,768]{2,1,0:T(8,128)},...) custom-call(bf16[768,512]{1,0:T(8,128)(2,1)} %get-tuple-element.112., ...), custom_call_target="tpu_custom_call" | custom-call | tf_op jit(solution)/shard_map/pallas_call | solution.py:129
  432.2 6.8 %shard_map.225 = (bf16[768,1024]{1,0:T(8,128)(2,1)}, f32[768,1024]{1,0:T(8,128)}, f32[2,128]{1,0:T(2,128)}, f32[2,128]{1,0:T(2,128)}, f32[2,2,128]{2,1,0:T(2,128...) custom-call(bf16[768,1024]{1,0:T(8,128)(2,1)} %get-tuple-element.93., ...), custom_call_target="tpu_custom_call" | custom-call | tf_op jit(solution)/shard_map/pallas_call | solution.py:129
  (3 shorter events, 0.0 us)

commit v3 on v2

--- a/solution.py
+++ b/solution.py
@@ -453,48 +453,36 @@
     )
 
 
-def first_projection(stream, w, tables, s):
-    def body(n):
-        loads = Loads(n.load_sems)
-        weights = (
-            loads(n.wk.at[0], n.wk_v),
-            loads(n.wv.at[0], n.wv_v),
-            loads(n.wq.at[0], n.wq_v),
-        )
-        stores = Stores(n.store_sems)
-        made = (
-            stores(n.a1_v, n.a1),
-            stores(n.qraw_v, n.qraw),
-            stores(n.kraw_v, n.kraw),
-            stores(n.q_v, n.q),
-        )
-        halo = Halo(n.kv_v, n.halo_sems, s.rows, s.count)
-        greet(halo_partners(s.rows, s.count))
-        halo.blank()
-        wait_all(*weights)
-
-        def each_keys(i):
-            project_keys(n, i * WIDE, WIDE, n.x[wide_rows(i)].astype(F32), 0)
-            for u in subs(i):
-                halo.send(u)
-
-        def each_queries(i):
-            project_queries(n, i * WIDE, WIDE, 0)
-            send_out(subs(i), *made)
-
-        each_of(s.rows // WIDE, each_keys)
-        each_of(s.rows // WIDE, each_queries)
-        each_of(s.units, halo.finish)
-        keys = loads(n.kv_v, n.kv)
-        each_of(s.units, stores.finish)
-        keys.wait()
-
-    return run_kernel(
-        body,
-        dict(x=(stream, VMEM)) | project_ins(w, tables),
-        outputs(project_shapes(s)),
-        project_scratch(s) | dict(load_sems=DMA((4,)), store_sems=DMA((4, s.units))),
-        1,
+def first_scratch(s):
+    return dict(
+        first_a1=VMEM((s.rows, s.model), BF16),
+        first_qraw=VMEM((s.rows, s.queries), F32),
+        first_kraw=VMEM((s.rows, s.keys), F32),
+        first_wq=VMEM((s.model, s.queries), BF16),
+        first_wk=VMEM((s.model, s.keys), BF16),
+        first_wv=VMEM((s.model, s.keys), BF16),
+        first_sems=DMA((2 * len(halo_plan(s.rows)), s.units)),
+    )
+
+
+def first_outs(s):
+    return outputs({"own_" + x: shape for x, shape in project_shapes(s).items()})
+
+
+def first_view(n):
+    return types.SimpleNamespace(
+        attn_gain=n.attn_gain,
+        qk_gain=n.qk_gain,
+        cosine=n.cosine,
+        sine=n.sine,
+        a1_v=n.first_a1,
+        qraw_v=n.first_qraw,
+        kraw_v=n.first_kraw,
+        q_v=n.qin_v,
+        kv_v=n.kvin_v,
+        wq_v=n.first_wq,
+        wk_v=n.first_wk,
+        wv_v=n.first_wv,
     )
 
 
@@ -770,10 +758,9 @@
 
 
 def layer_ins(stream, saved, w, tables):
-    return dict(
+    before = dict(qin=(saved.q, ANY), kvin=(saved.kv, ANY)) if saved else {}
+    return before | dict(
         x=(stream, ANY),
-        qin=(saved.q, ANY),
-        kvin=(saved.kv, ANY),
         ffn_gain=(w.ffn_gain, VMEM),
         lowest=(tables.lowest, VMEM),
         wo=(w.w_out, ANY),
@@ -792,26 +779,26 @@
     )
 
 
-def layer_scratch(stream, s):
+def layer_scratch(stream, s, stores):
     return weight_scratch(s) | dict(
         x_v=VMEM((s.rows, s.model), stream.dtype),
         qin_v=VMEM((s.rows, s.queries), BF16),
         kvin_v=VMEM((ATTENTION_WINDOW + s.rows, 2 * s.keys), BF16),
-        load_sems=DMA((16,)),
-        store_sems=DMA((16, s.units)),
+        load_sems=DMA((20,)),
+        store_sems=DMA((stores, s.units)),
         first=line_scratch(s.units, s.model),
         second=line_scratch(s.units, s.model),
     )
 
 
-def layer_loads(n, loads, layer):
-    early = (
-        loads(n.qin, n.qin_v),
-        loads(n.kvin, n.kvin_v),
-        loads(n.wo.at[layer], n.wo_v),
-    )
-    late = (
-        loads(n.x, n.x_v),
+def layer_loads(n, loads, layer, projected):
+    if projected:
+        early = (loads(n.qin, n.qin_v), loads(n.kvin, n.kvin_v))
+    else:
+        early = (loads(n.x, n.x_v),)
+    early += (loads(n.wo.at[layer], n.wo_v),)
+    late = () if not projected else (loads(n.x, n.x_v),)
+    late += (
         loads(n.wg.at[layer], n.wg_v),
         loads(n.wu.at[layer], n.wu_v),
         loads(n.wd.at[layer], n.wd_v),
@@ -840,7 +827,13 @@
 def forward_layer(layer, stream, saved, w, tables, s):
     def body(n):
         loads = Loads(n.load_sems)
-        early, late = layer_loads(n, loads, layer)
+        if not saved:
+            own_weights = (
+                loads(n.wk.at[layer], n.first_wk),
+                loads(n.wv.at[layer], n.first_wv),
+                loads(n.wq.at[layer], n.first_wq),
+            )
+        early, late = layer_loads(n, loads, layer, saved is not None)
         above = (
             loads(n.wq.at[layer + 1], n.wq_v),
             loads(n.wk.at[layer + 1], n.wk_v),
@@ -867,6 +860,30 @@
         greet(line_partners() + halo_partners(s.rows, s.count))
         halo.blank()
         wait_all(*early)
+        if not saved:
+            wait_all(*own_weights)
+            own = first_view(n)
+            own_halo = Halo(n.kvin_v, n.first_sems, s.rows, s.count)
+            own_halo.blank()
+
+            def own_keys(i):
+                project_keys(own, i * WIDE, WIDE, n.x_v[wide_rows(i)].astype(F32), layer)
+                for u in subs(i):
+                    own_halo.send(u)
+
+            def own_queries(i):
+                project_queries(own, i * WIDE, WIDE, layer)
+
+            each_of(s.rows // WIDE, own_keys)
+            each_of(s.rows // WIDE, own_queries)
+            each_of(s.units, own_halo.finish)
+            own_out = (
+                loads(n.kvin_v, n.own_kv),
+                loads(n.first_a1, n.own_a1),
+                loads(n.first_qraw, n.own_qraw),
+                loads(n.first_kraw, n.own_kraw),
+                loads(n.qin_v, n.own_q),
+            )
 
         def mix(i):
             attend(n, i, s)
@@ -911,12 +928,19 @@
 
         each_of(s.units, finish)
         keys.wait()
+        if not saved:
+            wait_all(*own_out)
 
     return run_kernel(
         body,
         layer_ins(stream, saved, w, tables) | project_ins(w, tables),
-        outputs(forward_shapes(s)) | outputs(project_shapes(s)),
-        layer_scratch(stream, s) | buffers(forward_shapes(s)) | project_scratch(s),
+        outputs(forward_shapes(s))
+        | outputs(project_shapes(s))
+        | ({} if saved else first_outs(s)),
+        layer_scratch(stream, s, 12)
+        | buffers(forward_shapes(s))
+        | project_scratch(s)
+        | ({} if saved else first_scratch(s)),
         2 + layer,
     )
 
@@ -924,7 +948,7 @@
 def turn_layer(layer, stream, saved, cotangent, w, tables, s):
     def body(n):
         loads = Loads(n.load_sems)
-        early, late = layer_loads(n, loads, layer)
+        early, late = layer_loads(n, loads, layer, True)
         late = late + (loads(n.grad, n.grad_v),)
         raws = (loads(n.qraw, n.qraw_v), loads(n.kraw, n.kraw_v))
         a1 = loads(n.a1, n.a1_v)
@@ -935,7 +959,6 @@
         first, second, lower = LineSum(n.first), LineSum(n.second), LineSum(n.lower)
         returns = Returns(n, s)
         greet(line_partners() + halo_partners(s.rows, s.count))
-        back_start(n, returns)
         wait_all(*early)
 
         def mix(i):
@@ -988,7 +1011,7 @@
             (n.a1_v, n.dv_v),
         ]
         after = at + ARRIVED + s.units
-        tasks = [(after, returns.send_rest), (after + 4, end_keys)]
+        tasks = [(1, lambda: back_start(n, returns)), (after, returns.send_rest), (after + 4, end_keys)]
         for index, step in enumerate((1, 2, 5, 3, 4, 6, 6)):
             tasks.append((after + step, lambda index=index: gradient(index)))
         tasks.sort(key=lambda item: item[0])
@@ -1039,7 +1062,7 @@
             y=(shaped(s.rows, s.model), ANY),
             grads=[(shaped(*block), ANY) for block in blocks],
         ),
-        layer_scratch(stream, s)
+        layer_scratch(stream, s, 5)
         | buffers(kept_shapes(s))
         | buffers(backs)
         | attention_back_scratch(s)
@@ -1177,9 +1200,9 @@
     def tasks(self, every, bases):
         found = []
         for index in range(len(self.sizes)):
-            found.append(((bases[0] + index) * every, lambda index=index: self.start(index)))
+            found.append((bases[0] + index * every, lambda index=index: self.start(index)))
             for step in range(self.bits):
-                at = (bases[min(step + 1, len(bases) - 1)] + index) * every
+                at = bases[min(step + 1, len(bases) - 1)] + index * every
                 at += 100 * max(0, step + 2 - len(bases))
                 found.append((at, lambda index=index, step=step: self.add(index, step)))
         found.sort(key=lambda item: item[0])
@@ -1334,7 +1357,6 @@
         returns = Returns(n, s)
         greet(line_partners() + halo_partners(s.rows, s.count) + halving_partners(s.count))
         n.attn_sum[...] = jnp.zeros_like(n.attn_sum)
-        back_start(n, returns)
         wait_all(*early)
 
         def middle_copy(i):
@@ -1369,7 +1391,7 @@
                 (at, pass_norm, WIDE // UNIT),
                 (0, inputs, WIDE // UNIT),
             ],
-            scatter.tasks(64 // UNIT, SCATTER_MIDDLE),
+            [(0, lambda: back_start(n, returns))] + scatter.tasks(1, SCATTER_MIDDLE),
         )
         returns.send_rest()
         returns.receive()
@@ -1501,7 +1523,7 @@
             head_norm(n, unit_rows(u), upper.take(u), 0)
             send_out([u], out)
 
-        tasks = scatter.tasks(64 // UNIT, SCATTER_END)
+        tasks = scatter.tasks(SCATTER_EVERY, SCATTER_END)
         tasks += [(2 * k + 1, lambda k=k: head_step(k)) for k in range(len(rounds) + 1)]
         tasks.sort(key=lambda item: item[0])
         pipeline(
@@ -1595,7 +1617,7 @@
     )
 
 
-OUTPUT_AT = 12
+OUTPUT_AT = 17
 def deliver(arrays):
     def body(n):
         copies = []
@@ -1626,6 +1648,7 @@
 
 
 SCATTER_MIDDLE = (0, 3, 9, 16)
+SCATTER_EVERY = 1
 SCATTER_END = (0, 2, 7, 11)
 
 
@@ -1662,13 +1685,22 @@
 
     kept = []
     stream = hidden_in
-    saved = first_projection(stream, w, tables, s)
+    saved = None
     for layer in range(layers):
         if layer < layers - 1:
             result = forward_layer(layer, stream, saved, w, tables, s)
         else:
             result = turn_layer(layer, stream, saved, cotangent, w, tables, s)
-        own = dict(a1=saved.a1, qraw=saved.qraw, kraw=saved.kraw, q=saved.q, kv=saved.kv)
+        if saved:
+            own = dict(a1=saved.a1, qraw=saved.qraw, kraw=saved.kraw, q=saved.q, kv=saved.kv)
+        else:
+            own = dict(
+                a1=result.own_a1,
+                qraw=result.own_qraw,
+                kraw=result.own_kraw,
+                q=result.own_q,
+                kv=result.own_kv,
+            )
         kept.append(types.SimpleNamespace(**(dict(grads=None) | vars(result) | own | dict(x=stream))))
         stream = result.y
         saved = result

time: 445 us -> 433 us (0.973)
  Pallas kernels: 433 us -> 422 us
    pallas_call x6 -> x5, Pallas kernels: 433 us -> 422 us  [run_kernel(): pl.pallas_call(lambda *refs: body(named(refs, groups)), out_shape=[shape...]
where the time goes in v3:
time: 433 us; the launch traced here: 428 us
  Pallas kernels  422 us (97%)
  other arithmetic  4.94 us (1%)
    pallas_call x5, Pallas kernels, run_kernel(): pl.pallas_call(lambda *refs: body(named(refs, groups)), out_shape=[shape...  422 us

profile of v3, /device:TPU:0, one launch (start us, length us, event | category | flops | bytes accessed | tf_op | source)
XLA Modules:
  0.0 427.8 jit_solution(6289601182298850557)
XLA Ops:
  0.6 0.8 select_reduce_fusion.1
  1.4 0.7 select_reduce_fusion
  2.2 0.9 fusion.1.refs_2_.refs_4_.refs_26_
  3.1 2.5 fusion
  5.6 104.8 %shard_map.220 = (bf16[768,512]{1,0:T(8,128)(2,1)}, bf16[768,1024]{1,0:T(8,128)(2,1)}, bf16[768,768]{1,0:T(8,128)(2,1)}, f32[768,128]{1,0:T(8,128)}, f32[768,102...) custom-call(bf16[768,1024]{1,0:T(8,128)(2,1)} %refs_6_.5, ...), custom_call_target="tpu_custom_call" | custom-call | tf_op jit(solution)/shard_map/pallas_call | solution.py:129
  110.4 140.9 %shard_map.221 = (bf16[768,512]{1,0:T(8,128)(2,1)}, bf16[768,256]{1,0:T(8,128)(2,1)}, bf16[768,256]{1,0:T(8,128)(2,1)}, f32[768,1024]{1,0:T(8,128)}, f32[1,1024]...) custom-call(bf16[768,512]{1,0:T(8,128)(2,1)} %get-tuple-element.85.r, ...), custom_call_target="tpu_custom_call" | custom-call | tf_op jit(solution)/shard_map/pallas_call | solution.py:129
  251.4 101.0 %shard_map.222 = (bf16[768,1024]{1,0:T(8,128)(2,1)}, bf16[768,768]{1,0:T(8,128)(2,1)}, bf16[768,768]{1,0:T(8,128)(2,1)}, bf16[768,1024]{1,0:T(8,128)(2,1)}, bf16...) custom-call(bf16[768,512]{1,0:T(8,128)(2,1)} %get-tuple-element.92.r, ...), custom_call_target="tpu_custom_call" | custom-call | tf_op jit(solution)/shard_map/pallas_call | solution.py:129
  352.4 68.4 %shard_map.223 = (f32[768,1024]{1,0:T(8,128)}, f32[2,128]{1,0:T(2,128)}, f32[2,128]{1,0:T(2,128)}, f32[2,2,128]{2,1,0:T(2,128)}, f32[2,128,768]{2,1,0:T(8,128)},...) custom-call(bf16[768,512]{1,0:T(8,128)(2,1)} %get-tuple-element.112., ...), custom_call_target="tpu_custom_call" | custom-call | tf_op jit(solution)/shard_map/pallas_call | solution.py:129
  420.8 6.8 %shard_map.224 = (bf16[768,1024]{1,0:T(8,128)(2,1)}, f32[768,1024]{1,0:T(8,128)}, f32[2,128]{1,0:T(2,128)}, f32[2,128]{1,0:T(2,128)}, f32[2,2,128]{2,1,0:T(2,128...) custom-call(bf16[768,1024]{1,0:T(8,128)(2,1)} %get-tuple-element.91., ...), custom_call_target="tpu_custom_call" | custom-call | tf_op jit(solution)/shard_map/pallas_call | solution.py:129
  (3 shorter events, 0.0 us)

commit v4 on v3

--- a/solution.py
+++ b/solution.py
@@ -262,7 +262,8 @@
             self.outwards(u).wait_send()
 
     def stages(self, begin, hop=HOP):
-        return [(begin + 2 * hop, self.spread, 1), (begin + hop, self.meet, 1)]
+        number = self.part.shape[0]
+        return [(begin + 2 * hop, self.spread, 1, number), (begin + hop, self.meet, 1, number)]
 
 
 def line_scratch(units, width):
@@ -271,11 +272,12 @@
 
 
 def pipeline(units, stages, tasks=()):
-    steps = units + max(delay + 1 - taken for delay, unused, taken in stages)
+    stages = [stage if len(stage) > 3 else stage + (units,) for stage in stages]
+    steps = max(number + delay + 1 - taken for delay, unused, taken, number in stages)
 
     def step(s, carry):
-        for delay, function, taken in stages:
-            ready = (s >= delay) & (s < units + delay)
+        for delay, function, taken, number in stages:
+            ready = (s >= delay) & (s < number + delay)
             if taken > 1:
                 ready = ready & ((s - delay) % taken == 0)
 
@@ -546,7 +548,7 @@
     n.inv_v[rows] = inverses
 
 
-def attend_back(n, i, grad_out, keys_ref, query_ref, s):
+def attend_back(n, i, grad_out, keys_ref, query_ref, s, first_done):
     rows = wide_rows(i)
     lowest = n.lowest[rows]
     query_rows, mixed_rows, inverses = query_ref[rows], n.o_v[rows], n.inv_v[rows]
@@ -573,6 +575,8 @@
             found[g] = found[g] + dot_nn(grad_scores, key_rows)
             n.dkv_v[keys, head_cols(g)] += dot_tn(grad_scores, queries[g])
             n.dkv_v[keys, head_cols(s.groups + g)] += dot_tn(probs.astype(BF16), grads[g])
+        if block == 0:
+            first_done()
     return [
         found[g][r * WIDE : (r + 1) * WIDE] for g in range(s.groups) for r in range(s.repeat)
     ]
@@ -714,8 +718,14 @@
     low = total.astype(BF16)
     n.dhb_v[here] = low
     grad_out = dot_nt(low, n.wo_v[...]).astype(BF16)
-    pieces = attend_back(n, i, grad_out, keys_ref, query_ref, s)
+    early = s.rows - WIDE + KEY_BLOCK >= ATTENTION_WINDOW
+    send_rest = lambda: pl.when(i == s.rows // WIDE - 1)(returns.send_rest)
+    pieces = attend_back(
+        n, i, grad_out, keys_ref, query_ref, s, send_rest if early else lambda: None
+    )
     returns.send_complete(i)
+    if not early:
+        send_rest()
     for head, piece in enumerate(pieces):
         n.dq_v[here, head_cols(head)] = head_back(
             n, here, piece * SCALE, n.qraw_v[here, head_cols(head)], 0, layer
@@ -945,6 +955,10 @@
     )
 
 
+def units_at_turn(s):
+    return s.units - min(REST_WIDES, s.rows // WIDE // 2) * (WIDE // UNIT)
+
+
 def turn_layer(layer, stream, saved, cotangent, w, tables, s):
     def body(n):
         loads = Loads(n.load_sems)
@@ -953,7 +967,8 @@
         raws = (loads(n.qraw, n.qraw_v), loads(n.kraw, n.kraw_v))
         a1 = loads(n.a1, n.a1_v)
         stores = Stores(n.store_sems)
-        closed = (stores(n.y_v, n.y),)
+        closed = Stores(n.y_sems)
+        put_result = closed(n.y_v, n.y)
         turned = (stores(n.g_v, n.dres), stores(n.dq_v, n.dq))
         keyed = (stores(n.dk_v, n.dk), stores(n.dv_v, n.dv))
         first, second, lower = LineSum(n.first), LineSum(n.second), LineSum(n.lower)
@@ -973,12 +988,30 @@
             n.g_v[here] = n.grad_v[here].astype(F32)
             gate, up, part = feed(n, i, middle, layer)
             feed_back(n, i, gate, up, lower, ())
-            second.hold(i, part)
+
+            @pl.when(i < here_units * UNIT // WIDE)
+            def _():
+                second.hold(i, part)
+
+            @pl.when(i >= here_units * UNIT // WIDE)
+            def _():
+                for k, u in enumerate(subs(i)):
+                    n.rest_v[u - here_units] = part[k * UNIT : (k + 1) * UNIT].astype(BF16)
 
         def close(u):
             here = unit_rows(u)
             n.y_v[here] = (n.x_v[here] + second.take(u)).astype(BF16)
-            send_out([u], *closed)
+            send_out([u], put_result)
+
+        rest_rows = pl.ds(here_units * UNIT, s.rows - here_units * UNIT)
+        rest = (
+            pltpu.make_async_copy(n.rest_v, n.rest, n.rest_sems.at[0]),
+            pltpu.make_async_copy(n.x_v.at[rest_rows], n.rest_h, n.rest_sems.at[1]),
+        )
+
+        def put_rest():
+            for copy in rest:
+                copy.start()
 
         def attention(i):
             pl.when(i == 0)(lambda: wait_all(*raws))
@@ -1011,7 +1044,7 @@
             (n.a1_v, n.dv_v),
         ]
         after = at + ARRIVED + s.units
-        tasks = [(1, lambda: back_start(n, returns)), (after, returns.send_rest), (after + 4, end_keys)]
+        tasks = [(1, lambda: back_start(n, returns)), (at + s.units, put_rest), (after + 4, end_keys)]
         for index, step in enumerate((1, 2, 5, 3, 4, 6, 6)):
             tasks.append((after + step, lambda index=index: gradient(index)))
         tasks.sort(key=lambda item: item[0])
@@ -1021,8 +1054,8 @@
             + second.stages(OUTPUT_AT, HOP + 1)
             + first.stages(0)
             + [
-                (OUTPUT_AT, second.send, 1),
-                (OUTPUT_AT + 3 * HOP + 3, close, 1),
+                (OUTPUT_AT, second.send, 1, here_units),
+                (OUTPUT_AT + 3 * HOP + 3, close, 1, here_units),
                 (at + ARRIVED, attention, WIDE // UNIT),
                 (at, feed_both, WIDE // UNIT),
                 (0, mix, WIDE // UNIT),
@@ -1033,17 +1066,25 @@
         for index in range(len(sizes)):
             gradient_store(index).wait()
 
+        wait_all(*rest)
+
         def finish(u):
             first.finish(u)
-            second.finish(u)
             lower.finish(u)
             stores.finish(u)
 
+        def finish_result(u):
+            second.finish(u)
+            closed.finish(u)
+
         each_of(s.units, finish)
+        each_of(here_units, finish_result)
 
     sizes = grad_sizes(s)
     backs = attention_back_shapes(s)
     blocks = block_shapes(s, sizes)
+    here_units = units_at_turn(s)
+    rest_units = s.units - here_units
     return run_kernel(
         body,
         layer_ins(stream, saved, w, tables)
@@ -1059,7 +1100,9 @@
         outputs({x: backs[x] for x in dict(dq=0, dk=0, dv=0)})
         | attention_back_sums(s)
         | dict(
-            y=(shaped(s.rows, s.model), ANY),
+            y=(shaped(here_units * UNIT, s.model), ANY),
+            rest=(shaped(rest_units, UNIT, s.model), ANY),
+            rest_h=(shaped(rest_units * UNIT, s.model, kind=F32), ANY),
             grads=[(shaped(*block), ANY) for block in blocks],
         ),
         layer_scratch(stream, s, 5)
@@ -1067,7 +1110,11 @@
         | buffers(backs)
         | attention_back_scratch(s)
         | dict(
-            y_v=VMEM((s.rows, s.model), BF16),
+            y_v=VMEM((here_units * UNIT, s.model), BF16),
+            y_sems=DMA((1, here_units)),
+            rest_v=VMEM((rest_units, UNIT, s.model), BF16),
+            rest_sems=DMA((2,)),
+            second=line_scratch(here_units, s.model),
             a1_v=VMEM((s.rows, s.model), BF16),
             grads_v=[VMEM(block, BF16) for block in blocks],
             grad_sems=DMA((len(sizes),)),
@@ -1328,11 +1375,23 @@
 def backward_layer(layer, kept, w, tables, s):
     above, here_kept = kept[layer + 1], kept[layer]
     sizes = grad_sizes(s)
+    rest_units = s.units - units_at_turn(s) if layer + 2 == len(kept) else 0
+    backs = attention_back_shapes(s)
+    extra_ins, extra_outs, extra_scratch = {}, {}, {}
+    if rest_units:
+        extra_ins = dict(rest=(above.rest, ANY), rest_h=(above.rest_h, ANY))
+        extra_outs = dict(y=(shaped(rest_units * UNIT, s.model), ANY))
+        extra_scratch = dict(
+            second=line_scratch(rest_units, s.model),
+            y_sems=DMA((1, rest_units)),
+            rest_sems=DMA((1,)),
+        )
 
     def body(n):
         loads = Loads(n.load_sems)
         early, middle_loads = head_loads(n, loads, layer + 1)
         scatter = Scatter(n, s, sizes)
+        n.dgate_v, n.dup_v = n.gate_v, n.up_v
         feeds = (
             loads(n.wd.at[layer], n.wd_v),
             loads(n.gate, n.gate_v),
@@ -1359,6 +1418,28 @@
         n.attn_sum[...] = jnp.zeros_like(n.attn_sum)
         wait_all(*early)
 
+        if rest_units:
+            second = LineSum(n.second)
+            rest = loads(n.rest, second.part)
+            rest_h = pltpu.make_async_copy(
+                n.rest_h, n.x_v.at[pl.ds(0, rest_units * UNIT)], n.rest_sems.at[0]
+            )
+
+            def result_copy(u):
+                return pltpu.make_async_copy(
+                    second.inner.at[u], n.y.at[unit_rows(u)], n.y_sems.at[0, u]
+                )
+
+            def send_result(u):
+                pl.when(u == 0)(rest.wait)
+                second.send(u)
+
+            def close(u):
+                pl.when(u == 0)(rest_h.wait)
+                total = n.x_v[unit_rows(u)].astype(F32) + second.take(u)
+                second.inner[u] = total.astype(BF16)
+                result_copy(u).start()
+
         def middle_copy(i):
             rows = wide_rows(i)
             return pltpu.make_async_copy(n.h.at[rows], n.x_v.at[rows], n.middle_sems.at[i])
@@ -1382,22 +1463,42 @@
             )
 
         at = ARRIVED
+        after = at + ARRIVED + s.units
+
+        def end_keys():
+            returns.receive()
+            keys_back(n, layer, returns, keyed, s)
+
+        tasks = [(0, lambda: back_start(n, returns)), (after + 2, end_keys)]
+        tasks += scatter.tasks(1, SCATTER_MIDDLE)
+        stages = lower.stages(at) + upper.stages(0)
+        if rest_units:
+            passed = at + ARRIVED + -(-rest_units * UNIT // WIDE) * (WIDE // UNIT) - 1
+            tasks.append((passed, rest_h.start))
+            stages += second.stages(REST_AT, REST_HOP) + [
+                (REST_AT, send_result, 1, rest_units),
+                (max(REST_AT + 3 * REST_HOP, passed + 1), close, 1, rest_units),
+            ]
+        tasks.sort(key=lambda item: item[0])
         pipeline(
             s.units,
-            lower.stages(at)
-            + upper.stages(0)
+            stages
             + [
                 (at + ARRIVED, attention, WIDE // UNIT),
                 (at, pass_norm, WIDE // UNIT),
                 (0, inputs, WIDE // UNIT),
             ],
-            [(0, lambda: back_start(n, returns))] + scatter.tasks(1, SCATTER_MIDDLE),
-        )
-        returns.send_rest()
-        returns.receive()
-        keys_back(n, layer, returns, keyed, s)
+            tasks,
+        )
         returns.finish()
         scatter.finish()
+        if rest_units:
+
+            def finish_result(u):
+                second.finish(u)
+                result_copy(u).wait()
+
+            each_of(rest_units, finish_result)
 
         def finish(u):
             upper.finish(u)
@@ -1435,17 +1536,20 @@
             sine=(tables.sine, VMEM),
             lowest=(tables.lowest, VMEM),
             whole=[(array, ANY) for array in whole],
-        ),
+        )
+        | extra_ins,
         outputs(attention_back_shapes(s))
         | attention_back_sums(s)
         | dict(
             attn_sum=(shaped(1, s.model, kind=F32), VMEM),
             sums=[(shaped(*size, kind=F32), ANY) for size in sizes],
-        ),
+        )
+        | extra_outs,
         head_scratch(above, s)
+        | extra_scratch
         | weight_scratch(s)
         | {x + "_v": VMEM(array.shape, array.dtype) for x, array in held.items()}
-        | buffers(attention_back_shapes(s))
+        | buffers({x: b for x, b in backs.items() if x not in dict(dgate=0, dup=0)})
         | attention_back_scratch(s)
         | scatter_scratch(s, sizes, False, 1)
         | dict(
@@ -1617,15 +1721,22 @@
     )
 
 
-OUTPUT_AT = 17
-def deliver(arrays):
+def deliver(results):
+    pieces = [piece for result in results for piece in result]
+    spots = [
+        (index, sum(other.shape[0] for other in result[:k]), result[k].shape[0])
+        for index, result in enumerate(results)
+        for k in range(len(result))
+    ]
+
     def body(n):
         copies = []
-        for index, (source, target, held) in enumerate(zip(n.given, n.result, n.held)):
+        for k, (index, first, rows) in enumerate(spots):
+            target = n.result[index].at[pl.ds(first, rows)]
             copies.append(
                 (
-                    pltpu.make_async_copy(source, held, n.sems.at[0, index]),
-                    pltpu.make_async_copy(held, target, n.sems.at[1, index]),
+                    pltpu.make_async_copy(n.given[k], n.held[k], n.sems.at[0, k]),
+                    pltpu.make_async_copy(n.held[k], target, n.sems.at[1, k]),
                 )
             )
             copies[-1][0].start()
@@ -1635,18 +1746,30 @@
         for fetch, put in copies:
             put.wait()
 
+    shapes = [
+        (sum(piece.shape[0] for piece in result),) + result[0].shape[1:] for result in results
+    ]
     return run_kernel(
         body,
-        dict(given=[(array, ANY) for array in arrays]),
-        dict(result=[(shaped(*array.shape, kind=array.dtype), ANY) for array in arrays]),
+        dict(given=[(piece, ANY) for piece in pieces]),
         dict(
-            held=[VMEM(array.shape, array.dtype) for array in arrays],
-            sems=DMA((2, len(arrays))),
+            result=[
+                (shaped(*shape, kind=result[0].dtype), ANY)
+                for shape, result in zip(shapes, results)
+            ]
+        ),
+        dict(
+            held=[VMEM(piece.shape, piece.dtype) for piece in pieces],
+            sems=DMA((2, len(pieces))),
         ),
         None,
     ).result
 
 
+OUTPUT_AT = 17
+REST_AT = 19
+REST_WIDES = 2
+REST_HOP = 3
 SCATTER_MIDDLE = (0, 3, 9, 16)
 SCATTER_EVERY = 1
 SCATTER_END = (0, 2, 7, 11)
@@ -1704,9 +1827,12 @@
         kept.append(types.SimpleNamespace(**(dict(grads=None) | vars(result) | own | dict(x=stream))))
         stream = result.y
         saved = result
+    streams = [stream]
 
     for layer in range(layers - 2, -1, -1):
         result = backward_layer(layer, kept, w, tables, s)
+        if layer == layers - 2:
+            streams.append(result.y)
         kept[layer + 1].attn_sum = result.attn_sum
         kept[layer + 1].sums = result.sums
         vars(kept[layer]).update(
@@ -1724,7 +1850,7 @@
     end = backward_end(kept, w, s)
     small = [end.attn_total, end.ffn_total, end.qk_total]
     stream, grad, *gains, up, gate, query, down, out, key, value = deliver(
-        [stream, end.dres] + small + end.sums
+        [streams] + [[array] for array in [end.dres] + small + end.sums]
     )
     return (
         stream,

time: 433 us -> 422 us (0.975)
  Pallas kernels: 422 us -> 411 us
    pallas_call x5, Pallas kernels: 422 us -> 411 us  [run_kernel(): pl.pallas_call(lambda *refs: body(named(refs, groups)), out_shape=[shape...]
where the time goes in v4:
time: 422 us; the launch traced here: 417 us
  Pallas kernels  411 us (97%)
  other arithmetic  4.94 us (1%)
    pallas_call x5, Pallas kernels, run_kernel(): pl.pallas_call(lambda *refs: body(named(refs, groups)), out_shape=[shape...  411 us

profile of v4, /device:TPU:0, one launch (start us, length us, event | category | flops | bytes accessed | tf_op | source)
XLA Modules:
  0.0 416.9 jit_solution(3376053303706064445)
XLA Ops:
  0.6 0.8 select_reduce_fusion.1
  1.4 0.7 select_reduce_fusion
  2.2 0.9 fusion.1.refs_2_.refs_4_.refs_26_
  3.1 2.5 fusion
  5.6 104.8 %shard_map.220 = (bf16[768,512]{1,0:T(8,128)(2,1)}, bf16[768,1024]{1,0:T(8,128)(2,1)}, bf16[768,768]{1,0:T(8,128)(2,1)}, f32[768,128]{1,0:T(8,128)}, f32[768,102...) custom-call(bf16[768,1024]{1,0:T(8,128)(2,1)} %refs_6_.5, ...), custom_call_target="tpu_custom_call" | custom-call | tf_op jit(solution)/shard_map/pallas_call | solution.py:129
  110.4 128.7 %shard_map.221 = (bf16[768,512]{1,0:T(8,128)(2,1)}, bf16[768,256]{1,0:T(8,128)(2,1)}, bf16[768,256]{1,0:T(8,128)(2,1)}, f32[768,1024]{1,0:T(8,128)}, f32[1,1024]...) custom-call(bf16[768,512]{1,0:T(8,128)(2,1)} %get-tuple-element.88.r, ...), custom_call_target="tpu_custom_call" | custom-call | tf_op jit(solution)/shard_map/pallas_call | solution.py:129
  239.1 110.2 %shard_map.222 = (bf16[768,1024]{1,0:T(8,128)(2,1)}, bf16[768,768]{1,0:T(8,128)(2,1)}, bf16[768,768]{1,0:T(8,128)(2,1)}, bf16[768,1024]{1,0:T(8,128)(2,1)}, bf16...) custom-call(bf16[768,512]{1,0:T(8,128)(2,1)} %get-tuple-element.95.r, ...), custom_call_target="tpu_custom_call" | custom-call | tf_op jit(solution)/shard_map/pallas_call | solution.py:129
  349.3 61.1 %shard_map.223 = (f32[768,1024]{1,0:T(8,128)}, f32[2,128]{1,0:T(2,128)}, f32[2,128]{1,0:T(2,128)}, f32[2,2,128]{2,1,0:T(2,128)}, f32[2,128,768]{2,1,0:T(8,128)},...) custom-call(bf16[768,512]{1,0:T(8,128)(2,1)} %get-tuple-element.118., ...), custom_call_target="tpu_custom_call" | custom-call | tf_op jit(solution)/shard_map/pallas_call | solution.py:129
  410.4 6.0 %shard_map.224 = (bf16[768,1024]{1,0:T(8,128)(2,1)}, f32[768,1024]{1,0:T(8,128)}, f32[2,128]{1,0:T(2,128)}, f32[2,128]{1,0:T(2,128)}, f32[2,2,128]{2,1,0:T(2,128...) custom-call(bf16[512,1024]{1,0:T(8,128)(2,1)} %get-tuple-element.94., ...), custom_call_target="tpu_custom_call" | custom-call | tf_op jit(solution)/shard_map/pallas_call | solution.py:129
  (3 shorter events, 0.0 us)

commit v5 on v4

--- a/solution.py
+++ b/solution.py
@@ -63,23 +63,27 @@
     return jnp.sum(value_rows, axis=0, keepdims=True)
 
 
-def make_tables(lengths, rows):
+def rotation_frequencies():
+    half = jnp.arange(HEAD_SIZE // 2, dtype=F32)
+    freq = THETA ** (-(half * 2.0) / HEAD_SIZE)
+    return jnp.concatenate([freq, freq])[None, :]
+
+
+def fill_tables(n, i, rows):
+    here = wide_rows(i)
     start = lax.axis_index(CTX) * rows
-    spot = start + jnp.arange(rows, dtype=jnp.int32)
-    order = jnp.arange(lengths.shape[0])
-    ends = jnp.sum(jnp.where(order[None, :] <= order[:, None], lengths[None, :], 0), axis=1)
-    passed = ends[None, :] <= spot[:, None]
-    begin = jnp.sum(jnp.where(passed, lengths[None, :], 0), axis=1)
-    lane = jnp.arange(HEAD_SIZE)
-    half = HEAD_SIZE // 2
-    freq = THETA ** (-((lane % half).astype(F32) * 2.0) / HEAD_SIZE)
-    angle = (spot - begin).astype(F32)[:, None] * freq[None, :]
+    shape = (WIDE, HEAD_SIZE)
+    spot = start + i * WIDE + lax.broadcasted_iota(jnp.int32, shape, 0)
+    begin, end = jnp.zeros(shape, jnp.int32), 0
+    for doc in range(n.lengths.shape[0]):
+        end = end + n.lengths[doc]
+        begin = begin + jnp.where(spot >= end, n.lengths[doc], 0)
+    angle = (spot - begin).astype(F32) * n.frequencies[...]
+    lane = lax.broadcasted_iota(jnp.int32, shape, 1)
+    n.cosine[here] = jnp.cos(angle)
+    n.sine[here] = jnp.sin(angle) * jnp.where(lane < HEAD_SIZE // 2, -1.0, 1.0)
     lowest = jnp.maximum(begin, spot - (ATTENTION_WINDOW - 1)) - (start - ATTENTION_WINDOW)
-    return types.SimpleNamespace(
-        cosine=jnp.cos(angle),
-        sine=jnp.sin(angle) * jnp.where(lane < half, -1.0, 1.0)[None, :],
-        lowest=lowest[:, None],
-    )
+    n.lowest[here] = lowest[:, :1]
 
 
 def halo_plan(rows):
@@ -156,7 +160,7 @@
     )
 
 
-def greet(partners):
+def greet(partners, meanwhile=lambda: None):
     barrier = pltpu.get_barrier_semaphore()
     total = 0
     for exists, device in partners:
@@ -166,6 +170,7 @@
         def _():
             pl.semaphore_signal(barrier, inc=1, device_id=device, device_id_type=MESH)
 
+    meanwhile()
     pl.semaphore_wait(barrier, total)
 
 
@@ -435,11 +440,10 @@
 
 
 def project_ins(w, tables):
-    return dict(
+    turns = dict(cosine=(tables.cosine, VMEM), sine=(tables.sine, VMEM)) if tables else {}
+    return turns | dict(
         attn_gain=(w.attn_gain, VMEM),
         qk_gain=(w.qk_gain, VMEM),
-        cosine=(tables.cosine, VMEM),
-        sine=(tables.sine, VMEM),
         wq=(w.w_query, ANY),
         wk=(w.key_weight, ANY),
         wv=(w.value_weight, ANY),
@@ -468,7 +472,11 @@
 
 
 def first_outs(s):
-    return outputs({"own_" + x: shape for x, shape in project_shapes(s).items()})
+    return outputs({"own_" + x: shape for x, shape in project_shapes(s).items()}) | dict(
+        cosine=(shaped(s.rows, HEAD_SIZE, kind=F32), VMEM),
+        sine=(shaped(s.rows, HEAD_SIZE, kind=F32), VMEM),
+        lowest=(shaped(s.rows, 1, kind=jnp.int32), VMEM),
+    )
 
 
 def first_view(n):
@@ -768,11 +776,14 @@
 
 
 def layer_ins(stream, saved, w, tables):
-    before = dict(qin=(saved.q, ANY), kvin=(saved.kv, ANY)) if saved else {}
+    before = {}
+    if saved:
+        before = dict(
+            qin=(saved.q, ANY), kvin=(saved.kv, ANY), lowest=(tables.lowest, VMEM)
+        )
     return before | dict(
         x=(stream, ANY),
         ffn_gain=(w.ffn_gain, VMEM),
-        lowest=(tables.lowest, VMEM),
         wo=(w.w_out, ANY),
         wg=(w.w_gate, ANY),
         wu=(w.w_up, ANY),
@@ -834,7 +845,7 @@
     )
 
 
-def forward_layer(layer, stream, saved, w, tables, s):
+def forward_layer(layer, stream, saved, w, tables, s, lengths):
     def body(n):
         loads = Loads(n.load_sems)
         if not saved:
@@ -867,8 +878,13 @@
         )
         first, second = LineSum(n.first), LineSum(n.second)
         halo = Halo(n.kv_v, n.halo_sems, s.rows, s.count)
-        greet(line_partners() + halo_partners(s.rows, s.count))
-        halo.blank()
+
+        def meanwhile():
+            halo.blank()
+            if not saved:
+                each_of(s.rows // WIDE, lambda i: fill_tables(n, i, s.rows))
+
+        greet(line_partners() + halo_partners(s.rows, s.count), meanwhile)
         wait_all(*early)
         if not saved:
             wait_all(*own_weights)
@@ -943,7 +959,16 @@
 
     return run_kernel(
         body,
-        layer_ins(stream, saved, w, tables) | project_ins(w, tables),
+        layer_ins(stream, saved, w, tables)
+        | project_ins(w, tables)
+        | (
+            {}
+            if saved
+            else dict(
+                lengths=(lengths, pltpu.SMEM),
+                frequencies=(rotation_frequencies(), VMEM),
+            )
+        ),
         outputs(forward_shapes(s))
         | outputs(project_shapes(s))
         | ({} if saved else first_outs(s)),
@@ -1804,14 +1829,14 @@
         count=lax.axis_size(CTX),
         line=lax.axis_size(TP),
     )
-    tables = make_tables(doc_lengths, rows)
+    tables = None
 
     kept = []
     stream = hidden_in
     saved = None
     for layer in range(layers):
         if layer < layers - 1:
-            result = forward_layer(layer, stream, saved, w, tables, s)
+            result = forward_layer(layer, stream, saved, w, tables, s, doc_lengths)
         else:
             result = turn_layer(layer, stream, saved, cotangent, w, tables, s)
         if saved:
@@ -1823,6 +1848,9 @@
                 kraw=result.own_kraw,
                 q=result.own_q,
                 kv=result.own_kv,
+            )
+            tables = types.SimpleNamespace(
+                cosine=result.cosine, sine=result.sine, lowest=result.lowest
             )
         kept.append(types.SimpleNamespace(**(dict(grads=None) | vars(result) | own | dict(x=stream))))
         stream = result.y

time: 422 us -> 413 us (0.979); the launches traced: 417 us -> 413 us
  other arithmetic: 4.94 us -> 0.6 us
where the time goes in v5:
time: 413 us
  Pallas kernels  411 us (100%)
    pallas_call x5, Pallas kernels, run_kernel(): pl.pallas_call(lambda *refs: body(named(refs, groups)), out_shape=[shape...  411 us

profile of v5, /device:TPU:0, one launch (start us, length us, event | category | flops | bytes accessed | tf_op | source)
XLA Modules:
  0.0 412.5 jit_solution(8752978796842064971)
XLA Ops:
  0.7 0.6 maximum_bitcast_fusion.refs_12_
  1.2 105.4 %shard_map.220 = (bf16[768,512]{1,0:T(8,128)(2,1)}, bf16[768,1024]{1,0:T(8,128)(2,1)}, bf16[768,768]{1,0:T(8,128)(2,1)}, f32[768,128]{1,0:T(8,128)}, f32[768,102...) custom-call(bf16[768,1024]{1,0:T(8,128)(2,1)} %refs_6_.5, ...), custom_call_target="tpu_custom_call" | custom-call | tf_op jit(solution)/shard_map/pallas_call | solution.py:133
  106.6 128.4 %shard_map.221 = (bf16[768,512]{1,0:T(8,128)(2,1)}, bf16[768,256]{1,0:T(8,128)(2,1)}, bf16[768,256]{1,0:T(8,128)(2,1)}, f32[768,1024]{1,0:T(8,128)}, f32[1,1024]...) custom-call(bf16[768,512]{1,0:T(8,128)(2,1)} %get-tuple-element.91.r, ...), custom_call_target="tpu_custom_call" | custom-call | tf_op jit(solution)/shard_map/pallas_call | solution.py:133
  235.1 110.2 %shard_map.222 = (bf16[768,1024]{1,0:T(8,128)(2,1)}, bf16[768,768]{1,0:T(8,128)(2,1)}, bf16[768,768]{1,0:T(8,128)(2,1)}, bf16[768,1024]{1,0:T(8,128)(2,1)}, bf16...) custom-call(bf16[768,512]{1,0:T(8,128)(2,1)} %get-tuple-element.101., ...), custom_call_target="tpu_custom_call" | custom-call | tf_op jit(solution)/shard_map/pallas_call | solution.py:133
  345.2 61.1 %shard_map.223 = (f32[768,1024]{1,0:T(8,128)}, f32[2,128]{1,0:T(2,128)}, f32[2,128]{1,0:T(2,128)}, f32[2,2,128]{2,1,0:T(2,128)}, f32[2,128,768]{2,1,0:T(8,128)},...) custom-call(bf16[768,512]{1,0:T(8,128)(2,1)} %get-tuple-element.124., ...), custom_call_target="tpu_custom_call" | custom-call | tf_op jit(solution)/shard_map/pallas_call | solution.py:133
  406.4 6.0 %shard_map.224 = (bf16[768,1024]{1,0:T(8,128)(2,1)}, f32[768,1024]{1,0:T(8,128)}, f32[2,128]{1,0:T(2,128)}, f32[2,128]{1,0:T(2,128)}, f32[2,2,128]{2,1,0:T(2,128...) custom-call(bf16[512,1024]{1,0:T(8,128)(2,1)} %get-tuple-element.100, ...), custom_call_target="tpu_custom_call" | custom-call | tf_op jit(solution)/shard_map/pallas_call | solution.py:133
  (1 shorter events, 0.0 us)

commit v6 on v5

--- a/solution.py
+++ b/solution.py
@@ -1795,7 +1795,7 @@
 REST_AT = 19
 REST_WIDES = 2
 REST_HOP = 3
-SCATTER_MIDDLE = (0, 3, 9, 16)
+SCATTER_MIDDLE = (3, 7, 13, 19)
 SCATTER_EVERY = 1
 SCATTER_END = (0, 2, 7, 11)
 

time: 413 us -> 413 us (level)
  no operation moved by 1% of the time
where the time goes in v6:
time: 413 us
  Pallas kernels  411 us (100%)
    pallas_call x5, Pallas kernels, run_kernel(): pl.pallas_call(lambda *refs: body(named(refs, groups)), out_shape=[shape...  411 us

profile of v6, /device:TPU:0, one launch (start us, length us, event | category | flops | bytes accessed | tf_op | source)
XLA Modules:
  0.0 412.5 jit_solution(12709694360295724723)
XLA Ops:
  0.7 0.6 maximum_bitcast_fusion.refs_12_
  1.2 105.4 %shard_map.220 = (bf16[768,512]{1,0:T(8,128)(2,1)}, bf16[768,1024]{1,0:T(8,128)(2,1)}, bf16[768,768]{1,0:T(8,128)(2,1)}, f32[768,128]{1,0:T(8,128)}, f32[768,102...) custom-call(bf16[768,1024]{1,0:T(8,128)(2,1)} %refs_6_.5, ...), custom_call_target="tpu_custom_call" | custom-call | tf_op jit(solution)/shard_map/pallas_call | solution.py:133
  106.6 128.4 %shard_map.221 = (bf16[768,512]{1,0:T(8,128)(2,1)}, bf16[768,256]{1,0:T(8,128)(2,1)}, bf16[768,256]{1,0:T(8,128)(2,1)}, f32[768,1024]{1,0:T(8,128)}, f32[1,1024]...) custom-call(bf16[768,512]{1,0:T(8,128)(2,1)} %get-tuple-element.91.r, ...), custom_call_target="tpu_custom_call" | custom-call | tf_op jit(solution)/shard_map/pallas_call | solution.py:133
  235.1 111.0 %shard_map.222 = (bf16[768,1024]{1,0:T(8,128)(2,1)}, bf16[768,768]{1,0:T(8,128)(2,1)}, bf16[768,768]{1,0:T(8,128)(2,1)}, bf16[768,1024]{1,0:T(8,128)(2,1)}, bf16...) custom-call(bf16[768,512]{1,0:T(8,128)(2,1)} %get-tuple-element.101., ...), custom_call_target="tpu_custom_call" | custom-call | tf_op jit(solution)/shard_map/pallas_call | solution.py:133
  346.1 60.2 %shard_map.223 = (f32[768,1024]{1,0:T(8,128)}, f32[2,128]{1,0:T(2,128)}, f32[2,128]{1,0:T(2,128)}, f32[2,2,128]{2,1,0:T(2,128)}, f32[2,128,768]{2,1,0:T(8,128)},...) custom-call(bf16[768,512]{1,0:T(8,128)(2,1)} %get-tuple-element.124., ...), custom_call_target="tpu_custom_call" | custom-call | tf_op jit(solution)/shard_map/pallas_call | solution.py:133
  406.4 6.0 %shard_map.224 = (bf16[768,1024]{1,0:T(8,128)(2,1)}, f32[768,1024]{1,0:T(8,128)}, f32[2,128]{1,0:T(2,128)}, f32[2,128]{1,0:T(2,128)}, f32[2,2,128]{2,1,0:T(2,128...) custom-call(bf16[512,1024]{1,0:T(8,128)(2,1)} %get-tuple-element.100, ...), custom_call_target="tpu_custom_call" | custom-call | tf_op jit(solution)/shard_map/pallas_call | solution.py:133
  (1 shorter events, 0.0 us)

commit v7 on v5

--- a/solution.py
+++ b/solution.py
@@ -355,10 +355,33 @@
 
 
 class Halo:
-    def __init__(self, keys, sems, rows, count):
+    def __init__(self, keys, sems, rows, count, relayed=False):
         self.keys, self.sems, self.rows, self.count = keys, sems, rows, count
         self.plan = halo_plan(rows)
         self.c, self.t = place()
+        self.relayed = relayed and len(self.plan) == 2
+        self.even = self.c % 2 == 0
+
+    def relays(self, u):
+        return self.even & (self.c >= 2) & (u >= (self.rows - self.plan[1][1]) // UNIT)
+
+    def relay_copy(self, u):
+        offset, skipped = self.plan[1][2], self.rows - self.plan[1][1]
+        source = pl.multiple_of(self.plan[0][2] + u * UNIT, UNIT)
+        target = pl.multiple_of(offset + u * UNIT - skipped, UNIT)
+        return remote(
+            self.keys.at[pl.ds(source, UNIT)],
+            self.keys.at[pl.ds(target, UNIT)],
+            self.sems.at[2, u - skipped // UNIT],
+            self.sems.at[3, u],
+            (jnp.minimum(self.c + 1, self.count - 1), self.t),
+        )
+
+    def relay(self, u):
+        @pl.when(self.relays(u))
+        def _():
+            self.copy(0, u, *self.plan[0]).wait_recv()
+            self.relay_copy(u).start()
 
     def copy(self, index, u, hop, need, offset):
         target = pl.multiple_of(offset + u * UNIT - (self.rows - need), UNIT)
@@ -373,6 +396,10 @@
     def each(self, u, function, receives):
         for index, (hop, need, offset) in enumerate(self.plan):
             exists = self.c >= hop if receives else self.c + hop < self.count
+            if self.relayed and receives and index == 0:
+                exists = exists & jnp.logical_not(self.relays(u))
+            if self.relayed and not receives and index == 1:
+                exists = exists & self.even
 
             @pl.when(exists & (u >= (self.rows - need) // UNIT))
             def _():
@@ -392,6 +419,8 @@
     def finish(self, u):
         self.each(u, lambda copy: copy.wait_recv(), True)
         self.each(u, lambda copy: copy.wait_send(), False)
+        if self.relayed:
+            pl.when(self.relays(u))(lambda: self.relay_copy(u).wait_send())
 
 
 def project_heads(n, raw, out, out_rows, rows, which, layer):
@@ -889,7 +918,7 @@
         if not saved:
             wait_all(*own_weights)
             own = first_view(n)
-            own_halo = Halo(n.kvin_v, n.first_sems, s.rows, s.count)
+            own_halo = Halo(n.kvin_v, n.first_sems, s.rows, s.count, True)
             own_halo.blank()
 
             def own_keys(i):
@@ -902,6 +931,8 @@
 
             each_of(s.rows // WIDE, own_keys)
             each_of(s.rows // WIDE, own_queries)
+            if own_halo.relayed:
+                each_of(s.units, own_halo.relay)
             each_of(s.units, own_halo.finish)
             own_out = (
                 loads(n.kvin_v, n.own_kv),

time: 413 us -> 416 us (level)
  no operation moved by 1% of the time
where the time goes in v7:
time: 416 us; the launch traced here: 412 us
  Pallas kernels  410 us (99%)
    pallas_call x5, Pallas kernels, run_kernel(): pl.pallas_call(lambda *refs: body(named(refs, groups)), out_shape=[shape...  410 us

profile of v7, /device:TPU:0, one launch (start us, length us, event | category | flops | bytes accessed | tf_op | source)
XLA Modules:
  0.0 411.5 jit_solution(12076068503957741105)
XLA Ops:
  0.7 0.6 maximum_bitcast_fusion.refs_12_
  1.2 106.8 %shard_map.220 = (bf16[768,512]{1,0:T(8,128)(2,1)}, bf16[768,1024]{1,0:T(8,128)(2,1)}, bf16[768,768]{1,0:T(8,128)(2,1)}, f32[768,128]{1,0:T(8,128)}, f32[768,102...) custom-call(bf16[768,1024]{1,0:T(8,128)(2,1)} %refs_6_.5, ...), custom_call_target="tpu_custom_call" | custom-call | tf_op jit(solution)/shard_map/pallas_call | solution.py:133
  108.0 126.0 %shard_map.221 = (bf16[768,512]{1,0:T(8,128)(2,1)}, bf16[768,256]{1,0:T(8,128)(2,1)}, bf16[768,256]{1,0:T(8,128)(2,1)}, f32[768,1024]{1,0:T(8,128)}, f32[1,1024]...) custom-call(bf16[768,512]{1,0:T(8,128)(2,1)} %get-tuple-element.91.r, ...), custom_call_target="tpu_custom_call" | custom-call | tf_op jit(solution)/shard_map/pallas_call | solution.py:133
  234.0 110.3 %shard_map.222 = (bf16[768,1024]{1,0:T(8,128)(2,1)}, bf16[768,768]{1,0:T(8,128)(2,1)}, bf16[768,768]{1,0:T(8,128)(2,1)}, bf16[768,1024]{1,0:T(8,128)(2,1)}, bf16...) custom-call(bf16[768,512]{1,0:T(8,128)(2,1)} %get-tuple-element.101., ...), custom_call_target="tpu_custom_call" | custom-call | tf_op jit(solution)/shard_map/pallas_call | solution.py:133
  344.4 60.9 %shard_map.223 = (f32[768,1024]{1,0:T(8,128)}, f32[2,128]{1,0:T(2,128)}, f32[2,128]{1,0:T(2,128)}, f32[2,2,128]{2,1,0:T(2,128)}, f32[2,128,768]{2,1,0:T(8,128)},...) custom-call(bf16[768,512]{1,0:T(8,128)(2,1)} %get-tuple-element.124., ...), custom_call_target="tpu_custom_call" | custom-call | tf_op jit(solution)/shard_map/pallas_call | solution.py:133
  405.3 6.0 %shard_map.224 = (bf16[768,1024]{1,0:T(8,128)(2,1)}, f32[768,1024]{1,0:T(8,128)}, f32[2,128]{1,0:T(2,128)}, f32[2,128]{1,0:T(2,128)}, f32[2,2,128]{2,1,0:T(2,128...) custom-call(bf16[512,1024]{1,0:T(8,128)(2,1)} %get-tuple-element.100, ...), custom_call_target="tpu_custom_call" | custom-call | tf_op jit(solution)/shard_map/pallas_call | solution.py:133
  (1 shorter events, 0.0 us)
